TPU v7x, 32 devices: a whole 2x2x4 slice. The times are simulated.
32 devices in a mesh: groups: 2 (over y), wide: 16 (over z, x, core), narrow: 1.
Axes of the slice: x: 2, y: 2, z: 4, core: 2. Of those that a mesh axis runs over, the one named last changes fastest.
Arguments:
- pair: bfloat16 [256, 128, 128], P(('groups', 'wide'), 'narrow'), parts along dimension 0, may hold values from -6 to 6
- adjoint: bfloat16 [256, 128, 128], P(('groups', 'wide'), 'narrow'), parts along dimension 0, may hold values from -6 to 6
- mask: int32 [256], P('groups'), parts along dimension 0, may hold values 0 or 1
- chain: int32 [256], P('groups'), parts along dimension 0, may hold values from 0 to 3, never falling along the last dimension, each value on 1 to 64 neighbouring positions
- gain_in: float32 [128], replicated, may hold values from 0.1 to 1.9
- w_proj: bfloat16 [128, 512], replicated, may hold values from -0.5 to 0.5
- w_gate: bfloat16 [128, 128], replicated, may hold values from -0.5 to 0.5
- chain_bias: float32 [2, 128], replicated, may hold values from -4 to 4
- gain_out: float32 [128], replicated, may hold values from 0.1 to 1.9
- w_out: bfloat16 [128, 128], replicated, may hold values from -0.5 to 0.5
Outputs:
- output: bfloat16 [256, 128, 128], P(('groups', 'wide'), 'narrow'), parts along dimension 0
- d_pair: bfloat16 [256, 128, 128], P(('groups', 'wide'), 'narrow'), parts along dimension 0
- d_proj: float32 [256, 512], P('groups'), parts along dimension 0
- d_gate: float32 [256, 128], P('groups'), parts along dimension 0
There are 2 independent parts, one for each index of `groups`. A program takes and returns all parts, laid end to end along the dimension named above; an argument that names none is the same for every part. Nothing has to cross between parts.
All inputs are finite; a program needn't handle non-finite values.
Results may differ from a plain program's by a relative error of at most 0.017.
Values may be sent and summed in bfloat16 or wider, within the bound.
No kernel may reach another device: no remote copies, remote signals or barrier semaphores. Data moves between devices by JAX's collectives and lax.ppermute only.
A program may use at most 64 MiB of HBM per device.

v0:
```python
import functools

import jax
import jax.numpy as jnp
from jax import lax
from jax.experimental import pallas as pl
from jax.experimental.pallas import tpu as pltpu
from jax.sharding import PartitionSpec as P

EPS = 1e-05


def normalize(values, gain, axis):
    centre = values - jnp.mean(values, axis, keepdims=True)
    rstd = lax.rsqrt(jnp.mean(centre * centre, axis, keepdims=True) + EPS)
    hat = centre * rstd
    return (hat * gain, hat, rstd)


def norm_back(scaled, hat, rstd, axis):
    return rstd * (
        scaled
        - jnp.mean(scaled, axis, keepdims=True)
        - hat * jnp.mean(scaled * hat, axis, keepdims=True)
    )


def swap(blocks):
    return lax.all_to_all(blocks, ("wide", "narrow"), split_axis=0, concat_axis=0, tiled=True)


def gather_cells(blocks, n_wide, n_narrow):
    _, own, rows, cols = blocks.shape
    shaped = blocks.reshape(n_wide, n_narrow, own, rows, cols)
    return jnp.transpose(shaped, (2, 0, 3, 1, 4)).reshape(own, n_wide * rows, n_narrow * cols)


def split_cells(field, n_wide, n_narrow):
    own, rows, cols = field.shape
    shaped = field.reshape(own, n_wide, rows // n_wide, n_narrow, cols // n_narrow)
    moved = jnp.transpose(shaped, (1, 3, 0, 2, 4))
    return moved.reshape(n_wide * n_narrow, own, rows // n_wide, cols // n_narrow)


BF = jnp.bfloat16
F32 = jnp.float32


def dot(a, b, over=((1,), (0,))):
    return lax.dot_general(a, b, (over, ((), ())), preferred_element_type=F32)


def column(row):
    return jnp.broadcast_to(row, (row.shape[1], row.shape[1])).T


def centred(x):
    centre = x - jnp.mean(x, 0, keepdims=True)
    rstd = lax.rsqrt(jnp.mean(centre * centre, 0, keepdims=True) + EPS)
    return centre * rstd, rstd


def back_t(scaled, hat, rstd):
    inner = hat * jnp.mean(scaled * hat, 0, keepdims=True)
    return rstd * (scaled - jnp.mean(scaled, 0, keepdims=True) - inner)


def two_rows(first, second, devices):
    own, cols = first.shape[0] // devices, first.shape[1]
    shape = (devices, own, cols)
    return jnp.concatenate([first.reshape(shape), second.reshape(shape)], 1).astype(BF)


def apart(block, devices):
    wide = block.astype(F32)
    own, cols = wide.shape[1] // 2, wide.shape[2]
    return [wide[:, at * own : (at + 1) * own].reshape(devices * own, cols) for at in range(2)]


def project_kernel(pair_ref, mask_ref, gain_ref, w_ref, sent_ref, zn_ref):
    devices, depth, _ = sent_ref.shape
    rows, cols, width = pair_ref.shape
    gain = column(gain_ref[...])
    weights = w_ref[...].astype(F32).T.astype(BF)
    hidden = weights.shape[0] // 4
    half = depth // 2
    for two in range(rows // 2):
        pieces = []
        for row in (2 * two, 2 * two + 1):
            hat, _ = centred(pair_ref[row].astype(F32).T)
            zn = (hat * gain).astype(BF)
            zn_ref[:, row * cols : (row + 1) * cols] = zn
            proj = dot(weights, zn)
            mask = mask_ref[row : row + 1, :]
            left = mask * jax.nn.sigmoid(proj[hidden : 2 * hidden]) * proj[:hidden]
            right = mask * jax.nn.sigmoid(proj[3 * hidden :]) * proj[2 * hidden : 3 * hidden]
            pieces.append((left, right))
        at = two * 16
        sent_ref[:, at : at + 16, :] = two_rows(pieces[0][0], pieces[1][0], devices)
        sent_ref[:, half + at : half + at + 16, :] = two_rows(pieces[0][1], pieces[1][1], devices)


def gate_kernel(
    zn_ref, adj_ref, mask_ref, same_ref, w_ref, w_gate_ref, bias_ref, gain_ref, w_out_ref,
    factor_ref, gate_ref, t_ref,
):
    rows, cols, width = adj_ref.shape
    weights = w_ref[...].astype(F32).T.astype(BF)
    hidden = weights.shape[0] // 4
    w_gate = w_gate_ref[...].astype(F32).T.astype(BF)
    across, within = column(bias_ref[0:1, :]), column(bias_ref[1:2, :])
    gain = column(gain_ref[...])
    for row in range(rows):
        lanes = slice(row * cols, (row + 1) * cols)
        zn = zn_ref[:, lanes]
        proj = dot(weights, zn)
        mask = mask_ref[row : row + 1, :]
        for side in range(2):
            lin = proj[2 * side * hidden : (2 * side + 1) * hidden]
            sig = jax.nn.sigmoid(proj[(2 * side + 1) * hidden : (2 * side + 2) * hidden])
            factor_ref[2 * side * hidden : (2 * side + 1) * hidden, lanes] = mask * sig
            factor_ref[(2 * side + 1) * hidden : (2 * side + 2) * hidden, lanes] = (
                mask * lin * sig * (1.0 - sig)
            )
        bias = jnp.where(same_ref[row : row + 1, :] > 0.5, within, across)
        gate = jax.nn.sigmoid(dot(w_gate, zn) + bias).T
        gate_ref[row] = gate
        d_out = (adj_ref[row].astype(F32) * gate).astype(BF)
        t_ref[:, lanes] = dot(w_out_ref[...], d_out, ((1,), (1,))) * gain


def mix_kernel(got_ref, sent_ref, left_ref, right_ref, left_s, right_s, out_s):
    devices, depth, cols = got_ref.shape
    own = left_ref.shape[0]
    half = depth // 2
    count = devices * half // own
    left_s[...] = got_ref[:, :half, :].astype(F32).reshape(devices * half, cols)
    right_s[...] = got_ref[:, half:, :].astype(F32).reshape(devices * half, cols)
    for h in range(own):
        left = left_s[pl.ds(h, count, stride=own), :].astype(BF)
        right = right_s[pl.ds(h, count, stride=own), :].astype(BF)
        left_ref[h] = left
        right_ref[h] = right
        out_s[pl.ds(h, count, stride=own), :] = dot(left, right, ((1,), (1,)))
    sent_ref[...] = out_s[...].reshape(devices, half, cols).astype(BF)


def norm_kernel(got_ref, t_ref, gain_ref, sent_ref, xn_ref):
    devices, depth, cols = got_ref.shape
    gain = column(gain_ref[...])
    for two in range(depth // 16):
        pieces = []
        for part, mixed in enumerate(apart(got_ref[:, two * 16 : two * 16 + 16, :], devices)):
            row = 2 * two + part
            lanes = slice(row * cols, (row + 1) * cols)
            hat, rstd = centred(mixed)
            xn_ref[:, lanes] = (hat * gain).astype(BF)
            pieces.append(back_t(t_ref[:, lanes], hat, rstd))
        sent_ref[:, two * 16 : two * 16 + 16, :] = two_rows(*pieces, devices)


def output_kernel(
    xn_ref, gate_ref, adj_ref, zn_ref, w_out_ref, output_ref, d_logit_ref, part_ref
):
    rows, cols, width = adj_ref.shape
    total = None
    for row in range(rows):
        lanes = slice(row * cols, (row + 1) * cols)
        xn = xn_ref[:, lanes].astype(F32).T.astype(BF)
        proj_out = dot(xn, w_out_ref[...])
        gate = gate_ref[row]
        output_ref[row] = (gate * proj_out).astype(BF)
        d_logit = (adj_ref[row].astype(F32) * proj_out * gate * (1.0 - gate)).astype(BF)
        d_logit_ref[row] = d_logit
        term = dot(zn_ref[:, lanes], d_logit)
        total = term if total is None else total + term
    part_ref[...] = total


def unmix_kernel(got_ref, left_ref, right_ref, sent_ref, in_s, left_s, right_s):
    devices, half, cols = got_ref.shape
    own = left_ref.shape[0]
    count = devices * half // own
    in_s[...] = got_ref[...].astype(F32).reshape(devices * half, cols)
    for h in range(own):
        grad = in_s[pl.ds(h, count, stride=own), :]
        left_s[pl.ds(h, count, stride=own), :] = dot(grad.astype(BF), right_ref[h])
        right_s[pl.ds(h, count, stride=own), :] = dot(grad.T.astype(BF), left_ref[h])
    sent_ref[:, :half, :] = left_s[...].reshape(devices, half, cols).astype(BF)
    sent_ref[:, half:, :] = right_s[...].reshape(devices, half, cols).astype(BF)


def cells_kernel(got_ref, factor_ref, zn_ref, gate_part_ref, cells_ref, part_ref):
    devices, depth, cols = got_ref.shape
    half = depth // 2
    hidden = factor_ref.shape[0] // 4
    for side in range(2):
        for two in range(half // 16):
            at = side * half + two * 16
            for part, grad in enumerate(apart(got_ref[:, at : at + 16, :], devices)):
                row = 2 * two + part
                lanes = slice(row * cols, (row + 1) * cols)
                for kind in (2 * side, 2 * side + 1):
                    place = slice(kind * hidden, (kind + 1) * hidden)
                    cells_ref[place, lanes] = (grad * factor_ref[place, lanes]).astype(BF)
    total = dot(zn_ref[...], cells_ref[...], ((1,), (1,)))
    part_ref[:, : 4 * hidden] = total.astype(BF)
    part_ref[:, 4 * hidden :] = gate_part_ref[...].astype(BF)


def pair_kernel(cells_ref, d_logit_ref, pair_ref, gain_ref, w_ref, w_gate_ref, d_pair_ref):
    rows, cols, width = pair_ref.shape
    gain = column(gain_ref[...])
    for row in range(rows):
        lanes = slice(row * cols, (row + 1) * cols)
        hat, rstd = centred(pair_ref[row].astype(F32).T)
        d_zn = dot(w_ref[...], cells_ref[:, lanes])
        d_zn = d_zn + dot(w_gate_ref[...], d_logit_ref[row], ((1,), (1,)))
        d_pair_ref[row] = back_t(d_zn * gain, hat, rstd).T.astype(BF)


def sum_kernel(residues, got_ref, sent_ref):
    total = jnp.sum(got_ref[...].astype(F32), 0) / residues
    sent_ref[...] = jnp.broadcast_to(total.astype(BF)[None], sent_ref.shape)


def call(kernel, outs, scratch=(), flops=0, name=None):
    spec = pl.BlockSpec(memory_space=pltpu.VMEM)

    def run(*args):
        moved = sum(a.size * a.dtype.itemsize for a in (*args, *outs))
        return pl.pallas_call(
            kernel,
            out_shape=list(outs),
            in_specs=[spec] * len(args),
            out_specs=[spec] * len(outs),
            scratch_shapes=list(scratch),
            compiler_params=pltpu.CompilerParams(vmem_limit_bytes=32 * 1024 * 1024),
            cost_estimate=pl.CostEstimate(
                flops=flops, bytes_accessed=moved, transcendentals=0
            ),
            name=name,
        )(*args)

    return run


def small_blocks(pair, adjoint, mask, chain, gain_in, w_proj, w_gate, chain_bias, gain_out, w_out):
    rows, cols, width = pair.shape
    hidden = w_out.shape[0]
    devices = lax.axis_size("wide")
    own = hidden // devices
    residues = rows * devices
    cells = rows * cols
    half = rows * own
    shape = jax.ShapeDtypeStruct
    start = lax.axis_index("wide") * rows
    mask_f = mask.astype(F32)
    row_mask = lax.dynamic_slice_in_dim(mask_f, start, rows, 0)
    row_chain = lax.dynamic_slice_in_dim(chain, start, rows, 0)
    cell_mask = row_mask[:, None] * mask_f[None, :]
    same = (row_chain[:, None] == chain[None, :]).astype(F32)
    gain_in, gain_out = gain_in[None], gain_out[None]
    sent, zn = call(
        project_kernel,
        [shape((devices, 2 * half, cols), BF), shape((width, cells), BF)],
        name="project",
    )(pair, cell_mask, gain_in, w_proj)
    got = swap(sent)
    factor, gate, t = call(
        gate_kernel,
        [shape((4 * hidden, cells), F32), shape((rows, cols, width), F32), shape((hidden, cells), F32)],
        flops=2 * 10**9,
        name="gate",
    )(zn, adjoint, cell_mask, same, w_proj, w_gate, chain_bias, gain_out, w_out)
    field = pltpu.VMEM((devices * half, cols), F32)
    channels = shape((own, residues, cols), BF)
    block = shape((devices, half, cols), BF)
    sent, left, right = call(mix_kernel, [block, channels, channels], [field] * 3, name="mix")(got)
    got = swap(sent)
    sent, xn = call(norm_kernel, [block, shape((hidden, cells), BF)], name="norm")(got, t, gain_out)
    got = swap(sent)
    output, d_logit, gate_part = call(
        output_kernel,
        [shape(pair.shape, BF), shape(pair.shape, BF), shape((width, width), F32)],
        flops=2 * 10**9,
        name="output",
    )(xn, gate, adjoint, zn, w_out)
    sent = call(
        unmix_kernel, [shape((devices, 2 * half, cols), BF)], [field] * 3, name="unmix"
    )(got, left, right)[0]
    got = swap(sent)
    d_cells, part = call(
        cells_kernel,
        [shape((4 * hidden, cells), BF), shape((width, 4 * hidden + width), BF)],
        name="cells",
    )(got, factor, zn, gate_part)
    got = swap(part.reshape(devices, width // devices, -1))
    d_pair = call(pair_kernel, [shape(pair.shape, BF)], flops=2 * 10**9, name="pair")(
        d_cells, d_logit, pair, gain_in, w_proj, w_gate
    )[0]
    sent = call(
        functools.partial(sum_kernel, residues), [shape(got.shape, BF)], name="sum"
    )(got)[0]
    total = swap(sent).reshape(width, -1).astype(F32)
    return (output, d_pair, total[:, : 4 * hidden], total[:, 4 * hidden :])


def per_device(pair, adjoint, mask, chain, gain_in, w_proj, w_gate, chain_bias, gain_out, w_out):
    rows, cols, width = pair.shape
    hidden = w_out.shape[0]
    n_wide = lax.axis_size("wide")
    n_narrow = lax.axis_size("narrow")
    if n_narrow == 1 and (rows, cols, width) == (8, 128, 128) and hidden == 8 * n_wide == 128:
        return small_blocks(
            pair, adjoint, mask, chain, gain_in, w_proj, w_gate, chain_bias, gain_out, w_out
        )
    residues = rows * n_wide
    devices = n_wide * n_narrow
    own = hidden // devices
    row_start = lax.axis_index("wide") * rows
    col_start = lax.axis_index("narrow") * cols
    mask_f = mask.astype(jnp.float32)
    row_mask = lax.dynamic_slice_in_dim(mask_f, row_start, rows, 0)
    col_mask = lax.dynamic_slice_in_dim(mask_f, col_start, cols, 0)
    cell_mask = (row_mask[:, None] * col_mask[None, :])[None]
    row_chain = lax.dynamic_slice_in_dim(chain, row_start, rows, 0)
    col_chain = lax.dynamic_slice_in_dim(chain, col_start, cols, 0)
    same = (row_chain[:, None] == col_chain[None, :])[:, :, None]
    zn_f, z_hat, z_rstd = normalize(pair.astype(jnp.float32), gain_in, -1)
    zn = zn_f.astype(jnp.bfloat16)
    proj_a = jnp.einsum(
        "ijc,ch->hij", zn, w_proj[:, : 2 * hidden], preferred_element_type=jnp.float32
    )
    proj_b = jnp.einsum(
        "ijc,ch->hij", zn, w_proj[:, 2 * hidden :], preferred_element_type=jnp.float32
    )
    a_lin = proj_a[:hidden]
    sig_a = jax.nn.sigmoid(proj_a[hidden:])
    b_lin = proj_b[:hidden]
    sig_b = jax.nn.sigmoid(proj_b[hidden:])
    left_t = (cell_mask * sig_a * a_lin).astype(jnp.bfloat16)
    right_t = (cell_mask * sig_b * b_lin).astype(jnp.bfloat16)
    pairs = jnp.concatenate(
        [left_t.reshape(devices, own, rows, cols), right_t.reshape(devices, own, rows, cols)], 1
    )
    pairs = gather_cells(swap(pairs), n_wide, n_narrow)
    left_c, right_c = pairs[:own], pairs[own:]
    mixed_c = jnp.einsum("hik,hjk->hij", left_c, right_c, preferred_element_type=jnp.float32)
    mixed_t = swap(split_cells(mixed_c.astype(jnp.bfloat16), n_wide, n_narrow))
    mixed_t = mixed_t.reshape(hidden, rows, cols).astype(jnp.float32)
    xn_f, x_hat, x_rstd = normalize(mixed_t, gain_out[:, None, None], 0)
    xn = xn_f.astype(jnp.bfloat16)
    proj_out = jnp.einsum("hij,hc->ijc", xn, w_out, preferred_element_type=jnp.float32)
    logits = jnp.dot(zn, w_gate, preferred_element_type=jnp.float32) + jnp.where(
        same, chain_bias[1], chain_bias[0]
    )
    gate = jax.nn.sigmoid(logits)
    output = (gate * proj_out).astype(jnp.bfloat16)
    adj = adjoint.astype(jnp.float32)
    d_out = (adj * gate).astype(jnp.bfloat16)
    d_logit = (adj * proj_out * gate * (1.0 - gate)).astype(jnp.bfloat16)
    d_xn = jnp.einsum("ijc,hc->hij", d_out, w_out, preferred_element_type=jnp.float32)
    d_mixed_t = norm_back(d_xn * gain_out[:, None, None], x_hat, x_rstd, 0).astype(jnp.bfloat16)
    d_mixed_c = gather_cells(swap(d_mixed_t.reshape(devices, own, rows, cols)), n_wide, n_narrow)
    d_left_c = jnp.einsum("hij,hjk->hik", d_mixed_c, right_c, preferred_element_type=jnp.float32)
    d_right_c = jnp.einsum("hij,hik->hjk", d_mixed_c, left_c, preferred_element_type=jnp.float32)
    back = jnp.concatenate([d_left_c.astype(jnp.bfloat16), d_right_c.astype(jnp.bfloat16)], 0)
    back = swap(split_cells(back, n_wide, n_narrow))
    d_left = back[:, :own].reshape(hidden, rows, cols).astype(jnp.float32)
    d_right = back[:, own:].reshape(hidden, rows, cols).astype(jnp.float32)
    d_cells_a = jnp.concatenate(
        [d_left * cell_mask * sig_a, d_left * cell_mask * a_lin * sig_a * (1.0 - sig_a)], 0
    ).astype(jnp.bfloat16)
    d_cells_b = jnp.concatenate(
        [d_right * cell_mask * sig_b, d_right * cell_mask * b_lin * sig_b * (1.0 - sig_b)], 0
    ).astype(jnp.bfloat16)
    d_zn = jnp.einsum(
        "hij,ch->ijc", d_cells_a, w_proj[:, : 2 * hidden], preferred_element_type=jnp.float32
    )
    d_zn = d_zn + jnp.einsum(
        "hij,ch->ijc", d_cells_b, w_proj[:, 2 * hidden :], preferred_element_type=jnp.float32
    )
    d_zn = d_zn + jnp.dot(d_logit, w_gate.T, preferred_element_type=jnp.float32)
    d_pair = norm_back(d_zn * gain_in, z_hat, z_rstd, -1).astype(jnp.bfloat16)
    proj_part = jnp.concatenate(
        [
            jnp.einsum("ijc,hij->ch", zn, d_cells_a, preferred_element_type=jnp.float32),
            jnp.einsum("ijc,hij->ch", zn, d_cells_b, preferred_element_type=jnp.float32),
        ],
        1,
    )
    flat_z = zn.reshape(-1, width)
    gate_part = jnp.dot(flat_z.T, d_logit.reshape(-1, width), preferred_element_type=jnp.float32)
    parts = jnp.concatenate([proj_part, gate_part], 1)
    chunk = width // devices
    mine = swap(parts.astype(jnp.bfloat16).reshape(devices, chunk, -1))
    mine = jnp.sum(mine.astype(jnp.float32), 0) / residues
    mine = mine.astype(jnp.bfloat16)
    total = swap(jnp.broadcast_to(mine, (devices,) + mine.shape)).reshape(width, -1)
    total = total.astype(jnp.float32)
    return (output, d_pair, total[:, : 4 * hidden], total[:, 4 * hidden :])


def solution(mesh):
    placed = (
        P(("groups", "wide"), "narrow", None),
        P(("groups", "wide"), "narrow", None),
        P("groups"),
        P("groups"),
        P(),
        P(),
        P(),
        P(),
        P(),
        P(),
    )
    return jax.shard_map(
        per_device,
        mesh=mesh,
        in_specs=placed,
        out_specs=(
            P(("groups", "wide"), "narrow", None),
            P(("groups", "wide"), "narrow", None),
            P("groups", None),
            P("groups", None),
        ),
        check_vma=False,
    )
```

profile of v0, /device:TPU:0, one launch (start us, length us, event | category | flops | bytes accessed | tf_op | source)
XLA Modules:
  0.0 103.6 jit_solution(18323993856607277261)
XLA Ops:
  1.5 0.9 copy-done.2
  2.4 0.9 copy-done.4
  4.6 21.6 %all_to_all.30.got_ref = bf16[16,128,128]{2,1,0:T(8,128)(2,1)S(1)} all-to-all(bf16[16,128,128]{2,1,0:T(8,128)(2,1)S(1)} %get-tuple-element.19), channel_id=1, replica_groups=mesh['groups'=2,'wide'=16,'narrow'=1] {'wide','narrow'}, dimensions={0} | all-to-all | bytes 1048576 | tf_op jit(solution)/shard_map/all_to_all | solution.py:29
  26.3 1.1 %mix.1 = (bf16[16,64,128]{2,1,0:T(8,128)(2,1)}, bf16[8,128,128]{2,1,0:T(8,128)(2,1)S(1)}, bf16[8,128,128]{2,1,0:T(8,128)(2,1)S(1)}) custom-call(bf16[16,128,128]{2,1,0:T(8,128)(2,1)S(1)} %all_to_all.30.got_ref), custom_call_target="tpu_custom_call" | custom-call | bytes 1310720 | tf_op jit(solution)/shard_map/mix/pallas_call | solution.py:232
  28.0 4.1 %all-to-all-start.1 = ((bf16[16,64,128]{2,1,0:T(8,128)(2,1)}), bf16[16,64,128]{2,1,0:T(8,128)(2,1)S(1)}, u32[]{:S(2)}, u32[]{:S(2)}) async-start(bf16[16,64,128]{2,1,0:T(8,128)(2,1)} %get-tuple-element.20), calls=%async_computation.1 | async-start | bytes 524288 | tf_op jit(solution)/shard_map/all_to_all | solution.py:29
  32.3 0.9 copy-done.11
  34.8 1.5 %gate.1 = (f32[512,1024]{1,0:T(8,128)S(1)}, f32[8,128,128]{2,1,0:T(8,128)S(1)}, f32[128,1024]{1,0:T(8,128)S(1)}) custom-call(bf16[128,1024]{1,0:T(8,128)(2,1)S(1)} %get-tuple-element.21.zn_ref, bf16[8,128,128]{2,1,0:T(8,128)(2,1)S(1)} %copy-done.11, f32[8,128]{1,0:T(8,128)S(1)} %broadcast_multiply_fusion.mask_ref, ...), custom_call_target="tpu_custom_call" | custom-call | flops 2000000000 | bytes 3876352 | tf_op jit(solution)/shard_map/gate/pallas_call | solution.py:232
  36.3 0.8 copy-done.20
  37.1 5.1 %all-to-all-done.1.got_ref = bf16[16,64,128]{2,1,0:T(8,128)(2,1)S(1)} async-done(((bf16[16,64,128]{2,1,0:T(8,128)(2,1)}), bf16[16,64,128]{2,1,0:T(8,128)(2,1)S(1)}, u32[]{:S(2)}, u32[]{:S(2)}) %all-to-all-start.1) | async-done | bytes 262176 | tf_op jit(solution)/shard_map/all_to_all | solution.py:29
  42.6 13.0 %all_to_all.31.got_ref = bf16[16,64,128]{2,1,0:T(8,128)(2,1)S(1)} all-to-all(bf16[16,64,128]{2,1,0:T(8,128)(2,1)S(1)} %get-tuple-element.26), channel_id=1, replica_groups=mesh['groups'=2,'wide'=16,'narrow'=1] {'wide','narrow'}, dimensions={0} | all-to-all | bytes 524288 | tf_op jit(solution)/shard_map/all_to_all | solution.py:29
  55.6 0.9 copy-done.1
  56.5 1.2 %unmix.1 = bf16[16,128,128]{2,1,0:T(8,128)(2,1)} custom-call(bf16[16,64,128]{2,1,0:T(8,128)(2,1)S(1)} %all_to_all.31.got_ref, bf16[8,128,128]{2,1,0:T(8,128)(2,1)S(1)} %get-tuple-element.27.left_ref, bf16[8,128,128]{2,1,0:T(8,128)(2,1)S(1)} %copy-done.1), custom_call_target="tpu_custom_call" | custom-call | bytes 1310720 | tf_op jit(solution)/shard_map/unmix/pallas_call | solution.py:232
  57.8 3.6 %all-to-all-start.3 = ((bf16[16,128,128]{2,1,0:T(8,128)(2,1)}), bf16[16,128,128]{2,1,0:T(8,128)(2,1)S(1)}, u32[]{:S(2)}, u32[]{:S(2)}) async-start(bf16[16,128,128]{2,1,0:T(8,128)(2,1)} %unmix.1), calls=%async_computation.3 | async-start | bytes 1048576 | tf_op jit(solution)/shard_map/all_to_all | solution.py:29
  61.4 0.9 copy-done.14
  63.1 1.0 %copy-done.21 = f32[8,128,128]{2,1,0:T(8,128)S(1)} copy-done((f32[8,128,128]{2,1,0:T(8,128)S(1)}, f32[8,128,128]{2,1,0:T(8,128)}, u32[]{:S(2)}) %copy-start.21) | copy-done | bytes 524312
  64.1 1.0 %output.1 = (bf16[8,128,128]{2,1,0:T(8,128)(2,1)}, bf16[8,128,128]{2,1,0:T(8,128)(2,1)S(1)}, f32[128,128]{1,0:T(8,128)S(1)}) custom-call(bf16[128,1024]{1,0:T(8,128)(2,1)S(1)} %copy-done.14, f32[8,128,128]{2,1,0:T(8,128)S(1)} %copy-done.21, bf16[8,128,128]{2,1,0:T(8,128)(2,1)S(1)} %copy-done.12, bf16[128,1024]{1,0:T(8,128)(2,1)S(1)} %get-tuple-element.21.zn_ref, ...), custom_call_target="tpu_custom_call" | custom-call | flops 2000000000 | bytes 1933312 | tf_op jit(solution)/shard_map/output/pallas_call | solution.py:232
  65.9 9.9 %all-to-all-done.3.got_ref = bf16[16,128,128]{2,1,0:T(8,128)(2,1)S(1)} async-done(((bf16[16,128,128]{2,1,0:T(8,128)(2,1)}), bf16[16,128,128]{2,1,0:T(8,128)(2,1)S(1)}, u32[]{:S(2)}, u32[]{:S(2)}) %all-to-all-start.3) | async-done | bytes 524320 | tf_op jit(solution)/shard_map/all_to_all | solution.py:29
  76.3 1.0 copy-done.9
  77.3 12.3 %all_to_all.32.got_ref = bf16[16,8,640]{2,1,0:T(8,128)(2,1)S(1)} all-to-all(bf16[16,8,640]{2,1,0:T(8,128)(2,1)S(1)} %bitcast.6), channel_id=1, replica_groups=mesh['groups'=2,'wide'=16,'narrow'=1] {'wide','narrow'}, dimensions={0} | all-to-all | bytes 327680 | tf_op jit(solution)/shard_map/all_to_all | solution.py:29
  90.3 3.5 %all-to-all-start.5 = ((bf16[16,8,640]{2,1,0:T(8,128)(2,1)}), bf16[16,8,640]{2,1,0:T(8,128)(2,1)S(1)}, u32[]{:S(2)}, u32[]{:S(2)}) async-start(bf16[16,8,640]{2,1,0:T(8,128)(2,1)} %sum.1), calls=%async_computation.5 | async-start | bytes 327680 | tf_op jit(solution)/shard_map/all_to_all | solution.py:29
  93.8 1.2 %copy-done.10 = bf16[512,1024]{1,0:T(8,128)(2,1)S(1)} copy-done((bf16[512,1024]{1,0:T(8,128)(2,1)S(1)}, bf16[512,1024]{1,0:T(8,128)(2,1)}, u32[]{:S(2)}) %copy-start.10) | copy-done | bytes 1048600
  95.0 0.9 copy-done.23
  96.0 1.5 %pair.1 = bf16[8,128,128]{2,1,0:T(8,128)(2,1)} custom-call(bf16[512,1024]{1,0:T(8,128)(2,1)S(1)} %copy-done.10, bf16[8,128,128]{2,1,0:T(8,128)(2,1)S(1)} %copy-done.23, bf16[8,128,128]{2,1,0:T(8,128)(2,1)S(1)} %copy-done.3, f32[1,128]{1,0:T(1,128)S(1)} %bitcast.8, bf16[128,512]{1,0:T(8,128)(2,1)S(1)} %copy-done.5, bf16[128,128]{1,0:T(8,128)(2,1)S(1)} %copy-done.18), custom_call_target="tpu_custom_call" | custom-call | flops 2000000000 | bytes 1999360 | tf_op jit(solution)/shard_map/pair/pallas_call | solution.py:232
  97.5 4.7 %all-to-all-done.5 = bf16[16,8,640]{2,1,0:T(8,128)(2,1)S(1)} async-done(((bf16[16,8,640]{2,1,0:T(8,128)(2,1)}), bf16[16,8,640]{2,1,0:T(8,128)(2,1)S(1)}, u32[]{:S(2)}, u32[]{:S(2)}) %all-to-all-start.5) | async-done | bytes 163872 | tf_op jit(solution)/shard_map/all_to_all | solution.py:29
  (52 shorter events, 9.0 us)
Async XLA Ops:
  0.6 31.5 %copy-start.24 = (s32[128]{0:T(128)S(1)}, s32[128]{0:T(128)}, u32[]{:S(2)}) copy-start(s32[128]{0:T(128)} %param.13) | copy-start | bytes 1540
  0.6 31.7 %copy-start.8 = (f32[128]{0:T(128)S(1)}, f32[128]{0:T(128)}, u32[]{:S(2)}) copy-start(f32[128]{0:T(128)} %param.18) | copy-start | bytes 1540
  0.7 31.7 %copy-start.19 = (f32[2,128]{1,0:T(2,128)S(1)}, f32[2,128]{1,0:T(2,128)}, u32[]{:S(2)}) copy-start(f32[2,128]{1,0:T(2,128)} %bias_ref.1) | copy-start | bytes 3076
  1.5 0.9 copy-start.2
  2.4 0.9 copy-start.4
  4.0 28.3 %copy-start.5 = (bf16[128,512]{1,0:T(8,128)(2,1)S(1)}, bf16[128,512]{1,0:T(8,128)(2,1)}, u32[]{:S(2)}) copy-start(bf16[128,512]{1,0:T(8,128)(2,1)} %w_ref.5) | copy-start | bytes 393220
  28.0 14.2 %all-to-all-start.1 = ((bf16[16,64,128]{2,1,0:T(8,128)(2,1)}), bf16[16,64,128]{2,1,0:T(8,128)(2,1)S(1)}, u32[]{:S(2)}, u32[]{:S(2)}) async-start(bf16[16,64,128]{2,1,0:T(8,128)(2,1)} %get-tuple-element.20), calls=%async_computation.1 | async-start | bytes 524288 | tf_op jit(solution)/shard_map/all_to_all | solution.py:29
  32.3 1.0 copy-start.11
  33.3 0.8 copy-start.15
  34.0 0.8 copy-start.17
  36.3 0.8 copy-start.20
  42.6 13.0 %copy-start.13 = (bf16[128,1024]{1,0:T(8,128)(2,1)}, bf16[128,1024]{1,0:T(8,128)(2,1)S(1)}, u32[]{:S(2)}) copy-start(bf16[128,1024]{1,0:T(8,128)(2,1)S(1)} %get-tuple-element.23.xn_ref) | copy-start | bytes 786436
  42.6 18.7 %copy-start.12 = (bf16[8,128,128]{2,1,0:T(8,128)(2,1)S(1)}, bf16[8,128,128]{2,1,0:T(8,128)(2,1)}, u32[]{:S(2)}) copy-start(bf16[8,128,128]{2,1,0:T(8,128)(2,1)} %adj_ref.3) | copy-start | bytes 786436
  55.6 1.0 copy-start.1
  57.8 18.0 %all-to-all-start.3 = ((bf16[16,128,128]{2,1,0:T(8,128)(2,1)}), bf16[16,128,128]{2,1,0:T(8,128)(2,1)S(1)}, u32[]{:S(2)}, u32[]{:S(2)}) async-start(bf16[16,128,128]{2,1,0:T(8,128)(2,1)} %unmix.1), calls=%async_computation.3 | async-start | bytes 1048576 | tf_op jit(solution)/shard_map/all_to_all | solution.py:29
  61.3 1.0 copy-start.14
  63.1 1.0 %copy-start.21 = (f32[8,128,128]{2,1,0:T(8,128)S(1)}, f32[8,128,128]{2,1,0:T(8,128)}, u32[]{:S(2)}) copy-start(f32[8,128,128]{2,1,0:T(8,128)} %copy-done.20) | copy-start | bytes 1572868
  65.9 27.9 %copy-start.3 = (bf16[8,128,128]{2,1,0:T(8,128)(2,1)S(1)}, bf16[8,128,128]{2,1,0:T(8,128)(2,1)}, u32[]{:S(2)}) copy-start(bf16[8,128,128]{2,1,0:T(8,128)(2,1)} %pair_ref.3) | copy-start | bytes 786436
  65.9 27.9 %copy-start.7 = (f32[128]{0:T(128)S(1)}, f32[128]{0:T(128)}, u32[]{:S(2)}) copy-start(f32[128]{0:T(128)} %param.14) | copy-start | bytes 1540
  65.9 27.9 %copy-start.18 = (bf16[128,128]{1,0:T(8,128)(2,1)S(1)}, bf16[128,128]{1,0:T(8,128)(2,1)}, u32[]{:S(2)}) copy-start(bf16[128,128]{1,0:T(8,128)(2,1)} %w_gate_ref.3) | copy-start | bytes 98308
  76.3 1.0 copy-start.9
  90.3 11.9 %all-to-all-start.5 = ((bf16[16,8,640]{2,1,0:T(8,128)(2,1)}), bf16[16,8,640]{2,1,0:T(8,128)(2,1)S(1)}, u32[]{:S(2)}, u32[]{:S(2)}) async-start(bf16[16,8,640]{2,1,0:T(8,128)(2,1)} %sum.1), calls=%async_computation.5 | async-start | bytes 327680 | tf_op jit(solution)/shard_map/all_to_all | solution.py:29
  93.8 1.2 %copy-start.10 = (bf16[512,1024]{1,0:T(8,128)(2,1)S(1)}, bf16[512,1024]{1,0:T(8,128)(2,1)}, u32[]{:S(2)}) copy-start(bf16[512,1024]{1,0:T(8,128)(2,1)} %copy-done.9) | copy-start | bytes 3145732
  95.0 0.9 copy-start.23
  (4 other events, 2.8 us)
where the time goes:
time: 105 us; the launch traced here: 104 us
  blocking collectives  46.9 us (45%)
  waiting for transfers between devices  19.7 us (19%)
  local copies, waits for them, and re-layouts  15.6 us (15%)
  starting transfers between devices  11.2 us (11%)
  Pallas kernels  8.62 us (8%)
    all_to_all x3, blocking collectives, swap(): lax.all_to_all(blocks, ('wide', 'narrow'), split_axis=0, concat_axis=0, t...  46.9 us
    all_to_all x3, waiting for transfers between devices, swap(): lax.all_to_all(blocks, ('wide', 'narrow'), split_axis=0, concat_axis=0, t...  19.7 us
    unnamed x50, local copies, waits for them, and re-layouts  14 us
    all_to_all x3, starting transfers between devices, swap(): lax.all_to_all(blocks, ('wide', 'narrow'), split_axis=0, concat_axis=0, t...  11.2 us
    pallas_call x9, Pallas kernels, run(): pl.pallas_call(kernel, out_shape=list(outs), in_specs=[spec] * len(args),...  8.62 us
  transfers between devices with their start and end apart: 3, of which 3 were waited for; matrix products, arithmetic and copies ran while one was open for 0% of the time, Pallas kernels for 4%

commit v1 on v0

--- a/solution.py
+++ b/solution.py
@@ -77,9 +77,30 @@
     return [wide[:, at * own : (at + 1) * own].reshape(devices * own, cols) for at in range(2)]
 
 
-def project_kernel(pair_ref, mask_ref, gain_ref, w_ref, sent_ref, zn_ref):
+def project_kernel(
+    pair_hbm, mask_hbm, gain_hbm, w_hbm, sent_ref, zn_ref, mask_ref,
+    pair_ref, mask_v, mask_s, gain_ref, w_ref, sems, row_sems,
+):
     devices, depth, _ = sent_ref.shape
     rows, cols, width = pair_ref.shape
+    start = lax.axis_index("wide") * rows
+    row_copies = [
+        pltpu.make_async_copy(pair_hbm.at[row], pair_ref.at[row], row_sems.at[row])
+        for row in range(rows)
+    ]
+    copies = [
+        pltpu.make_async_copy(gain_hbm, gain_ref, sems.at[0]),
+        pltpu.make_async_copy(w_hbm, w_ref, sems.at[1]),
+        pltpu.make_async_copy(mask_hbm, mask_v, sems.at[2]),
+        pltpu.make_async_copy(mask_hbm, mask_s, sems.at[3]),
+    ]
+    for copy in copies + row_copies:
+        copy.start()
+    for copy in copies:
+        copy.wait()
+    mask_f = mask_v[...].astype(F32)
+    for row in range(rows):
+        mask_ref[row : row + 1, :] = mask_f * mask_s[0, start + row].astype(F32)
     gain = column(gain_ref[...])
     weights = w_ref[...].astype(F32).T.astype(BF)
     hidden = weights.shape[0] // 4
@@ -87,6 +108,7 @@
     for two in range(rows // 2):
         pieces = []
         for row in (2 * two, 2 * two + 1):
+            row_copies[row].wait()
             hat, _ = centred(pair_ref[row].astype(F32).T)
             zn = (hat * gain).astype(BF)
             zn_ref[:, row * cols : (row + 1) * cols] = zn
@@ -224,7 +246,15 @@
     sent_ref[...] = jnp.broadcast_to(total.astype(BF)[None], sent_ref.shape)
 
 
-def call(kernel, outs, scratch=(), flops=0, name=None):
+def finish_kernel(got_ref, proj_ref, gate_ref):
+    devices, chunk, depth = got_ref.shape
+    wide = proj_ref.shape[1]
+    total = got_ref[...].astype(F32).reshape(devices * chunk, depth)
+    proj_ref[...] = total[:, :wide]
+    gate_ref[...] = total[:, wide:]
+
+
+def call(kernel, outs, scratch=(), flops=0, name=None, space=pltpu.VMEM):
     spec = pl.BlockSpec(memory_space=pltpu.VMEM)
 
     def run(*args):
@@ -232,10 +262,10 @@
         return pl.pallas_call(
             kernel,
             out_shape=list(outs),
-            in_specs=[spec] * len(args),
+            in_specs=[pl.BlockSpec(memory_space=space)] * len(args),
             out_specs=[spec] * len(outs),
             scratch_shapes=list(scratch),
-            compiler_params=pltpu.CompilerParams(vmem_limit_bytes=32 * 1024 * 1024),
+            compiler_params=pltpu.CompilerParams(vmem_limit_bytes=12 * 1024 * 1024),
             cost_estimate=pl.CostEstimate(
                 flops=flops, bytes_accessed=moved, transcendentals=0
             ),
@@ -255,17 +285,24 @@
     half = rows * own
     shape = jax.ShapeDtypeStruct
     start = lax.axis_index("wide") * rows
-    mask_f = mask.astype(F32)
-    row_mask = lax.dynamic_slice_in_dim(mask_f, start, rows, 0)
     row_chain = lax.dynamic_slice_in_dim(chain, start, rows, 0)
-    cell_mask = row_mask[:, None] * mask_f[None, :]
     same = (row_chain[:, None] == chain[None, :]).astype(F32)
     gain_in, gain_out = gain_in[None], gain_out[None]
-    sent, zn = call(
+    sent, zn, cell_mask = call(
         project_kernel,
-        [shape((devices, 2 * half, cols), BF), shape((width, cells), BF)],
+        [shape((devices, 2 * half, cols), BF), shape((width, cells), BF), shape((rows, cols), F32)],
+        [
+            pltpu.VMEM(pair.shape, BF),
+            pltpu.VMEM((1, residues), jnp.int32),
+            pltpu.SMEM((1, residues), jnp.int32),
+            pltpu.VMEM(gain_in.shape, F32),
+            pltpu.VMEM(w_proj.shape, BF),
+            pltpu.SemaphoreType.DMA((4,)),
+            pltpu.SemaphoreType.DMA((rows,)),
+        ],
         name="project",
-    )(pair, cell_mask, gain_in, w_proj)
+        space=pl.ANY,
+    )(pair, mask[None], gain_in, w_proj)
     got = swap(sent)
     factor, gate, t = call(
         gate_kernel,
@@ -302,8 +339,10 @@
     sent = call(
         functools.partial(sum_kernel, residues), [shape(got.shape, BF)], name="sum"
     )(got)[0]
-    total = swap(sent).reshape(width, -1).astype(F32)
-    return (output, d_pair, total[:, : 4 * hidden], total[:, 4 * hidden :])
+    d_proj, d_gate = call(
+        finish_kernel, [shape((width, 4 * hidden), F32), shape((width, width), F32)], name="finish"
+    )(swap(sent))
+    return (output, d_pair, d_proj, d_gate)
 
 
 def per_device(pair, adjoint, mask, chain, gain_in, w_proj, w_gate, chain_bias, gain_out, w_out):

time: 105 us -> 107 us (1.019)
  Pallas kernels: 8.62 us -> 12.4 us
    pallas_call x9 -> x10, Pallas kernels: 8.62 us -> 12.4 us  [run(): pl.pallas_call(kernel, out_shape=list(outs), in_specs=[pl.BlockSpec(memor...]
    slice x2 -> x0, local copies, waits for them, and re-layouts: 1.36 us -> none  [small_blocks(): return (output, d_pair, total[:, :4 * hidden], total[:, 4 * hidden:])]
    unnamed x50 -> x52, local copies, waits for them, and re-layouts: 14 us -> 14.7 us
where the time goes in v1:
time: 107 us; the launch traced here: 106 us
  blocking collectives  46.9 us (44%)
  waiting for transfers between devices  19.7 us (18%)
  local copies, waits for them, and re-layouts  14.8 us (14%)
  Pallas kernels  12.4 us (12%)
  starting transfers between devices  11.2 us (10%)
    all_to_all x3, blocking collectives, swap(): lax.all_to_all(blocks, ('wide', 'narrow'), split_axis=0, concat_axis=0, t...  46.9 us
    all_to_all x3, waiting for transfers between devices, swap(): lax.all_to_all(blocks, ('wide', 'narrow'), split_axis=0, concat_axis=0, t...  19.7 us
    unnamed x52, local copies, waits for them, and re-layouts  14.7 us
    pallas_call x10, Pallas kernels, run(): pl.pallas_call(kernel, out_shape=list(outs), in_specs=[pl.BlockSpec(memor...  12.4 us
    all_to_all x3, starting transfers between devices, swap(): lax.all_to_all(blocks, ('wide', 'narrow'), split_axis=0, concat_axis=0, t...  11.2 us
  transfers between devices with their start and end apart: 3, of which 3 were waited for; matrix products, arithmetic and copies ran while one was open for 0% of the time, Pallas kernels for 4%

profile of v1, /device:TPU:0, one launch (start us, length us, event | category | flops | bytes accessed | tf_op | source)
XLA Modules:
  0.0 105.9 jit_solution(13045018382006567384)
XLA Ops:
  0.7 1.0 copy-done.2
  1.6 0.9 copy-done.4
  3.8 3.8 %project.1 = (bf16[16,128,128]{2,1,0:T(8,128)(2,1)S(1)}, bf16[128,1024]{1,0:T(8,128)(2,1)S(1)}, f32[8,128]{1,0:T(8,128)S(1)}) custom-call(bf16[8,128,128]{2,1,0:T(8,128)(2,1)S(1)} %copy-done.2, s32[1,128]{1,0:T(1,128)S(1)} %bitcast.5, f32[1,128]{1,0:T(1,128)S(1)} %bitcast.6, bf16[128,512]{1,0:T(8,128)(2,1)S(1)} %copy-done.4), custom_call_target="tpu_custom_call" | custom-call | bytes 1184768 | tf_op jit(solution)/shard_map/project/pallas_call | solution.py:262
  7.6 21.6 %all_to_all.30.got_ref = bf16[16,128,128]{2,1,0:T(8,128)(2,1)S(1)} all-to-all(bf16[16,128,128]{2,1,0:T(8,128)(2,1)S(1)} %get-tuple-element.22), channel_id=1, replica_groups=mesh['groups'=2,'wide'=16,'narrow'=1] {'wide','narrow'}, dimensions={0} | all-to-all | bytes 1048576 | tf_op jit(solution)/shard_map/all_to_all | solution.py:29
  29.2 1.1 %mix.1 = (bf16[16,64,128]{2,1,0:T(8,128)(2,1)}, bf16[8,128,128]{2,1,0:T(8,128)(2,1)S(1)}, bf16[8,128,128]{2,1,0:T(8,128)(2,1)S(1)}) custom-call(bf16[16,128,128]{2,1,0:T(8,128)(2,1)S(1)} %all_to_all.30.got_ref), custom_call_target="tpu_custom_call" | custom-call | bytes 1310720 | tf_op jit(solution)/shard_map/mix/pallas_call | solution.py:262
  31.0 4.1 %all-to-all-start.1 = ((bf16[16,64,128]{2,1,0:T(8,128)(2,1)}), bf16[16,64,128]{2,1,0:T(8,128)(2,1)S(1)}, u32[]{:S(2)}, u32[]{:S(2)}) async-start(bf16[16,64,128]{2,1,0:T(8,128)(2,1)} %get-tuple-element.23), calls=%async_computation.1 | async-start | bytes 524288 | tf_op jit(solution)/shard_map/all_to_all | solution.py:29
  35.3 0.9 copy-done.12
  37.8 1.5 %gate.1 = (f32[512,1024]{1,0:T(8,128)S(1)}, f32[8,128,128]{2,1,0:T(8,128)S(1)}, f32[128,1024]{1,0:T(8,128)S(1)}) custom-call(bf16[128,1024]{1,0:T(8,128)(2,1)S(1)} %get-tuple-element.24.zn_ref, bf16[8,128,128]{2,1,0:T(8,128)(2,1)S(1)} %copy-done.12, f32[8,128]{1,0:T(8,128)S(1)} %get-tuple-element.25.mask_ref, f32[8,128]{1,0:T(8,128)S(1)} %compare_convert_fusion.same_ref, ...), custom_call_target="tpu_custom_call" | custom-call | flops 2000000000 | bytes 3876352 | tf_op jit(solution)/shard_map/gate/pallas_call | solution.py:262
  40.1 5.1 %all-to-all-done.1.got_ref = bf16[16,64,128]{2,1,0:T(8,128)(2,1)S(1)} async-done(((bf16[16,64,128]{2,1,0:T(8,128)(2,1)}), bf16[16,64,128]{2,1,0:T(8,128)(2,1)S(1)}, u32[]{:S(2)}, u32[]{:S(2)}) %all-to-all-start.1) | async-done | bytes 262176 | tf_op jit(solution)/shard_map/all_to_all | solution.py:29
  45.6 13.0 %all_to_all.31.got_ref = bf16[16,64,128]{2,1,0:T(8,128)(2,1)S(1)} all-to-all(bf16[16,64,128]{2,1,0:T(8,128)(2,1)S(1)} %get-tuple-element.30), channel_id=1, replica_groups=mesh['groups'=2,'wide'=16,'narrow'=1] {'wide','narrow'}, dimensions={0} | all-to-all | bytes 524288 | tf_op jit(solution)/shard_map/all_to_all | solution.py:29
  58.6 0.9 copy-done.1
  59.5 1.2 %unmix.1 = bf16[16,128,128]{2,1,0:T(8,128)(2,1)} custom-call(bf16[16,64,128]{2,1,0:T(8,128)(2,1)S(1)} %all_to_all.31.got_ref, bf16[8,128,128]{2,1,0:T(8,128)(2,1)S(1)} %get-tuple-element.31.left_ref, bf16[8,128,128]{2,1,0:T(8,128)(2,1)S(1)} %copy-done.1), custom_call_target="tpu_custom_call" | custom-call | bytes 1310720 | tf_op jit(solution)/shard_map/unmix/pallas_call | solution.py:262
  60.7 3.6 %all-to-all-start.3 = ((bf16[16,128,128]{2,1,0:T(8,128)(2,1)}), bf16[16,128,128]{2,1,0:T(8,128)(2,1)S(1)}, u32[]{:S(2)}, u32[]{:S(2)}) async-start(bf16[16,128,128]{2,1,0:T(8,128)(2,1)} %unmix.1), calls=%async_computation.3 | async-start | bytes 1048576 | tf_op jit(solution)/shard_map/all_to_all | solution.py:29
  64.3 0.9 copy-done.15
  66.0 1.0 copy-done.22
  67.1 1.0 output.1
  68.8 9.9 %all-to-all-done.3.got_ref = bf16[16,128,128]{2,1,0:T(8,128)(2,1)S(1)} async-done(((bf16[16,128,128]{2,1,0:T(8,128)(2,1)}), bf16[16,128,128]{2,1,0:T(8,128)(2,1)S(1)}, u32[]{:S(2)}, u32[]{:S(2)}) %all-to-all-start.3) | async-done | bytes 524320 | tf_op jit(solution)/shard_map/all_to_all | solution.py:29
  79.3 1.0 copy-done.10
  80.2 12.3 %all_to_all.32.got_ref = bf16[16,8,640]{2,1,0:T(8,128)(2,1)S(1)} all-to-all(bf16[16,8,640]{2,1,0:T(8,128)(2,1)S(1)} %bitcast.4), channel_id=1, replica_groups=mesh['groups'=2,'wide'=16,'narrow'=1] {'wide','narrow'}, dimensions={0} | all-to-all | bytes 327680 | tf_op jit(solution)/shard_map/all_to_all | solution.py:29
  93.2 3.5 %all-to-all-start.5 = ((bf16[16,8,640]{2,1,0:T(8,128)(2,1)}), bf16[16,8,640]{2,1,0:T(8,128)(2,1)S(1)}, u32[]{:S(2)}, u32[]{:S(2)}) async-start(bf16[16,8,640]{2,1,0:T(8,128)(2,1)} %sum.1), calls=%async_computation.5 | async-start | bytes 327680 | tf_op jit(solution)/shard_map/all_to_all | solution.py:29
  96.8 1.2 %copy-done.11 = bf16[512,1024]{1,0:T(8,128)(2,1)S(1)} copy-done((bf16[512,1024]{1,0:T(8,128)(2,1)S(1)}, bf16[512,1024]{1,0:T(8,128)(2,1)}, u32[]{:S(2)}) %copy-start.11) | copy-done | bytes 1048600
  98.0 0.9 copy-done.24
  99.0 1.5 %pair.1 = bf16[8,128,128]{2,1,0:T(8,128)(2,1)} custom-call(bf16[512,1024]{1,0:T(8,128)(2,1)S(1)} %copy-done.11, bf16[8,128,128]{2,1,0:T(8,128)(2,1)S(1)} %copy-done.24, bf16[8,128,128]{2,1,0:T(8,128)(2,1)S(1)} %copy-done.3, f32[1,128]{1,0:T(1,128)S(1)} %bitcast.7, bf16[128,512]{1,0:T(8,128)(2,1)S(1)} %copy-done.5, bf16[128,128]{1,0:T(8,128)(2,1)S(1)} %copy-done.19), custom_call_target="tpu_custom_call" | custom-call | flops 2000000000 | bytes 1999360 | tf_op jit(solution)/shard_map/pair/pallas_call | solution.py:262
  100.4 4.8 %all-to-all-done.5.got_ref = bf16[16,8,640]{2,1,0:T(8,128)(2,1)S(1)} async-done(((bf16[16,8,640]{2,1,0:T(8,128)(2,1)}), bf16[16,8,640]{2,1,0:T(8,128)(2,1)S(1)}, u32[]{:S(2)}, u32[]{:S(2)}) %all-to-all-start.5) | async-done | bytes 163872 | tf_op jit(solution)/shard_map/all_to_all | solution.py:29
  (49 shorter events, 8.3 us)
Async XLA Ops:
  0.6 34.5 %copy-start.25 = (s32[128]{0:T(128)S(1)}, s32[128]{0:T(128)}, u32[]{:S(2)}) copy-start(s32[128]{0:T(128)} %param.13) | copy-start | bytes 1540
  0.6 34.7 %copy-start.9 = (f32[128]{0:T(128)S(1)}, f32[128]{0:T(128)}, u32[]{:S(2)}) copy-start(f32[128]{0:T(128)} %param.18) | copy-start | bytes 1540
  0.7 34.7 %copy-start.20 = (f32[2,128]{1,0:T(2,128)S(1)}, f32[2,128]{1,0:T(2,128)}, u32[]{:S(2)}) copy-start(f32[2,128]{1,0:T(2,128)} %bias_ref.1) | copy-start | bytes 3076
  0.7 1.0 copy-start.2
  1.6 0.9 copy-start.4
  3.8 31.5 %copy-start.5 = (bf16[128,512]{1,0:T(8,128)(2,1)S(1)}, bf16[128,512]{1,0:T(8,128)(2,1)}, u32[]{:S(2)}) copy-start(bf16[128,512]{1,0:T(8,128)(2,1)} %w_ref.3) | copy-start | bytes 393220
  31.0 14.2 %all-to-all-start.1 = ((bf16[16,64,128]{2,1,0:T(8,128)(2,1)}), bf16[16,64,128]{2,1,0:T(8,128)(2,1)S(1)}, u32[]{:S(2)}, u32[]{:S(2)}) async-start(bf16[16,64,128]{2,1,0:T(8,128)(2,1)} %get-tuple-element.23), calls=%async_computation.1 | async-start | bytes 524288 | tf_op jit(solution)/shard_map/all_to_all | solution.py:29
  35.3 1.0 copy-start.12
  36.3 0.8 copy-start.16
  37.0 0.8 copy-start.18
  39.3 0.8 copy-start.21
  45.6 13.0 %copy-start.14 = (bf16[128,1024]{1,0:T(8,128)(2,1)}, bf16[128,1024]{1,0:T(8,128)(2,1)S(1)}, u32[]{:S(2)}) copy-start(bf16[128,1024]{1,0:T(8,128)(2,1)S(1)} %get-tuple-element.27.xn_ref) | copy-start | bytes 786436
  45.6 18.7 %copy-start.13 = (bf16[8,128,128]{2,1,0:T(8,128)(2,1)S(1)}, bf16[8,128,128]{2,1,0:T(8,128)(2,1)}, u32[]{:S(2)}) copy-start(bf16[8,128,128]{2,1,0:T(8,128)(2,1)} %adj_ref.3) | copy-start | bytes 786436
  58.6 1.0 copy-start.1
  60.7 18.0 %all-to-all-start.3 = ((bf16[16,128,128]{2,1,0:T(8,128)(2,1)}), bf16[16,128,128]{2,1,0:T(8,128)(2,1)S(1)}, u32[]{:S(2)}, u32[]{:S(2)}) async-start(bf16[16,128,128]{2,1,0:T(8,128)(2,1)} %unmix.1), calls=%async_computation.3 | async-start | bytes 1048576 | tf_op jit(solution)/shard_map/all_to_all | solution.py:29
  64.3 1.0 copy-start.15
  66.0 1.0 copy-start.22
  68.8 27.9 %copy-start.3 = (bf16[8,128,128]{2,1,0:T(8,128)(2,1)S(1)}, bf16[8,128,128]{2,1,0:T(8,128)(2,1)}, u32[]{:S(2)}) copy-start(bf16[8,128,128]{2,1,0:T(8,128)(2,1)} %pair_ref.1) | copy-start | bytes 786436
  68.8 27.9 %copy-start.8 = (f32[128]{0:T(128)S(1)}, f32[128]{0:T(128)}, u32[]{:S(2)}) copy-start(f32[128]{0:T(128)} %param.14) | copy-start | bytes 1540
  68.8 27.9 %copy-start.19 = (bf16[128,128]{1,0:T(8,128)(2,1)S(1)}, bf16[128,128]{1,0:T(8,128)(2,1)}, u32[]{:S(2)}) copy-start(bf16[128,128]{1,0:T(8,128)(2,1)} %w_gate_ref.3) | copy-start | bytes 98308
  79.3 1.0 copy-start.10
  93.2 11.9 %all-to-all-start.5 = ((bf16[16,8,640]{2,1,0:T(8,128)(2,1)}), bf16[16,8,640]{2,1,0:T(8,128)(2,1)S(1)}, u32[]{:S(2)}, u32[]{:S(2)}) async-start(bf16[16,8,640]{2,1,0:T(8,128)(2,1)} %sum.1), calls=%async_computation.5 | async-start | bytes 327680 | tf_op jit(solution)/shard_map/all_to_all | solution.py:29
  96.8 1.2 %copy-start.11 = (bf16[512,1024]{1,0:T(8,128)(2,1)S(1)}, bf16[512,1024]{1,0:T(8,128)(2,1)}, u32[]{:S(2)}) copy-start(bf16[512,1024]{1,0:T(8,128)(2,1)} %copy-done.10) | copy-start | bytes 3145732
  98.0 0.9 copy-start.24
  (5 other events, 3.5 us)

commit v2 on v1

--- a/solution.py
+++ b/solution.py
@@ -79,7 +79,7 @@
 
 def project_kernel(
     pair_hbm, mask_hbm, gain_hbm, w_hbm, sent_ref, zn_ref, mask_ref,
-    pair_ref, mask_v, mask_s, gain_ref, w_ref, sems, row_sems,
+    pair_ref, mask_v, gain_ref, w_ref, sems, row_sems,
 ):
     devices, depth, _ = sent_ref.shape
     rows, cols, width = pair_ref.shape
@@ -92,15 +92,16 @@
         pltpu.make_async_copy(gain_hbm, gain_ref, sems.at[0]),
         pltpu.make_async_copy(w_hbm, w_ref, sems.at[1]),
         pltpu.make_async_copy(mask_hbm, mask_v, sems.at[2]),
-        pltpu.make_async_copy(mask_hbm, mask_s, sems.at[3]),
     ]
     for copy in copies + row_copies:
         copy.start()
     for copy in copies:
         copy.wait()
     mask_f = mask_v[...].astype(F32)
-    for row in range(rows):
-        mask_ref[row : row + 1, :] = mask_f * mask_s[0, start + row].astype(F32)
+    shape = (rows, mask_f.shape[1])
+    lane = lax.broadcasted_iota(jnp.int32, shape, 1)
+    own = lane == start + lax.broadcasted_iota(jnp.int32, shape, 0)
+    mask_ref[...] = mask_f * jnp.sum(jnp.where(own, mask_f, 0.0), 1, keepdims=True)
     gain = column(gain_ref[...])
     weights = w_ref[...].astype(F32).T.astype(BF)
     hidden = weights.shape[0] // 4
@@ -140,15 +141,15 @@
         for side in range(2):
             lin = proj[2 * side * hidden : (2 * side + 1) * hidden]
             sig = jax.nn.sigmoid(proj[(2 * side + 1) * hidden : (2 * side + 2) * hidden])
-            factor_ref[2 * side * hidden : (2 * side + 1) * hidden, lanes] = mask * sig
+            factor_ref[2 * side * hidden : (2 * side + 1) * hidden, lanes] = (mask * sig).astype(BF)
             factor_ref[(2 * side + 1) * hidden : (2 * side + 2) * hidden, lanes] = (
                 mask * lin * sig * (1.0 - sig)
-            )
+            ).astype(BF)
         bias = jnp.where(same_ref[row : row + 1, :] > 0.5, within, across)
         gate = jax.nn.sigmoid(dot(w_gate, zn) + bias).T
         gate_ref[row] = gate
         d_out = (adj_ref[row].astype(F32) * gate).astype(BF)
-        t_ref[:, lanes] = dot(w_out_ref[...], d_out, ((1,), (1,))) * gain
+        t_ref[:, lanes] = (dot(w_out_ref[...], d_out, ((1,), (1,))) * gain).astype(BF)
 
 
 def mix_kernel(got_ref, sent_ref, left_ref, right_ref, left_s, right_s, out_s):
@@ -177,7 +178,7 @@
             lanes = slice(row * cols, (row + 1) * cols)
             hat, rstd = centred(mixed)
             xn_ref[:, lanes] = (hat * gain).astype(BF)
-            pieces.append(back_t(t_ref[:, lanes], hat, rstd))
+            pieces.append(back_t(t_ref[:, lanes].astype(F32), hat, rstd))
         sent_ref[:, two * 16 : two * 16 + 16, :] = two_rows(*pieces, devices)
 
 
@@ -224,7 +225,7 @@
                 lanes = slice(row * cols, (row + 1) * cols)
                 for kind in (2 * side, 2 * side + 1):
                     place = slice(kind * hidden, (kind + 1) * hidden)
-                    cells_ref[place, lanes] = (grad * factor_ref[place, lanes]).astype(BF)
+                    cells_ref[place, lanes] = (grad * factor_ref[place, lanes].astype(F32)).astype(BF)
     total = dot(zn_ref[...], cells_ref[...], ((1,), (1,)))
     part_ref[:, : 4 * hidden] = total.astype(BF)
     part_ref[:, 4 * hidden :] = gate_part_ref[...].astype(BF)
@@ -294,19 +295,18 @@
         [
             pltpu.VMEM(pair.shape, BF),
             pltpu.VMEM((1, residues), jnp.int32),
-            pltpu.SMEM((1, residues), jnp.int32),
             pltpu.VMEM(gain_in.shape, F32),
             pltpu.VMEM(w_proj.shape, BF),
-            pltpu.SemaphoreType.DMA((4,)),
+            pltpu.SemaphoreType.DMA((3,)),
             pltpu.SemaphoreType.DMA((rows,)),
         ],
         name="project",
-        space=pl.ANY,
+        space=pltpu.HBM,
     )(pair, mask[None], gain_in, w_proj)
     got = swap(sent)
     factor, gate, t = call(
         gate_kernel,
-        [shape((4 * hidden, cells), F32), shape((rows, cols, width), F32), shape((hidden, cells), F32)],
+        [shape((4 * hidden, cells), BF), shape((rows, cols, width), F32), shape((hidden, cells), BF)],
         flops=2 * 10**9,
         name="gate",
     )(zn, adjoint, cell_mask, same, w_proj, w_gate, chain_bias, gain_out, w_out)

time: 107 us -> 103 us (0.963)
  local copies, waits for them, and re-layouts: 14.8 us -> 5.76 us
  waiting for transfers between devices: 19.7 us -> 25.4 us
    unnamed x52 -> x30, local copies, waits for them, and re-layouts: 14.7 us -> 5.69 us
    all_to_all x3, waiting for transfers between devices: 19.7 us -> 25.4 us  [swap(): lax.all_to_all(blocks, ('wide', 'narrow'), split_axis=0, concat_axis=0, t...]
where the time goes in v2:
time: 103 us
  blocking collectives  46.7 us (45%)
  waiting for transfers between devices  25.4 us (25%)
  Pallas kernels  12.4 us (12%)
  starting transfers between devices  11.5 us (11%)
  local copies, waits for them, and re-layouts  5.76 us (6%)
    all_to_all x3, blocking collectives, swap(): lax.all_to_all(blocks, ('wide', 'narrow'), split_axis=0, concat_axis=0, t...  46.7 us
    all_to_all x3, waiting for transfers between devices, swap(): lax.all_to_all(blocks, ('wide', 'narrow'), split_axis=0, concat_axis=0, t...  25.4 us
    pallas_call x10, Pallas kernels, run(): pl.pallas_call(kernel, out_shape=list(outs), in_specs=[pl.BlockSpec(memor...  12.4 us
    all_to_all x3, starting transfers between devices, swap(): lax.all_to_all(blocks, ('wide', 'narrow'), split_axis=0, concat_axis=0, t...  11.5 us
    unnamed x30, local copies, waits for them, and re-layouts  5.69 us
  transfers between devices with their start and end apart: 3, of which 3 were waited for; matrix products, arithmetic and copies ran while one was open for 0% of the time, Pallas kernels for 4%

profile of v2, /device:TPU:0, one launch (start us, length us, event | category | flops | bytes accessed | tf_op | source)
XLA Modules:
  0.0 102.6 jit_solution(136925840518026540)
XLA Ops:
  0.7 0.6 copy-done.4
  1.3 0.9 copy-done
  2.3 0.9 copy-done.2
  3.2 3.6 %project.1 = (bf16[16,128,128]{2,1,0:T(8,128)(2,1)S(1)}, bf16[128,1024]{1,0:T(8,128)(2,1)S(1)}, f32[8,128]{1,0:T(8,128)S(1)}) custom-call(bf16[8,128,128]{2,1,0:T(8,128)(2,1)S(1)} %copy-done, s32[1,128]{1,0:T(1,128)S(1)} %bitcast.5, f32[1,128]{1,0:T(1,128)S(1)} %bitcast.8, bf16[128,512]{1,0:T(8,128)(2,1)S(1)} %copy-done.2), custom_call_target="tpu_custom_call" | custom-call | bytes 1184768 | tf_op jit(solution)/shard_map/project/pallas_call | solution.py:263
  6.7 21.6 %all_to_all.30.got_ref = bf16[16,128,128]{2,1,0:T(8,128)(2,1)S(1)} all-to-all(bf16[16,128,128]{2,1,0:T(8,128)(2,1)S(1)} %get-tuple-element.22), channel_id=1, replica_groups=mesh['groups'=2,'wide'=16,'narrow'=1] {'wide','narrow'}, dimensions={0} | all-to-all | bytes 1048576 | tf_op jit(solution)/shard_map/all_to_all | solution.py:29
  28.3 1.1 %mix.1 = (bf16[16,64,128]{2,1,0:T(8,128)(2,1)}, bf16[8,128,128]{2,1,0:T(8,128)(2,1)S(1)}, bf16[8,128,128]{2,1,0:T(8,128)(2,1)S(1)}) custom-call(bf16[16,128,128]{2,1,0:T(8,128)(2,1)S(1)} %all_to_all.30.got_ref), custom_call_target="tpu_custom_call" | custom-call | bytes 1310720 | tf_op jit(solution)/shard_map/mix/pallas_call | solution.py:263
  29.4 4.2 %all-to-all-start.1 = ((bf16[16,64,128]{2,1,0:T(8,128)(2,1)}), bf16[16,64,128]{2,1,0:T(8,128)(2,1)S(1)}, u32[]{:S(2)}, u32[]{:S(2)}) async-start(bf16[16,64,128]{2,1,0:T(8,128)(2,1)} %get-tuple-element.23), calls=%async_computation.1 | async-start | bytes 524288 | tf_op jit(solution)/shard_map/all_to_all | solution.py:29
  33.7 0.6 copy-done.14
  34.5 0.6 copy-done.5
  35.2 1.5 %gate.1 = (bf16[512,1024]{1,0:T(8,128)(2,1)S(1)}, f32[8,128,128]{2,1,0:T(8,128)S(1)}, bf16[128,1024]{1,0:T(8,128)(2,1)S(1)}) custom-call(bf16[128,1024]{1,0:T(8,128)(2,1)S(1)} %get-tuple-element.24.zn_ref, bf16[8,128,128]{2,1,0:T(8,128)(2,1)S(1)} %copy-done.7, f32[8,128]{1,0:T(8,128)S(1)} %get-tuple-element.25.mask_ref, ...), custom_call_target="tpu_custom_call" | custom-call | flops 2000000000 | bytes 2565632 | tf_op jit(solution)/shard_map/gate/pallas_call | solution.py:263
  36.7 0.8 copy-done.12
  37.5 6.2 %all-to-all-done.1.got_ref = bf16[16,64,128]{2,1,0:T(8,128)(2,1)S(1)} async-done(((bf16[16,64,128]{2,1,0:T(8,128)(2,1)}), bf16[16,64,128]{2,1,0:T(8,128)(2,1)S(1)}, u32[]{:S(2)}, u32[]{:S(2)}) %all-to-all-start.1) | async-done | bytes 262176 | tf_op jit(solution)/shard_map/all_to_all | solution.py:29
  44.2 12.8 %all_to_all.31.got_ref = bf16[16,64,128]{2,1,0:T(8,128)(2,1)S(1)} all-to-all(bf16[16,64,128]{2,1,0:T(8,128)(2,1)S(1)} %get-tuple-element.30), channel_id=1, replica_groups=mesh['groups'=2,'wide'=16,'narrow'=1] {'wide','narrow'}, dimensions={0} | all-to-all | bytes 524288 | tf_op jit(solution)/shard_map/all_to_all | solution.py:29
  57.0 1.2 %unmix.1 = bf16[16,128,128]{2,1,0:T(8,128)(2,1)} custom-call(bf16[16,64,128]{2,1,0:T(8,128)(2,1)S(1)} %all_to_all.31.got_ref, bf16[8,128,128]{2,1,0:T(8,128)(2,1)S(1)} %get-tuple-element.31.left_ref, bf16[8,128,128]{2,1,0:T(8,128)(2,1)S(1)} %get-tuple-element.32.right_ref), custom_call_target="tpu_custom_call" | custom-call | bytes 1310720 | tf_op jit(solution)/shard_map/unmix/pallas_call | solution.py:263
  58.2 3.6 %all-to-all-start.3 = ((bf16[16,128,128]{2,1,0:T(8,128)(2,1)}), bf16[16,128,128]{2,1,0:T(8,128)(2,1)S(1)}, u32[]{:S(2)}, u32[]{:S(2)}) async-start(bf16[16,128,128]{2,1,0:T(8,128)(2,1)} %unmix.1), calls=%async_computation.3 | async-start | bytes 1048576 | tf_op jit(solution)/shard_map/all_to_all | solution.py:29
  61.8 1.0 %copy-done.13 = f32[8,128,128]{2,1,0:T(8,128)S(1)} copy-done((f32[8,128,128]{2,1,0:T(8,128)S(1)}, f32[8,128,128]{2,1,0:T(8,128)}, u32[]{:S(2)}) %copy-start.13) | copy-done | bytes 524312
  62.8 1.1 %output.1 = (bf16[8,128,128]{2,1,0:T(8,128)(2,1)}, bf16[8,128,128]{2,1,0:T(8,128)(2,1)S(1)}, f32[128,128]{1,0:T(8,128)S(1)}) custom-call(bf16[128,1024]{1,0:T(8,128)(2,1)S(1)} %get-tuple-element.27.xn_ref, f32[8,128,128]{2,1,0:T(8,128)S(1)} %copy-done.13, bf16[8,128,128]{2,1,0:T(8,128)(2,1)S(1)} %copy-done.7, ...), custom_call_target="tpu_custom_call" | custom-call | flops 2000000000 | bytes 1933312 | tf_op jit(solution)/shard_map/output/pallas_call | solution.py:263
  63.9 12.3 %all-to-all-done.3.got_ref = bf16[16,128,128]{2,1,0:T(8,128)(2,1)S(1)} async-done(((bf16[16,128,128]{2,1,0:T(8,128)(2,1)}), bf16[16,128,128]{2,1,0:T(8,128)(2,1)S(1)}, u32[]{:S(2)}, u32[]{:S(2)}) %all-to-all-start.3) | async-done | bytes 524320 | tf_op jit(solution)/shard_map/all_to_all | solution.py:29
  76.8 12.3 %all_to_all.32.got_ref = bf16[16,8,640]{2,1,0:T(8,128)(2,1)S(1)} all-to-all(bf16[16,8,640]{2,1,0:T(8,128)(2,1)S(1)} %bitcast.4), channel_id=1, replica_groups=mesh['groups'=2,'wide'=16,'narrow'=1] {'wide','narrow'}, dimensions={0} | all-to-all | bytes 327680 | tf_op jit(solution)/shard_map/all_to_all | solution.py:29
  89.1 0.7 sum.1
  89.8 3.6 %all-to-all-start.5 = ((bf16[16,8,640]{2,1,0:T(8,128)(2,1)}), bf16[16,8,640]{2,1,0:T(8,128)(2,1)S(1)}, u32[]{:S(2)}, u32[]{:S(2)}) async-start(bf16[16,8,640]{2,1,0:T(8,128)(2,1)} %sum.1), calls=%async_computation.5 | async-start | bytes 327680 | tf_op jit(solution)/shard_map/all_to_all | solution.py:29
  93.5 1.5 %pair.1 = bf16[8,128,128]{2,1,0:T(8,128)(2,1)} custom-call(bf16[512,1024]{1,0:T(8,128)(2,1)S(1)} %get-tuple-element.35.cells_ref, bf16[8,128,128]{2,1,0:T(8,128)(2,1)S(1)} %get-tuple-element.36.d_logit_ref, bf16[8,128,128]{2,1,0:T(8,128)(2,1)S(1)} %copy-done.1, f32[1,128]{1,0:T(1,128)S(1)} %bitcast.9, bf16[128,512]{1,0:T(8,128)(2,1)S(1)} %copy-done.3, ...), custom_call_target="tpu_custom_call" | custom-call | flops 2000000000 | bytes 1999360 | tf_op jit(solution)/shard_map/pair/pallas_call | solution.py:263
  95.0 6.9 %all-to-all-done.5.got_ref = bf16[16,8,640]{2,1,0:T(8,128)(2,1)S(1)} async-done(((bf16[16,8,640]{2,1,0:T(8,128)(2,1)}), bf16[16,8,640]{2,1,0:T(8,128)(2,1)S(1)}, u32[]{:S(2)}, u32[]{:S(2)}) %all-to-all-start.5) | async-done | bytes 163872 | tf_op jit(solution)/shard_map/all_to_all | solution.py:29
  101.9 0.7 finish.1
  (27 shorter events, 1.3 us)
Async XLA Ops:
  0.6 0.7 copy-start.4
  0.6 0.7 copy-start.6
  1.3 0.9 copy-start
  2.3 0.9 copy-start.2
  29.4 5.1 %copy-start.3 = (bf16[128,512]{1,0:T(8,128)(2,1)S(1)}, bf16[128,512]{1,0:T(8,128)(2,1)}, u32[]{:S(2)}) copy-start(bf16[128,512]{1,0:T(8,128)(2,1)} %w_ref.3) | copy-start | bytes 393220
  29.4 5.1 %copy-start.7 = (bf16[8,128,128]{2,1,0:T(8,128)(2,1)S(1)}, bf16[8,128,128]{2,1,0:T(8,128)(2,1)}, u32[]{:S(2)}) copy-start(bf16[8,128,128]{2,1,0:T(8,128)(2,1)} %adj_ref.3) | copy-start | bytes 786436
  29.4 5.1 %copy-start.8 = (bf16[128,128]{1,0:T(8,128)(2,1)S(1)}, bf16[128,128]{1,0:T(8,128)(2,1)}, u32[]{:S(2)}) copy-start(bf16[128,128]{1,0:T(8,128)(2,1)} %w_out_ref.3) | copy-start | bytes 98308
  29.4 5.1 %copy-start.9 = (bf16[128,128]{1,0:T(8,128)(2,1)S(1)}, bf16[128,128]{1,0:T(8,128)(2,1)}, u32[]{:S(2)}) copy-start(bf16[128,128]{1,0:T(8,128)(2,1)} %w_gate_ref.3) | copy-start | bytes 98308
  29.4 14.3 %all-to-all-start.1 = ((bf16[16,64,128]{2,1,0:T(8,128)(2,1)}), bf16[16,64,128]{2,1,0:T(8,128)(2,1)S(1)}, u32[]{:S(2)}, u32[]{:S(2)}) async-start(bf16[16,64,128]{2,1,0:T(8,128)(2,1)} %get-tuple-element.23), calls=%async_computation.1 | async-start | bytes 524288 | tf_op jit(solution)/shard_map/all_to_all | solution.py:29
  33.7 0.7 copy-start.14
  34.5 0.7 copy-start.5
  34.5 0.7 copy-start.11
  36.7 0.8 copy-start.12
  58.2 18.0 %all-to-all-start.3 = ((bf16[16,128,128]{2,1,0:T(8,128)(2,1)}), bf16[16,128,128]{2,1,0:T(8,128)(2,1)S(1)}, u32[]{:S(2)}, u32[]{:S(2)}) async-start(bf16[16,128,128]{2,1,0:T(8,128)(2,1)} %unmix.1), calls=%async_computation.3 | async-start | bytes 1048576 | tf_op jit(solution)/shard_map/all_to_all | solution.py:29
  61.8 1.0 %copy-start.13 = (f32[8,128,128]{2,1,0:T(8,128)S(1)}, f32[8,128,128]{2,1,0:T(8,128)}, u32[]{:S(2)}) copy-start(f32[8,128,128]{2,1,0:T(8,128)} %copy-done.12) | copy-start | bytes 1572868
  89.1 4.4 %copy-start.1 = (bf16[8,128,128]{2,1,0:T(8,128)(2,1)S(1)}, bf16[8,128,128]{2,1,0:T(8,128)(2,1)}, u32[]{:S(2)}) copy-start(bf16[8,128,128]{2,1,0:T(8,128)(2,1)} %pair_ref.1) | copy-start | bytes 786436
  89.8 3.7 %copy-start.10 = (bf16[128,128]{1,0:T(8,128)(2,1)S(1)}, bf16[128,128]{1,0:T(8,128)(2,1)}, u32[]{:S(2)}) copy-start(bf16[128,128]{1,0:T(8,128)(2,1)} %w_gate_ref.3) | copy-start | bytes 98308
  89.8 12.1 %all-to-all-start.5 = ((bf16[16,8,640]{2,1,0:T(8,128)(2,1)}), bf16[16,8,640]{2,1,0:T(8,128)(2,1)S(1)}, u32[]{:S(2)}, u32[]{:S(2)}) async-start(bf16[16,8,640]{2,1,0:T(8,128)(2,1)} %sum.1), calls=%async_computation.5 | async-start | bytes 327680 | tf_op jit(solution)/shard_map/all_to_all | solution.py:29

commit v3 on v2

--- a/solution.py
+++ b/solution.py
@@ -255,7 +255,7 @@
     gate_ref[...] = total[:, wide:]
 
 
-def call(kernel, outs, scratch=(), flops=0, name=None, space=pltpu.VMEM):
+def call(kernel, outs, scratch=(), flops=0, name=None, space=pltpu.VMEM, mib=12):
     spec = pl.BlockSpec(memory_space=pltpu.VMEM)
 
     def run(*args):
@@ -266,7 +266,7 @@
             in_specs=[pl.BlockSpec(memory_space=space)] * len(args),
             out_specs=[spec] * len(outs),
             scratch_shapes=list(scratch),
-            compiler_params=pltpu.CompilerParams(vmem_limit_bytes=12 * 1024 * 1024),
+            compiler_params=pltpu.CompilerParams(vmem_limit_bytes=mib * 1024 * 1024),
             cost_estimate=pl.CostEstimate(
                 flops=flops, bytes_accessed=moved, transcendentals=0
             ),
@@ -302,6 +302,7 @@
         ],
         name="project",
         space=pltpu.HBM,
+        mib=56,
     )(pair, mask[None], gain_in, w_proj)
     got = swap(sent)
     factor, gate, t = call(

time: 103 us -> 102 us (level)
  local copies, waits for them, and re-layouts: 5.76 us -> 3.87 us
  Pallas kernels: 12.4 us -> 13.7 us
    unnamed x30 -> x28, local copies, waits for them, and re-layouts: 5.69 us -> 3.8 us
    pallas_call x10, Pallas kernels: 12.4 us -> 13.7 us  [run(): pl.pallas_call(kernel, out_shape=list(outs), in_specs=[pl.BlockSpec(memor...]
where the time goes in v3:
time: 102 us
  blocking collectives  46.9 us (46%)
  waiting for transfers between devices  24.8 us (24%)
  Pallas kernels  13.7 us (13%)
  starting transfers between devices  11.5 us (11%)
  local copies, waits for them, and re-layouts  3.87 us (4%)
    all_to_all x3, blocking collectives, swap(): lax.all_to_all(blocks, ('wide', 'narrow'), split_axis=0, concat_axis=0, t...  46.9 us
    all_to_all x3, waiting for transfers between devices, swap(): lax.all_to_all(blocks, ('wide', 'narrow'), split_axis=0, concat_axis=0, t...  24.8 us
    pallas_call x10, Pallas kernels, run(): pl.pallas_call(kernel, out_shape=list(outs), in_specs=[pl.BlockSpec(memor...  13.7 us
    all_to_all x3, starting transfers between devices, swap(): lax.all_to_all(blocks, ('wide', 'narrow'), split_axis=0, concat_axis=0, t...  11.5 us
    unnamed x28, local copies, waits for them, and re-layouts  3.8 us
  transfers between devices with their start and end apart: 3, of which 3 were waited for; matrix products, arithmetic and copies ran while one was open for 0% of the time, Pallas kernels for 4%

profile of v3, /device:TPU:0, one launch (start us, length us, event | category | flops | bytes accessed | tf_op | source)
XLA Modules:
  0.0 101.7 jit_solution(4942308352972215740)
XLA Ops:
  0.6 4.9 %project.1 = (bf16[16,128,128]{2,1,0:T(8,128)(2,1)}, bf16[128,1024]{1,0:T(8,128)(2,1)}, f32[8,128]{1,0:T(8,128)}) custom-call(bf16[8,128,128]{2,1,0:T(8,128)(2,1)} %pair_ref.1, s32[1,128]{1,0:T(1,128)} %bitcast.9, f32[1,128]{1,0:T(1,128)} %bitcast.7, bf16[128,512]{1,0:T(8,128)(2,1)} %w_ref.3), custom_call_target="tpu_custom_call" | custom-call | bytes 1184768 | tf_op jit(solution)/shard_map/project/pallas_call | solution.py:263
  5.5 21.8 %all_to_all.30.got_ref = bf16[16,128,128]{2,1,0:T(8,128)(2,1)S(1)} all-to-all(bf16[16,128,128]{2,1,0:T(8,128)(2,1)} %get-tuple-element.22), channel_id=1, replica_groups=mesh['groups'=2,'wide'=16,'narrow'=1] {'wide','narrow'}, dimensions={0} | all-to-all | bytes 1048576 | tf_op jit(solution)/shard_map/all_to_all | solution.py:29
  27.4 1.1 %mix.1 = (bf16[16,64,128]{2,1,0:T(8,128)(2,1)}, bf16[8,128,128]{2,1,0:T(8,128)(2,1)S(1)}, bf16[8,128,128]{2,1,0:T(8,128)(2,1)S(1)}) custom-call(bf16[16,128,128]{2,1,0:T(8,128)(2,1)S(1)} %all_to_all.30.got_ref), custom_call_target="tpu_custom_call" | custom-call | bytes 1310720 | tf_op jit(solution)/shard_map/mix/pallas_call | solution.py:263
  28.5 4.2 %all-to-all-start.1 = ((bf16[16,64,128]{2,1,0:T(8,128)(2,1)}), bf16[16,64,128]{2,1,0:T(8,128)(2,1)S(1)}, u32[]{:S(2)}, u32[]{:S(2)}) async-start(bf16[16,64,128]{2,1,0:T(8,128)(2,1)} %get-tuple-element.23), calls=%async_computation.1 | async-start | bytes 524288 | tf_op jit(solution)/shard_map/all_to_all | solution.py:29
  32.7 0.6 copy-done.13
  33.6 0.6 copy-done.9
  34.2 1.5 %gate.1 = (bf16[512,1024]{1,0:T(8,128)(2,1)S(1)}, f32[8,128,128]{2,1,0:T(8,128)S(1)}, bf16[128,1024]{1,0:T(8,128)(2,1)S(1)}) custom-call(bf16[128,1024]{1,0:T(8,128)(2,1)S(1)} %copy-done.1, bf16[8,128,128]{2,1,0:T(8,128)(2,1)S(1)} %copy-done.5, f32[8,128]{1,0:T(8,128)S(1)} %copy-done.9, f32[8,128]{1,0:T(8,128)S(1)} %compare_convert_fusion.same_ref, ...), custom_call_target="tpu_custom_call" | custom-call | flops 2000000000 | bytes 2565632 | tf_op jit(solution)/shard_map/gate/pallas_call | solution.py:263
  35.8 0.8 copy-done.11
  36.6 6.2 %all-to-all-done.1.got_ref = bf16[16,64,128]{2,1,0:T(8,128)(2,1)S(1)} async-done(((bf16[16,64,128]{2,1,0:T(8,128)(2,1)}), bf16[16,64,128]{2,1,0:T(8,128)(2,1)S(1)}, u32[]{:S(2)}, u32[]{:S(2)}) %all-to-all-start.1) | async-done | bytes 262176 | tf_op jit(solution)/shard_map/all_to_all | solution.py:29
  42.8 0.4 norm.1
  43.2 12.8 %all_to_all.31.got_ref = bf16[16,64,128]{2,1,0:T(8,128)(2,1)S(1)} all-to-all(bf16[16,64,128]{2,1,0:T(8,128)(2,1)S(1)} %get-tuple-element.30), channel_id=1, replica_groups=mesh['groups'=2,'wide'=16,'narrow'=1] {'wide','narrow'}, dimensions={0} | all-to-all | bytes 524288 | tf_op jit(solution)/shard_map/all_to_all | solution.py:29
  56.0 1.2 %unmix.1 = bf16[16,128,128]{2,1,0:T(8,128)(2,1)} custom-call(bf16[16,64,128]{2,1,0:T(8,128)(2,1)S(1)} %all_to_all.31.got_ref, bf16[8,128,128]{2,1,0:T(8,128)(2,1)S(1)} %get-tuple-element.31.left_ref, bf16[8,128,128]{2,1,0:T(8,128)(2,1)S(1)} %get-tuple-element.32.right_ref), custom_call_target="tpu_custom_call" | custom-call | bytes 1310720 | tf_op jit(solution)/shard_map/unmix/pallas_call | solution.py:263
  57.2 3.6 %all-to-all-start.3 = ((bf16[16,128,128]{2,1,0:T(8,128)(2,1)}), bf16[16,128,128]{2,1,0:T(8,128)(2,1)S(1)}, u32[]{:S(2)}, u32[]{:S(2)}) async-start(bf16[16,128,128]{2,1,0:T(8,128)(2,1)} %unmix.1), calls=%async_computation.3 | async-start | bytes 1048576 | tf_op jit(solution)/shard_map/all_to_all | solution.py:29
  60.8 1.0 %copy-done.12 = f32[8,128,128]{2,1,0:T(8,128)S(1)} copy-done((f32[8,128,128]{2,1,0:T(8,128)S(1)}, f32[8,128,128]{2,1,0:T(8,128)}, u32[]{:S(2)}) %copy-start.12) | copy-done | bytes 524312
  61.9 1.1 %output.1 = (bf16[8,128,128]{2,1,0:T(8,128)(2,1)}, bf16[8,128,128]{2,1,0:T(8,128)(2,1)S(1)}, f32[128,128]{1,0:T(8,128)S(1)}) custom-call(bf16[128,1024]{1,0:T(8,128)(2,1)S(1)} %get-tuple-element.27.xn_ref, f32[8,128,128]{2,1,0:T(8,128)S(1)} %copy-done.12, bf16[8,128,128]{2,1,0:T(8,128)(2,1)S(1)} %copy-done.5, bf16[128,1024]{1,0:T(8,128)(2,1)S(1)} %copy-done.1, ...), custom_call_target="tpu_custom_call" | custom-call | flops 2000000000 | bytes 1933312 | tf_op jit(solution)/shard_map/output/pallas_call | solution.py:263
  62.9 12.3 %all-to-all-done.3.got_ref = bf16[16,128,128]{2,1,0:T(8,128)(2,1)S(1)} async-done(((bf16[16,128,128]{2,1,0:T(8,128)(2,1)}), bf16[16,128,128]{2,1,0:T(8,128)(2,1)S(1)}, u32[]{:S(2)}, u32[]{:S(2)}) %all-to-all-start.3) | async-done | bytes 524320 | tf_op jit(solution)/shard_map/all_to_all | solution.py:29
  75.2 0.6 cells.1
  75.9 12.3 %all_to_all.32.got_ref = bf16[16,8,640]{2,1,0:T(8,128)(2,1)S(1)} all-to-all(bf16[16,8,640]{2,1,0:T(8,128)(2,1)S(1)} %bitcast.4), channel_id=1, replica_groups=mesh['groups'=2,'wide'=16,'narrow'=1] {'wide','narrow'}, dimensions={0} | all-to-all | bytes 327680 | tf_op jit(solution)/shard_map/all_to_all | solution.py:29
  88.2 0.7 sum.1
  88.9 3.6 %all-to-all-start.5 = ((bf16[16,8,640]{2,1,0:T(8,128)(2,1)}), bf16[16,8,640]{2,1,0:T(8,128)(2,1)S(1)}, u32[]{:S(2)}, u32[]{:S(2)}) async-start(bf16[16,8,640]{2,1,0:T(8,128)(2,1)} %sum.1), calls=%async_computation.5 | async-start | bytes 327680 | tf_op jit(solution)/shard_map/all_to_all | solution.py:29
  92.5 0.6 copy-done.4
  93.2 1.4 %pair.1 = bf16[8,128,128]{2,1,0:T(8,128)(2,1)} custom-call(bf16[512,1024]{1,0:T(8,128)(2,1)S(1)} %get-tuple-element.35.cells_ref, bf16[8,128,128]{2,1,0:T(8,128)(2,1)S(1)} %get-tuple-element.36.d_logit_ref, bf16[8,128,128]{2,1,0:T(8,128)(2,1)S(1)} %copy-done, f32[1,128]{1,0:T(1,128)S(1)} %bitcast.8, bf16[128,512]{1,0:T(8,128)(2,1)S(1)} %copy-done.2, ...), custom_call_target="tpu_custom_call" | custom-call | flops 2000000000 | bytes 1999360 | tf_op jit(solution)/shard_map/pair/pallas_call | solution.py:263
  94.6 6.3 %all-to-all-done.5.got_ref = bf16[16,8,640]{2,1,0:T(8,128)(2,1)S(1)} async-done(((bf16[16,8,640]{2,1,0:T(8,128)(2,1)}), bf16[16,8,640]{2,1,0:T(8,128)(2,1)S(1)}, u32[]{:S(2)}, u32[]{:S(2)}) %all-to-all-start.5) | async-done | bytes 163872 | tf_op jit(solution)/shard_map/all_to_all | solution.py:29
  100.9 0.7 finish.1
  (25 shorter events, 0.2 us)
Async XLA Ops:
  27.4 6.2 %copy-start.5 = (bf16[8,128,128]{2,1,0:T(8,128)(2,1)S(1)}, bf16[8,128,128]{2,1,0:T(8,128)(2,1)}, u32[]{:S(2)}) copy-start(bf16[8,128,128]{2,1,0:T(8,128)(2,1)} %adj_ref.3) | copy-start | bytes 786436
  28.5 5.1 %copy-start.1 = (bf16[128,1024]{1,0:T(8,128)(2,1)S(1)}, bf16[128,1024]{1,0:T(8,128)(2,1)}, u32[]{:S(2)}) copy-start(bf16[128,1024]{1,0:T(8,128)(2,1)} %get-tuple-element.24.zn_ref) | copy-start | bytes 786436
  28.5 5.1 %copy-start.2 = (bf16[128,512]{1,0:T(8,128)(2,1)S(1)}, bf16[128,512]{1,0:T(8,128)(2,1)}, u32[]{:S(2)}) copy-start(bf16[128,512]{1,0:T(8,128)(2,1)} %w_ref.3) | copy-start | bytes 393220
  28.5 5.1 %copy-start.6 = (bf16[128,128]{1,0:T(8,128)(2,1)S(1)}, bf16[128,128]{1,0:T(8,128)(2,1)}, u32[]{:S(2)}) copy-start(bf16[128,128]{1,0:T(8,128)(2,1)} %w_out_ref.3) | copy-start | bytes 98308
  28.5 5.1 %copy-start.7 = (bf16[128,128]{1,0:T(8,128)(2,1)S(1)}, bf16[128,128]{1,0:T(8,128)(2,1)}, u32[]{:S(2)}) copy-start(bf16[128,128]{1,0:T(8,128)(2,1)} %w_gate_ref.3) | copy-start | bytes 98308
  28.5 14.3 %all-to-all-start.1 = ((bf16[16,64,128]{2,1,0:T(8,128)(2,1)}), bf16[16,64,128]{2,1,0:T(8,128)(2,1)S(1)}, u32[]{:S(2)}, u32[]{:S(2)}) async-start(bf16[16,64,128]{2,1,0:T(8,128)(2,1)} %get-tuple-element.23), calls=%async_computation.1 | async-start | bytes 524288 | tf_op jit(solution)/shard_map/all_to_all | solution.py:29
  32.7 0.7 copy-start.13
  33.5 0.7 copy-start.9
  33.5 0.7 copy-start.3
  33.5 0.7 copy-start.10
  35.8 0.8 copy-start.11
  57.2 18.0 %all-to-all-start.3 = ((bf16[16,128,128]{2,1,0:T(8,128)(2,1)}), bf16[16,128,128]{2,1,0:T(8,128)(2,1)S(1)}, u32[]{:S(2)}, u32[]{:S(2)}) async-start(bf16[16,128,128]{2,1,0:T(8,128)(2,1)} %unmix.1), calls=%async_computation.3 | async-start | bytes 1048576 | tf_op jit(solution)/shard_map/all_to_all | solution.py:29
  60.8 1.0 %copy-start.12 = (f32[8,128,128]{2,1,0:T(8,128)S(1)}, f32[8,128,128]{2,1,0:T(8,128)}, u32[]{:S(2)}) copy-start(f32[8,128,128]{2,1,0:T(8,128)} %copy-done.11) | copy-start | bytes 1572868
  88.2 4.4 %copy-start = (bf16[8,128,128]{2,1,0:T(8,128)(2,1)S(1)}, bf16[8,128,128]{2,1,0:T(8,128)(2,1)}, u32[]{:S(2)}) copy-start(bf16[8,128,128]{2,1,0:T(8,128)(2,1)} %pair_ref.1) | copy-start | bytes 786436
  88.9 3.7 %copy-start.8 = (bf16[128,128]{1,0:T(8,128)(2,1)S(1)}, bf16[128,128]{1,0:T(8,128)(2,1)}, u32[]{:S(2)}) copy-start(bf16[128,128]{1,0:T(8,128)(2,1)} %w_gate_ref.3) | copy-start | bytes 98308
  88.9 12.1 %all-to-all-start.5 = ((bf16[16,8,640]{2,1,0:T(8,128)(2,1)}), bf16[16,8,640]{2,1,0:T(8,128)(2,1)S(1)}, u32[]{:S(2)}, u32[]{:S(2)}) async-start(bf16[16,8,640]{2,1,0:T(8,128)(2,1)} %sum.1), calls=%async_computation.5 | async-start | bytes 327680 | tf_op jit(solution)/shard_map/all_to_all | solution.py:29
  92.5 0.7 copy-start.4

commit v4 on v3

--- a/solution.py
+++ b/solution.py
@@ -79,21 +79,18 @@
 
 def project_kernel(
     pair_hbm, mask_hbm, gain_hbm, w_hbm, sent_ref, zn_ref, mask_ref,
-    pair_ref, mask_v, gain_ref, w_ref, sems, row_sems,
+    pair_ref, mask_v, gain_ref, w_ref, sems,
 ):
     devices, depth, _ = sent_ref.shape
     rows, cols, width = pair_ref.shape
     start = lax.axis_index("wide") * rows
-    row_copies = [
-        pltpu.make_async_copy(pair_hbm.at[row], pair_ref.at[row], row_sems.at[row])
-        for row in range(rows)
-    ]
     copies = [
         pltpu.make_async_copy(gain_hbm, gain_ref, sems.at[0]),
         pltpu.make_async_copy(w_hbm, w_ref, sems.at[1]),
         pltpu.make_async_copy(mask_hbm, mask_v, sems.at[2]),
+        pltpu.make_async_copy(pair_hbm, pair_ref, sems.at[3]),
     ]
-    for copy in copies + row_copies:
+    for copy in copies:
         copy.start()
     for copy in copies:
         copy.wait()
@@ -109,7 +106,6 @@
     for two in range(rows // 2):
         pieces = []
         for row in (2 * two, 2 * two + 1):
-            row_copies[row].wait()
             hat, _ = centred(pair_ref[row].astype(F32).T)
             zn = (hat * gain).astype(BF)
             zn_ref[:, row * cols : (row + 1) * cols] = zn
@@ -297,8 +293,7 @@
             pltpu.VMEM((1, residues), jnp.int32),
             pltpu.VMEM(gain_in.shape, F32),
             pltpu.VMEM(w_proj.shape, BF),
-            pltpu.SemaphoreType.DMA((3,)),
-            pltpu.SemaphoreType.DMA((rows,)),
+            pltpu.SemaphoreType.DMA((4,)),
         ],
         name="project",
         space=pltpu.HBM,
@@ -314,6 +309,7 @@
     field = pltpu.VMEM((devices * half, cols), F32)
     channels = shape((own, residues, cols), BF)
     block = shape((devices, half, cols), BF)
+    got, t = lax.optimization_barrier((got, t))
     sent, left, right = call(mix_kernel, [block, channels, channels], [field] * 3, name="mix")(got)
     got = swap(sent)
     sent, xn = call(norm_kernel, [block, shape((hidden, cells), BF)], name="norm")(got, t, gain_out)
@@ -324,6 +320,7 @@
         flops=2 * 10**9,
         name="output",
     )(xn, gate, adjoint, zn, w_out)
+    got, gate_part = lax.optimization_barrier((got, gate_part))
     sent = call(
         unmix_kernel, [shape((devices, 2 * half, cols), BF)], [field] * 3, name="unmix"
     )(got, left, right)[0]

time: 102 us -> 99.9 us (0.979)
  blocking collectives: 46.9 us -> 43.5 us
  Pallas kernels: 13.7 us -> 10.6 us
  starting transfers between devices: 11.5 us -> 14.6 us
  local copies, waits for them, and re-layouts: 3.87 us -> 6.13 us
  waiting for transfers between devices: 24.8 us -> 23.6 us
    all_to_all x3, blocking collectives: 46.9 us -> 43.5 us  [swap(): lax.all_to_all(blocks, ('wide', 'narrow'), split_axis=0, concat_axis=0, t...]
    pallas_call x10, Pallas kernels: 13.7 us -> 10.6 us  [run(): pl.pallas_call(kernel, out_shape=list(outs), in_specs=[pl.BlockSpec(memor...]
    all_to_all x3, starting transfers between devices: 11.5 us -> 14.6 us  [swap(): lax.all_to_all(blocks, ('wide', 'narrow'), split_axis=0, concat_axis=0, t...]
    unnamed x28 -> x30, local copies, waits for them, and re-layouts: 3.8 us -> 6.05 us
    all_to_all x3, waiting for transfers between devices: 24.8 us -> 23.6 us  [swap(): lax.all_to_all(blocks, ('wide', 'narrow'), split_axis=0, concat_axis=0, t...]
where the time goes in v4:
time: 99.9 us; the launch traced here: 99.2 us
  blocking collectives  43.5 us (44%)
  waiting for transfers between devices  23.6 us (24%)
  starting transfers between devices  14.6 us (15%)
  Pallas kernels  10.6 us (11%)
  local copies, waits for them, and re-layouts  6.13 us (6%)
    all_to_all x3, blocking collectives, swap(): lax.all_to_all(blocks, ('wide', 'narrow'), split_axis=0, concat_axis=0, t...  43.5 us
    all_to_all x3, waiting for transfers between devices, swap(): lax.all_to_all(blocks, ('wide', 'narrow'), split_axis=0, concat_axis=0, t...  23.6 us
    all_to_all x3, starting transfers between devices, swap(): lax.all_to_all(blocks, ('wide', 'narrow'), split_axis=0, concat_axis=0, t...  14.6 us
    pallas_call x10, Pallas kernels, run(): pl.pallas_call(kernel, out_shape=list(outs), in_specs=[pl.BlockSpec(memor...  10.6 us
    unnamed x30, local copies, waits for them, and re-layouts  6.05 us
  transfers between devices with their start and end apart: 3, of which 3 were waited for; matrix products, arithmetic and copies ran while one was open for 0% of the time, Pallas kernels for 4%

profile of v4, /device:TPU:0, one launch (start us, length us, event | category | flops | bytes accessed | tf_op | source)
XLA Modules:
  0.0 99.2 jit_solution(14015614053213334015)
XLA Ops:
  0.6 2.5 %project.1 = (bf16[16,128,128]{2,1,0:T(8,128)(2,1)}, bf16[128,1024]{1,0:T(8,128)(2,1)}, f32[8,128]{1,0:T(8,128)}) custom-call(bf16[8,128,128]{2,1,0:T(8,128)(2,1)} %pair_ref.1, s32[1,128]{1,0:T(1,128)} %bitcast.9, f32[1,128]{1,0:T(1,128)} %bitcast.7, bf16[128,512]{1,0:T(8,128)(2,1)} %w_ref.3), custom_call_target="tpu_custom_call" | custom-call | bytes 1184768 | tf_op jit(solution)/shard_map/project/pallas_call | solution.py:259
  3.2 7.5 %all-to-all-start = ((bf16[16,128,128]{2,1,0:T(8,128)(2,1)}), bf16[16,128,128]{2,1,0:T(8,128)(2,1)S(1)}, u32[]{:S(2)}, u32[]{:S(2)}) async-start(bf16[16,128,128]{2,1,0:T(8,128)(2,1)} %get-tuple-element.26), calls=%async_computation | async-start | bytes 1048576 | tf_op jit(solution)/shard_map/all_to_all | solution.py:29
  10.8 0.6 copy-done.14
  11.6 0.6 copy-done.10
  12.3 1.5 %gate.1 = (bf16[512,1024]{1,0:T(8,128)(2,1)S(1)}, f32[8,128,128]{2,1,0:T(8,128)S(1)}, bf16[128,1024]{1,0:T(8,128)(2,1)S(1)}) custom-call(bf16[128,1024]{1,0:T(8,128)(2,1)S(1)} %copy-done.1, bf16[8,128,128]{2,1,0:T(8,128)(2,1)S(1)} %copy-done.7, f32[8,128]{1,0:T(8,128)S(1)} %copy-done.10, f32[8,128]{1,0:T(8,128)S(1)} %compare_convert_fusion.same_ref, ...), custom_call_target="tpu_custom_call" | custom-call | flops 2000000000 | bytes 2565632 | tf_op jit(solution)/shard_map/gate/pallas_call | solution.py:259
  13.8 0.8 copy-done.12
  14.6 10.6 %all-to-all-done.got_ref = bf16[16,128,128]{2,1,0:T(8,128)(2,1)S(1)} async-done(((bf16[16,128,128]{2,1,0:T(8,128)(2,1)}), bf16[16,128,128]{2,1,0:T(8,128)(2,1)S(1)}, u32[]{:S(2)}, u32[]{:S(2)}) %all-to-all-start) | async-done | bytes 524320 | tf_op jit(solution)/shard_map/all_to_all | solution.py:29
  25.6 13.9 %all_to_all.30.got_ref = bf16[16,64,128]{2,1,0:T(8,128)(2,1)S(1)} all-to-all(bf16[16,64,128]{2,1,0:T(8,128)(2,1)S(1)} %get-tuple-element.31), channel_id=1, replica_groups=mesh['groups'=2,'wide'=16,'narrow'=1] {'wide','narrow'}, dimensions={0} | all-to-all | bytes 524288 | tf_op jit(solution)/shard_map/all_to_all | solution.py:29
  39.5 1.1 %norm.1 = (bf16[16,64,128]{2,1,0:T(8,128)(2,1)}, bf16[128,1024]{1,0:T(8,128)(2,1)S(1)}) custom-call(bf16[16,64,128]{2,1,0:T(8,128)(2,1)S(1)} %all_to_all.30.got_ref, bf16[128,1024]{1,0:T(8,128)(2,1)S(1)} %get-tuple-element.32.t_ref, f32[1,128]{1,0:T(1,128)S(1)} %bitcast.6), custom_call_target="tpu_custom_call" | custom-call | bytes 1049088 | tf_op jit(solution)/shard_map/norm/pallas_call | solution.py:259
  40.7 3.5 %all-to-all-start.2 = ((bf16[16,64,128]{2,1,0:T(8,128)(2,1)}), bf16[16,64,128]{2,1,0:T(8,128)(2,1)S(1)}, u32[]{:S(2)}, u32[]{:S(2)}) async-start(bf16[16,64,128]{2,1,0:T(8,128)(2,1)} %get-tuple-element.36), calls=%async_computation.2 | async-start | bytes 524288 | tf_op jit(solution)/shard_map/all_to_all | solution.py:29
  44.2 1.0 %copy-done.13 = f32[8,128,128]{2,1,0:T(8,128)S(1)} copy-done((f32[8,128,128]{2,1,0:T(8,128)S(1)}, f32[8,128,128]{2,1,0:T(8,128)}, u32[]{:S(2)}) %copy-start.13) | copy-done | bytes 524312
  45.2 1.0 %output.1 = (bf16[8,128,128]{2,1,0:T(8,128)(2,1)}, bf16[8,128,128]{2,1,0:T(8,128)(2,1)S(1)}, f32[128,128]{1,0:T(8,128)S(1)}) custom-call(bf16[128,1024]{1,0:T(8,128)(2,1)S(1)} %get-tuple-element.33.xn_ref, f32[8,128,128]{2,1,0:T(8,128)S(1)} %copy-done.13, bf16[8,128,128]{2,1,0:T(8,128)(2,1)S(1)} %copy-done.7, bf16[128,1024]{1,0:T(8,128)(2,1)S(1)} %copy-done.1, ...), custom_call_target="tpu_custom_call" | custom-call | flops 2000000000 | bytes 1933312 | tf_op jit(solution)/shard_map/output/pallas_call | solution.py:259
  46.3 7.9 %all-to-all-done.2.got_ref = bf16[16,64,128]{2,1,0:T(8,128)(2,1)S(1)} async-done(((bf16[16,64,128]{2,1,0:T(8,128)(2,1)}), bf16[16,64,128]{2,1,0:T(8,128)(2,1)S(1)}, u32[]{:S(2)}, u32[]{:S(2)}) %all-to-all-start.2) | async-done | bytes 262176 | tf_op jit(solution)/shard_map/all_to_all | solution.py:29
  54.6 17.2 %all_to_all.31.got_ref = bf16[16,128,128]{2,1,0:T(8,128)(2,1)S(1)} all-to-all(bf16[16,128,128]{2,1,0:T(8,128)(2,1)S(1)} %unmix.1), channel_id=1, replica_groups=mesh['groups'=2,'wide'=16,'narrow'=1] {'wide','narrow'}, dimensions={0} | all-to-all | bytes 1048576 | tf_op jit(solution)/shard_map/all_to_all | solution.py:29
  71.9 0.6 cells.1
  72.5 1.0 %copy-done.5 = bf16[512,1024]{1,0:T(8,128)(2,1)} copy-done((bf16[512,1024]{1,0:T(8,128)(2,1)}, bf16[512,1024]{1,0:T(8,128)(2,1)S(1)}, u32[]{:S(2)}) %copy-start.5) | copy-done | bytes 1048600
  73.5 12.3 %all_to_all.32.got_ref = bf16[16,8,640]{2,1,0:T(8,128)(2,1)S(1)} all-to-all(bf16[16,8,640]{2,1,0:T(8,128)(2,1)S(1)} %bitcast.4), channel_id=1, replica_groups=mesh['groups'=2,'wide'=16,'narrow'=1] {'wide','narrow'}, dimensions={0} | all-to-all | bytes 327680 | tf_op jit(solution)/shard_map/all_to_all | solution.py:29
  85.9 0.7 sum.1
  86.6 3.5 %all-to-all-start.5 = ((bf16[16,8,640]{2,1,0:T(8,128)(2,1)}), bf16[16,8,640]{2,1,0:T(8,128)(2,1)S(1)}, u32[]{:S(2)}, u32[]{:S(2)}) async-start(bf16[16,8,640]{2,1,0:T(8,128)(2,1)} %sum.1), calls=%async_computation.5 | async-start | bytes 327680 | tf_op jit(solution)/shard_map/all_to_all | solution.py:29
  90.1 0.6 copy-done.4
  90.7 1.2 %copy-done.6 = bf16[512,1024]{1,0:T(8,128)(2,1)S(1)} copy-done((bf16[512,1024]{1,0:T(8,128)(2,1)S(1)}, bf16[512,1024]{1,0:T(8,128)(2,1)}, u32[]{:S(2)}) %copy-start.6) | copy-done | bytes 1048600
  92.0 1.5 %pair.1 = bf16[8,128,128]{2,1,0:T(8,128)(2,1)} custom-call(bf16[512,1024]{1,0:T(8,128)(2,1)S(1)} %copy-done.6, bf16[8,128,128]{2,1,0:T(8,128)(2,1)S(1)} %get-tuple-element.44.d_logit_ref, bf16[8,128,128]{2,1,0:T(8,128)(2,1)S(1)} %copy-done, f32[1,128]{1,0:T(1,128)S(1)} %bitcast.8, bf16[128,512]{1,0:T(8,128)(2,1)S(1)} %copy-done.2, bf16[128,128]{1,0:T(8,128)(2,1)S(1)} %copy-done.9), custom_call_target="tpu_custom_call" | custom-call | flops 2000000000 | bytes 1999360 | tf_op jit(solution)/shard_map/pair/pallas_call | solution.py:259
  93.5 5.0 %all-to-all-done.5.got_ref = bf16[16,8,640]{2,1,0:T(8,128)(2,1)S(1)} async-done(((bf16[16,8,640]{2,1,0:T(8,128)(2,1)}), bf16[16,8,640]{2,1,0:T(8,128)(2,1)S(1)}, u32[]{:S(2)}, u32[]{:S(2)}) %all-to-all-start.5) | async-done | bytes 163872 | tf_op jit(solution)/shard_map/all_to_all | solution.py:29
  98.5 0.7 finish.1
  (27 shorter events, 1.0 us)
Async XLA Ops:
  3.2 8.4 %copy-start.1 = (bf16[128,1024]{1,0:T(8,128)(2,1)S(1)}, bf16[128,1024]{1,0:T(8,128)(2,1)}, u32[]{:S(2)}) copy-start(bf16[128,1024]{1,0:T(8,128)(2,1)} %get-tuple-element.27.zn_ref) | copy-start | bytes 786436
  3.2 8.4 %copy-start.2 = (bf16[128,512]{1,0:T(8,128)(2,1)S(1)}, bf16[128,512]{1,0:T(8,128)(2,1)}, u32[]{:S(2)}) copy-start(bf16[128,512]{1,0:T(8,128)(2,1)} %w_ref.3) | copy-start | bytes 393220
  3.2 8.4 %copy-start.7 = (bf16[8,128,128]{2,1,0:T(8,128)(2,1)S(1)}, bf16[8,128,128]{2,1,0:T(8,128)(2,1)}, u32[]{:S(2)}) copy-start(bf16[8,128,128]{2,1,0:T(8,128)(2,1)} %adj_ref.3) | copy-start | bytes 786436
  3.2 8.4 %copy-start.8 = (bf16[128,128]{1,0:T(8,128)(2,1)S(1)}, bf16[128,128]{1,0:T(8,128)(2,1)}, u32[]{:S(2)}) copy-start(bf16[128,128]{1,0:T(8,128)(2,1)} %w_out_ref.3) | copy-start | bytes 98308
  3.2 8.4 %copy-start.9 = (bf16[128,128]{1,0:T(8,128)(2,1)S(1)}, bf16[128,128]{1,0:T(8,128)(2,1)}, u32[]{:S(2)}) copy-start(bf16[128,128]{1,0:T(8,128)(2,1)} %w_gate_ref.3) | copy-start | bytes 98308
  3.2 22.0 %all-to-all-start = ((bf16[16,128,128]{2,1,0:T(8,128)(2,1)}), bf16[16,128,128]{2,1,0:T(8,128)(2,1)S(1)}, u32[]{:S(2)}, u32[]{:S(2)}) async-start(bf16[16,128,128]{2,1,0:T(8,128)(2,1)} %get-tuple-element.26), calls=%async_computation | async-start | bytes 1048576 | tf_op jit(solution)/shard_map/all_to_all | solution.py:29
  10.8 0.7 copy-start.14
  11.6 0.7 copy-start.10
  11.6 0.7 copy-start.3
  11.6 0.7 copy-start.11
  13.8 0.8 copy-start.12
  40.7 13.5 %all-to-all-start.2 = ((bf16[16,64,128]{2,1,0:T(8,128)(2,1)}), bf16[16,64,128]{2,1,0:T(8,128)(2,1)S(1)}, u32[]{:S(2)}, u32[]{:S(2)}) async-start(bf16[16,64,128]{2,1,0:T(8,128)(2,1)} %get-tuple-element.36), calls=%async_computation.2 | async-start | bytes 524288 | tf_op jit(solution)/shard_map/all_to_all | solution.py:29
  44.2 1.0 %copy-start.13 = (f32[8,128,128]{2,1,0:T(8,128)S(1)}, f32[8,128,128]{2,1,0:T(8,128)}, u32[]{:S(2)}) copy-start(f32[8,128,128]{2,1,0:T(8,128)} %copy-done.12) | copy-start | bytes 1572868
  72.5 1.0 %copy-start.5 = (bf16[512,1024]{1,0:T(8,128)(2,1)}, bf16[512,1024]{1,0:T(8,128)(2,1)S(1)}, u32[]{:S(2)}) copy-start(bf16[512,1024]{1,0:T(8,128)(2,1)S(1)} %get-tuple-element.43.cells_ref) | copy-start | bytes 3145732
  85.9 4.2 %copy-start = (bf16[8,128,128]{2,1,0:T(8,128)(2,1)S(1)}, bf16[8,128,128]{2,1,0:T(8,128)(2,1)}, u32[]{:S(2)}) copy-start(bf16[8,128,128]{2,1,0:T(8,128)(2,1)} %pair_ref.1) | copy-start | bytes 786436
  86.6 12.0 %all-to-all-start.5 = ((bf16[16,8,640]{2,1,0:T(8,128)(2,1)}), bf16[16,8,640]{2,1,0:T(8,128)(2,1)S(1)}, u32[]{:S(2)}, u32[]{:S(2)}) async-start(bf16[16,8,640]{2,1,0:T(8,128)(2,1)} %sum.1), calls=%async_computation.5 | async-start | bytes 327680 | tf_op jit(solution)/shard_map/all_to_all | solution.py:29
  90.1 0.7 copy-start.4
  90.7 1.2 %copy-start.6 = (bf16[512,1024]{1,0:T(8,128)(2,1)S(1)}, bf16[512,1024]{1,0:T(8,128)(2,1)}, u32[]{:S(2)}) copy-start(bf16[512,1024]{1,0:T(8,128)(2,1)} %copy-done.5) | copy-start | bytes 3145732

commit v5 on v4

--- a/solution.py
+++ b/solution.py
@@ -334,6 +334,7 @@
     d_pair = call(pair_kernel, [shape(pair.shape, BF)], flops=2 * 10**9, name="pair")(
         d_cells, d_logit, pair, gain_in, w_proj, w_gate
     )[0]
+    got, d_pair = lax.optimization_barrier((got, d_pair))
     sent = call(
         functools.partial(sum_kernel, residues), [shape(got.shape, BF)], name="sum"
     )(got)[0]

time: 99.9 us -> 99.4 us (level)
  blocking collectives: 43.5 us -> 42.2 us
    all_to_all x3, blocking collectives: 43.5 us -> 42.2 us  [swap(): lax.all_to_all(blocks, ('wide', 'narrow'), split_axis=0, concat_axis=0, t...]
where the time goes in v5:
time: 99.4 us; the launch traced here: 98.7 us
  blocking collectives  42.2 us (42%)
  waiting for transfers between devices  23.6 us (24%)
  starting transfers between devices  15.3 us (15%)
  Pallas kernels  10.6 us (11%)
  local copies, waits for them, and re-layouts  6.13 us (6%)
    all_to_all x3, blocking collectives, swap(): lax.all_to_all(blocks, ('wide', 'narrow'), split_axis=0, concat_axis=0, t...  42.2 us
    all_to_all x3, waiting for transfers between devices, swap(): lax.all_to_all(blocks, ('wide', 'narrow'), split_axis=0, concat_axis=0, t...  23.6 us
    all_to_all x3, starting transfers between devices, swap(): lax.all_to_all(blocks, ('wide', 'narrow'), split_axis=0, concat_axis=0, t...  15.3 us
    pallas_call x10, Pallas kernels, run(): pl.pallas_call(kernel, out_shape=list(outs), in_specs=[pl.BlockSpec(memor...  10.6 us
    unnamed x30, local copies, waits for them, and re-layouts  6.06 us
  transfers between devices with their start and end apart: 3, of which 3 were waited for; matrix products, arithmetic and copies ran while one was open for 0% of the time, Pallas kernels for 4%

profile of v5, /device:TPU:0, one launch (start us, length us, event | category | flops | bytes accessed | tf_op | source)
XLA Modules:
  0.0 98.7 jit_solution(2126649534176125817)
XLA Ops:
  0.6 2.5 %project.1 = (bf16[16,128,128]{2,1,0:T(8,128)(2,1)}, bf16[128,1024]{1,0:T(8,128)(2,1)}, f32[8,128]{1,0:T(8,128)}) custom-call(bf16[8,128,128]{2,1,0:T(8,128)(2,1)} %pair_ref.1, s32[1,128]{1,0:T(1,128)} %bitcast.8, f32[1,128]{1,0:T(1,128)} %bitcast.6, bf16[128,512]{1,0:T(8,128)(2,1)} %w_ref.3), custom_call_target="tpu_custom_call" | custom-call | bytes 1184768 | tf_op jit(solution)/shard_map/project/pallas_call | solution.py:259
  3.2 7.5 %all-to-all-start = ((bf16[16,128,128]{2,1,0:T(8,128)(2,1)}), bf16[16,128,128]{2,1,0:T(8,128)(2,1)S(1)}, u32[]{:S(2)}, u32[]{:S(2)}) async-start(bf16[16,128,128]{2,1,0:T(8,128)(2,1)} %get-tuple-element.28), calls=%async_computation | async-start | bytes 1048576 | tf_op jit(solution)/shard_map/all_to_all | solution.py:29
  10.8 0.6 copy-done.14
  11.6 0.6 copy-done.10
  12.3 1.5 %gate.1 = (bf16[512,1024]{1,0:T(8,128)(2,1)S(1)}, f32[8,128,128]{2,1,0:T(8,128)S(1)}, bf16[128,1024]{1,0:T(8,128)(2,1)S(1)}) custom-call(bf16[128,1024]{1,0:T(8,128)(2,1)S(1)} %copy-done.1, bf16[8,128,128]{2,1,0:T(8,128)(2,1)S(1)} %copy-done.7, f32[8,128]{1,0:T(8,128)S(1)} %copy-done.10, f32[8,128]{1,0:T(8,128)S(1)} %compare_convert_fusion.same_ref, ...), custom_call_target="tpu_custom_call" | custom-call | flops 2000000000 | bytes 2565632 | tf_op jit(solution)/shard_map/gate/pallas_call | solution.py:259
  13.8 0.8 copy-done.12
  14.6 10.6 %all-to-all-done.got_ref = bf16[16,128,128]{2,1,0:T(8,128)(2,1)S(1)} async-done(((bf16[16,128,128]{2,1,0:T(8,128)(2,1)}), bf16[16,128,128]{2,1,0:T(8,128)(2,1)S(1)}, u32[]{:S(2)}, u32[]{:S(2)}) %all-to-all-start) | async-done | bytes 524320 | tf_op jit(solution)/shard_map/all_to_all | solution.py:29
  25.6 13.9 %all_to_all.30.got_ref = bf16[16,64,128]{2,1,0:T(8,128)(2,1)S(1)} all-to-all(bf16[16,64,128]{2,1,0:T(8,128)(2,1)S(1)} %get-tuple-element.33), channel_id=1, replica_groups=mesh['groups'=2,'wide'=16,'narrow'=1] {'wide','narrow'}, dimensions={0} | all-to-all | bytes 524288 | tf_op jit(solution)/shard_map/all_to_all | solution.py:29
  39.5 1.1 %norm.1 = (bf16[16,64,128]{2,1,0:T(8,128)(2,1)}, bf16[128,1024]{1,0:T(8,128)(2,1)S(1)}) custom-call(bf16[16,64,128]{2,1,0:T(8,128)(2,1)S(1)} %all_to_all.30.got_ref, bf16[128,1024]{1,0:T(8,128)(2,1)S(1)} %get-tuple-element.34.t_ref, f32[1,128]{1,0:T(1,128)S(1)} %bitcast.5), custom_call_target="tpu_custom_call" | custom-call | bytes 1049088 | tf_op jit(solution)/shard_map/norm/pallas_call | solution.py:259
  40.7 3.5 %all-to-all-start.2 = ((bf16[16,64,128]{2,1,0:T(8,128)(2,1)}), bf16[16,64,128]{2,1,0:T(8,128)(2,1)S(1)}, u32[]{:S(2)}, u32[]{:S(2)}) async-start(bf16[16,64,128]{2,1,0:T(8,128)(2,1)} %get-tuple-element.38), calls=%async_computation.2 | async-start | bytes 524288 | tf_op jit(solution)/shard_map/all_to_all | solution.py:29
  44.2 1.0 %copy-done.13 = f32[8,128,128]{2,1,0:T(8,128)S(1)} copy-done((f32[8,128,128]{2,1,0:T(8,128)S(1)}, f32[8,128,128]{2,1,0:T(8,128)}, u32[]{:S(2)}) %copy-start.13) | copy-done | bytes 524312
  45.2 1.0 %output.1 = (bf16[8,128,128]{2,1,0:T(8,128)(2,1)}, bf16[8,128,128]{2,1,0:T(8,128)(2,1)S(1)}, f32[128,128]{1,0:T(8,128)S(1)}) custom-call(bf16[128,1024]{1,0:T(8,128)(2,1)S(1)} %get-tuple-element.35.xn_ref, f32[8,128,128]{2,1,0:T(8,128)S(1)} %copy-done.13, bf16[8,128,128]{2,1,0:T(8,128)(2,1)S(1)} %copy-done.7, bf16[128,1024]{1,0:T(8,128)(2,1)S(1)} %copy-done.1, ...), custom_call_target="tpu_custom_call" | custom-call | flops 2000000000 | bytes 1933312 | tf_op jit(solution)/shard_map/output/pallas_call | solution.py:259
  46.3 7.9 %all-to-all-done.2.got_ref = bf16[16,64,128]{2,1,0:T(8,128)(2,1)S(1)} async-done(((bf16[16,64,128]{2,1,0:T(8,128)(2,1)}), bf16[16,64,128]{2,1,0:T(8,128)(2,1)S(1)}, u32[]{:S(2)}, u32[]{:S(2)}) %all-to-all-start.2) | async-done | bytes 262176 | tf_op jit(solution)/shard_map/all_to_all | solution.py:29
  54.2 0.4 unmix.1
  54.6 17.2 %all_to_all.31.got_ref = bf16[16,128,128]{2,1,0:T(8,128)(2,1)S(1)} all-to-all(bf16[16,128,128]{2,1,0:T(8,128)(2,1)S(1)} %unmix.1), channel_id=1, replica_groups=mesh['groups'=2,'wide'=16,'narrow'=1] {'wide','narrow'}, dimensions={0} | all-to-all | bytes 1048576 | tf_op jit(solution)/shard_map/all_to_all | solution.py:29
  71.9 1.3 %cells.1 = (bf16[512,1024]{1,0:T(8,128)(2,1)S(1)}, bf16[128,640]{1,0:T(8,128)(2,1)}) custom-call(bf16[16,128,128]{2,1,0:T(8,128)(2,1)S(1)} %all_to_all.31.got_ref, bf16[512,1024]{1,0:T(8,128)(2,1)S(1)} %get-tuple-element.43.factor_ref, bf16[128,1024]{1,0:T(8,128)(2,1)S(1)} %copy-done.1, f32[128,128]{1,0:T(8,128)S(1)} %get-tuple-element.44.gate_part_ref), custom_call_target="tpu_custom_call" | custom-call | bytes 3112960 | tf_op jit(solution)/shard_map/cells/pallas_call | solution.py:259
  73.2 1.0 %copy-done.5 = bf16[512,1024]{1,0:T(8,128)(2,1)} copy-done((bf16[512,1024]{1,0:T(8,128)(2,1)}, bf16[512,1024]{1,0:T(8,128)(2,1)S(1)}, u32[]{:S(2)}) %copy-start.5) | copy-done | bytes 1048600
  74.2 4.2 %all-to-all-start.4 = ((bf16[16,8,640]{2,1,0:T(8,128)(2,1)}), bf16[16,8,640]{2,1,0:T(8,128)(2,1)S(1)}, u32[]{:S(2)}, u32[]{:S(2)}) async-start(bf16[16,8,640]{2,1,0:T(8,128)(2,1)} %bitcast.3), calls=%async_computation.4 | async-start | bytes 327680 | tf_op jit(solution)/shard_map/all_to_all | solution.py:29
  78.4 0.6 copy-done.4
  79.1 1.2 %copy-done.6 = bf16[512,1024]{1,0:T(8,128)(2,1)S(1)} copy-done((bf16[512,1024]{1,0:T(8,128)(2,1)S(1)}, bf16[512,1024]{1,0:T(8,128)(2,1)}, u32[]{:S(2)}) %copy-start.6) | copy-done | bytes 1048600
  80.3 1.5 %pair.1 = bf16[8,128,128]{2,1,0:T(8,128)(2,1)} custom-call(bf16[512,1024]{1,0:T(8,128)(2,1)S(1)} %copy-done.6, bf16[8,128,128]{2,1,0:T(8,128)(2,1)S(1)} %get-tuple-element.47.d_logit_ref, bf16[8,128,128]{2,1,0:T(8,128)(2,1)S(1)} %copy-done, f32[1,128]{1,0:T(1,128)S(1)} %bitcast.7, bf16[128,512]{1,0:T(8,128)(2,1)S(1)} %copy-done.2, bf16[128,128]{1,0:T(8,128)(2,1)S(1)} %copy-done.9), custom_call_target="tpu_custom_call" | custom-call | flops 2000000000 | bytes 1999360 | tf_op jit(solution)/shard_map/pair/pallas_call | solution.py:259
  81.8 5.1 %all-to-all-done.4.got_ref = bf16[16,8,640]{2,1,0:T(8,128)(2,1)S(1)} async-done(((bf16[16,8,640]{2,1,0:T(8,128)(2,1)}), bf16[16,8,640]{2,1,0:T(8,128)(2,1)S(1)}, u32[]{:S(2)}, u32[]{:S(2)}) %all-to-all-start.4) | async-done | bytes 163872 | tf_op jit(solution)/shard_map/all_to_all | solution.py:29
  86.9 11.1 %all_to_all.32.got_ref = bf16[16,8,640]{2,1,0:T(8,128)(2,1)S(1)} all-to-all(bf16[16,8,640]{2,1,0:T(8,128)(2,1)S(1)} %sum.1), channel_id=1, replica_groups=mesh['groups'=2,'wide'=16,'narrow'=1] {'wide','narrow'}, dimensions={0} | all-to-all | bytes 327680 | tf_op jit(solution)/shard_map/all_to_all | solution.py:29
  98.0 0.7 finish.1
  (27 shorter events, 0.6 us)
Async XLA Ops:
  3.2 8.4 %copy-start.1 = (bf16[128,1024]{1,0:T(8,128)(2,1)S(1)}, bf16[128,1024]{1,0:T(8,128)(2,1)}, u32[]{:S(2)}) copy-start(bf16[128,1024]{1,0:T(8,128)(2,1)} %get-tuple-element.29.zn_ref) | copy-start | bytes 786436
  3.2 8.4 %copy-start.2 = (bf16[128,512]{1,0:T(8,128)(2,1)S(1)}, bf16[128,512]{1,0:T(8,128)(2,1)}, u32[]{:S(2)}) copy-start(bf16[128,512]{1,0:T(8,128)(2,1)} %w_ref.3) | copy-start | bytes 393220
  3.2 8.4 %copy-start.7 = (bf16[8,128,128]{2,1,0:T(8,128)(2,1)S(1)}, bf16[8,128,128]{2,1,0:T(8,128)(2,1)}, u32[]{:S(2)}) copy-start(bf16[8,128,128]{2,1,0:T(8,128)(2,1)} %adj_ref.3) | copy-start | bytes 786436
  3.2 8.4 %copy-start.8 = (bf16[128,128]{1,0:T(8,128)(2,1)S(1)}, bf16[128,128]{1,0:T(8,128)(2,1)}, u32[]{:S(2)}) copy-start(bf16[128,128]{1,0:T(8,128)(2,1)} %w_out_ref.3) | copy-start | bytes 98308
  3.2 8.4 %copy-start.9 = (bf16[128,128]{1,0:T(8,128)(2,1)S(1)}, bf16[128,128]{1,0:T(8,128)(2,1)}, u32[]{:S(2)}) copy-start(bf16[128,128]{1,0:T(8,128)(2,1)} %w_gate_ref.3) | copy-start | bytes 98308
  3.2 22.0 %all-to-all-start = ((bf16[16,128,128]{2,1,0:T(8,128)(2,1)}), bf16[16,128,128]{2,1,0:T(8,128)(2,1)S(1)}, u32[]{:S(2)}, u32[]{:S(2)}) async-start(bf16[16,128,128]{2,1,0:T(8,128)(2,1)} %get-tuple-element.28), calls=%async_computation | async-start | bytes 1048576 | tf_op jit(solution)/shard_map/all_to_all | solution.py:29
  10.8 0.7 copy-start.14
  11.6 0.7 copy-start.10
  11.6 0.7 copy-start.3
  11.6 0.7 copy-start.11
  13.8 0.8 copy-start.12
  40.7 13.5 %all-to-all-start.2 = ((bf16[16,64,128]{2,1,0:T(8,128)(2,1)}), bf16[16,64,128]{2,1,0:T(8,128)(2,1)S(1)}, u32[]{:S(2)}, u32[]{:S(2)}) async-start(bf16[16,64,128]{2,1,0:T(8,128)(2,1)} %get-tuple-element.38), calls=%async_computation.2 | async-start | bytes 524288 | tf_op jit(solution)/shard_map/all_to_all | solution.py:29
  44.2 1.0 %copy-start.13 = (f32[8,128,128]{2,1,0:T(8,128)S(1)}, f32[8,128,128]{2,1,0:T(8,128)}, u32[]{:S(2)}) copy-start(f32[8,128,128]{2,1,0:T(8,128)} %copy-done.12) | copy-start | bytes 1572868
  73.2 1.0 %copy-start.5 = (bf16[512,1024]{1,0:T(8,128)(2,1)}, bf16[512,1024]{1,0:T(8,128)(2,1)S(1)}, u32[]{:S(2)}) copy-start(bf16[512,1024]{1,0:T(8,128)(2,1)S(1)} %get-tuple-element.46.cells_ref) | copy-start | bytes 3145732
  74.2 4.3 %copy-start = (bf16[8,128,128]{2,1,0:T(8,128)(2,1)S(1)}, bf16[8,128,128]{2,1,0:T(8,128)(2,1)}, u32[]{:S(2)}) copy-start(bf16[8,128,128]{2,1,0:T(8,128)(2,1)} %pair_ref.1) | copy-start | bytes 786436
  74.2 12.7 %all-to-all-start.4 = ((bf16[16,8,640]{2,1,0:T(8,128)(2,1)}), bf16[16,8,640]{2,1,0:T(8,128)(2,1)S(1)}, u32[]{:S(2)}, u32[]{:S(2)}) async-start(bf16[16,8,640]{2,1,0:T(8,128)(2,1)} %bitcast.3), calls=%async_computation.4 | async-start | bytes 327680 | tf_op jit(solution)/shard_map/all_to_all | solution.py:29
  78.4 0.7 copy-start.4
  79.1 1.2 %copy-start.6 = (bf16[512,1024]{1,0:T(8,128)(2,1)S(1)}, bf16[512,1024]{1,0:T(8,128)(2,1)}, u32[]{:S(2)}) copy-start(bf16[512,1024]{1,0:T(8,128)(2,1)} %copy-done.5) | copy-start | bytes 3145732

commit v6 on v5

--- a/solution.py
+++ b/solution.py
@@ -209,7 +209,9 @@
     sent_ref[:, half:, :] = right_s[...].reshape(devices, half, cols).astype(BF)
 
 
-def cells_kernel(got_ref, factor_ref, zn_ref, gate_part_ref, cells_ref, part_ref):
+def cells_kernel(
+    got_ref, factor_ref, zn_ref, gate_part_ref, w_ref, d_zn_ref, part_ref, cells_ref
+):
     devices, depth, cols = got_ref.shape
     half = depth // 2
     hidden = factor_ref.shape[0] // 4
@@ -225,15 +227,16 @@
     total = dot(zn_ref[...], cells_ref[...], ((1,), (1,)))
     part_ref[:, : 4 * hidden] = total.astype(BF)
     part_ref[:, 4 * hidden :] = gate_part_ref[...].astype(BF)
-
-
-def pair_kernel(cells_ref, d_logit_ref, pair_ref, gain_ref, w_ref, w_gate_ref, d_pair_ref):
+    d_zn_ref[...] = dot(w_ref[...], cells_ref[...]).astype(BF)
+
+
+def pair_kernel(d_zn_ref, d_logit_ref, pair_ref, gain_ref, w_gate_ref, d_pair_ref):
     rows, cols, width = pair_ref.shape
     gain = column(gain_ref[...])
     for row in range(rows):
         lanes = slice(row * cols, (row + 1) * cols)
         hat, rstd = centred(pair_ref[row].astype(F32).T)
-        d_zn = dot(w_ref[...], cells_ref[:, lanes])
+        d_zn = d_zn_ref[:, lanes].astype(F32)
         d_zn = d_zn + dot(w_gate_ref[...], d_logit_ref[row], ((1,), (1,)))
         d_pair_ref[row] = back_t(d_zn * gain, hat, rstd).T.astype(BF)
 
@@ -325,14 +328,15 @@
         unmix_kernel, [shape((devices, 2 * half, cols), BF)], [field] * 3, name="unmix"
     )(got, left, right)[0]
     got = swap(sent)
-    d_cells, part = call(
+    d_zn, part = call(
         cells_kernel,
-        [shape((4 * hidden, cells), BF), shape((width, 4 * hidden + width), BF)],
+        [shape((width, cells), BF), shape((width, 4 * hidden + width), BF)],
+        [pltpu.VMEM((4 * hidden, cells), BF)],
         name="cells",
-    )(got, factor, zn, gate_part)
+    )(got, factor, zn, gate_part, w_proj)
     got = swap(part.reshape(devices, width // devices, -1))
     d_pair = call(pair_kernel, [shape(pair.shape, BF)], flops=2 * 10**9, name="pair")(
-        d_cells, d_logit, pair, gain_in, w_proj, w_gate
+        d_zn, d_logit, pair, gain_in, w_gate
     )[0]
     got, d_pair = lax.optimization_barrier((got, d_pair))
     sent = call(

time: 99.4 us -> 98.4 us (0.990)
  local copies, waits for them, and re-layouts: 6.13 us -> 3.89 us
  waiting for transfers between devices: 23.6 us -> 25 us
    unnamed x30 -> x26, local copies, waits for them, and re-layouts: 6.06 us -> 3.82 us
    all_to_all x3, waiting for transfers between devices: 23.6 us -> 25 us  [swap(): lax.all_to_all(blocks, ('wide', 'narrow'), split_axis=0, concat_axis=0, t...]
where the time goes in v6:
time: 98.4 us; the launch traced here: 97.8 us
  blocking collectives  42.2 us (43%)
  waiting for transfers between devices  25 us (25%)
  starting transfers between devices  15.3 us (16%)
  Pallas kernels  10.4 us (11%)
  local copies, waits for them, and re-layouts  3.89 us (4%)
    all_to_all x3, blocking collectives, swap(): lax.all_to_all(blocks, ('wide', 'narrow'), split_axis=0, concat_axis=0, t...  42.2 us
    all_to_all x3, waiting for transfers between devices, swap(): lax.all_to_all(blocks, ('wide', 'narrow'), split_axis=0, concat_axis=0, t...  25 us
    all_to_all x3, starting transfers between devices, swap(): lax.all_to_all(blocks, ('wide', 'narrow'), split_axis=0, concat_axis=0, t...  15.3 us
    pallas_call x10, Pallas kernels, run(): pl.pallas_call(kernel, out_shape=list(outs), in_specs=[pl.BlockSpec(memor...  10.4 us
    unnamed x26, local copies, waits for them, and re-layouts  3.82 us
  transfers between devices with their start and end apart: 3, of which 3 were waited for; matrix products, arithmetic and copies ran while one was open for 0% of the time, Pallas kernels for 4%

profile of v6, /device:TPU:0, one launch (start us, length us, event | category | flops | bytes accessed | tf_op | source)
XLA Modules:
  0.0 97.8 jit_solution(18019137256246037738)
XLA Ops:
  0.6 2.5 %project.1 = (bf16[16,128,128]{2,1,0:T(8,128)(2,1)}, bf16[128,1024]{1,0:T(8,128)(2,1)}, f32[8,128]{1,0:T(8,128)}) custom-call(bf16[8,128,128]{2,1,0:T(8,128)(2,1)} %pair_ref.1, s32[1,128]{1,0:T(1,128)} %bitcast.8, f32[1,128]{1,0:T(1,128)} %bitcast.6, bf16[128,512]{1,0:T(8,128)(2,1)} %w_ref.3), custom_call_target="tpu_custom_call" | custom-call | bytes 1184768 | tf_op jit(solution)/shard_map/project/pallas_call | solution.py:262
  3.2 7.5 %all-to-all-start = ((bf16[16,128,128]{2,1,0:T(8,128)(2,1)}), bf16[16,128,128]{2,1,0:T(8,128)(2,1)S(1)}, u32[]{:S(2)}, u32[]{:S(2)}) async-start(bf16[16,128,128]{2,1,0:T(8,128)(2,1)} %get-tuple-element.28), calls=%async_computation | async-start | bytes 1048576 | tf_op jit(solution)/shard_map/all_to_all | solution.py:29
  10.8 0.6 copy-done.12
  11.4 0.1 dynamic_slice.3
  11.6 0.6 copy-done.8
  12.3 1.5 %gate.1 = (bf16[512,1024]{1,0:T(8,128)(2,1)S(1)}, f32[8,128,128]{2,1,0:T(8,128)S(1)}, bf16[128,1024]{1,0:T(8,128)(2,1)S(1)}) custom-call(bf16[128,1024]{1,0:T(8,128)(2,1)S(1)} %copy-done.2, bf16[8,128,128]{2,1,0:T(8,128)(2,1)S(1)} %copy-done.5, f32[8,128]{1,0:T(8,128)S(1)} %copy-done.8, f32[8,128]{1,0:T(8,128)S(1)} %compare_convert_fusion.same_ref, ...), custom_call_target="tpu_custom_call" | custom-call | flops 2000000000 | bytes 2565632 | tf_op jit(solution)/shard_map/gate/pallas_call | solution.py:262
  13.8 0.8 copy-done.10
  14.6 10.6 %all-to-all-done.got_ref = bf16[16,128,128]{2,1,0:T(8,128)(2,1)S(1)} async-done(((bf16[16,128,128]{2,1,0:T(8,128)(2,1)}), bf16[16,128,128]{2,1,0:T(8,128)(2,1)S(1)}, u32[]{:S(2)}, u32[]{:S(2)}) %all-to-all-start) | async-done | bytes 524320 | tf_op jit(solution)/shard_map/all_to_all | solution.py:29
  25.2 0.4 mix.1
  25.6 13.9 %all_to_all.30.got_ref = bf16[16,64,128]{2,1,0:T(8,128)(2,1)S(1)} all-to-all(bf16[16,64,128]{2,1,0:T(8,128)(2,1)S(1)} %get-tuple-element.33), channel_id=1, replica_groups=mesh['groups'=2,'wide'=16,'narrow'=1] {'wide','narrow'}, dimensions={0} | all-to-all | bytes 524288 | tf_op jit(solution)/shard_map/all_to_all | solution.py:29
  39.5 1.1 %norm.1 = (bf16[16,64,128]{2,1,0:T(8,128)(2,1)}, bf16[128,1024]{1,0:T(8,128)(2,1)S(1)}) custom-call(bf16[16,64,128]{2,1,0:T(8,128)(2,1)S(1)} %all_to_all.30.got_ref, bf16[128,1024]{1,0:T(8,128)(2,1)S(1)} %get-tuple-element.34.t_ref, f32[1,128]{1,0:T(1,128)S(1)} %bitcast.5), custom_call_target="tpu_custom_call" | custom-call | bytes 1049088 | tf_op jit(solution)/shard_map/norm/pallas_call | solution.py:262
  40.7 3.5 %all-to-all-start.2 = ((bf16[16,64,128]{2,1,0:T(8,128)(2,1)}), bf16[16,64,128]{2,1,0:T(8,128)(2,1)S(1)}, u32[]{:S(2)}, u32[]{:S(2)}) async-start(bf16[16,64,128]{2,1,0:T(8,128)(2,1)} %get-tuple-element.38), calls=%async_computation.2 | async-start | bytes 524288 | tf_op jit(solution)/shard_map/all_to_all | solution.py:29
  44.2 1.0 %copy-done.11 = f32[8,128,128]{2,1,0:T(8,128)S(1)} copy-done((f32[8,128,128]{2,1,0:T(8,128)S(1)}, f32[8,128,128]{2,1,0:T(8,128)}, u32[]{:S(2)}) %copy-start.11) | copy-done | bytes 524312
  45.2 1.0 %output.1 = (bf16[8,128,128]{2,1,0:T(8,128)(2,1)}, bf16[8,128,128]{2,1,0:T(8,128)(2,1)S(1)}, f32[128,128]{1,0:T(8,128)S(1)}) custom-call(bf16[128,1024]{1,0:T(8,128)(2,1)S(1)} %get-tuple-element.35.xn_ref, f32[8,128,128]{2,1,0:T(8,128)S(1)} %copy-done.11, bf16[8,128,128]{2,1,0:T(8,128)(2,1)S(1)} %copy-done.5, bf16[128,1024]{1,0:T(8,128)(2,1)S(1)} %copy-done.2, ...), custom_call_target="tpu_custom_call" | custom-call | flops 2000000000 | bytes 1933312 | tf_op jit(solution)/shard_map/output/pallas_call | solution.py:262
  46.3 7.9 %all-to-all-done.2.got_ref = bf16[16,64,128]{2,1,0:T(8,128)(2,1)S(1)} async-done(((bf16[16,64,128]{2,1,0:T(8,128)(2,1)}), bf16[16,64,128]{2,1,0:T(8,128)(2,1)S(1)}, u32[]{:S(2)}, u32[]{:S(2)}) %all-to-all-start.2) | async-done | bytes 262176 | tf_op jit(solution)/shard_map/all_to_all | solution.py:29
  54.2 0.4 unmix.1
  54.6 17.2 %all_to_all.31.got_ref = bf16[16,128,128]{2,1,0:T(8,128)(2,1)S(1)} all-to-all(bf16[16,128,128]{2,1,0:T(8,128)(2,1)S(1)} %unmix.1), channel_id=1, replica_groups=mesh['groups'=2,'wide'=16,'narrow'=1] {'wide','narrow'}, dimensions={0} | all-to-all | bytes 1048576 | tf_op jit(solution)/shard_map/all_to_all | solution.py:29
  71.9 1.4 %cells.1 = (bf16[128,1024]{1,0:T(8,128)(2,1)S(1)}, bf16[128,640]{1,0:T(8,128)(2,1)}) custom-call(bf16[16,128,128]{2,1,0:T(8,128)(2,1)S(1)} %all_to_all.31.got_ref, bf16[512,1024]{1,0:T(8,128)(2,1)S(1)} %get-tuple-element.43.factor_ref, bf16[128,1024]{1,0:T(8,128)(2,1)S(1)} %copy-done.2, f32[128,128]{1,0:T(8,128)S(1)} %get-tuple-element.44.gate_part_ref, ...), custom_call_target="tpu_custom_call" | custom-call | bytes 2457600 | tf_op jit(solution)/shard_map/cells/pallas_call | solution.py:262
  73.2 4.2 %all-to-all-start.4 = ((bf16[16,8,640]{2,1,0:T(8,128)(2,1)}), bf16[16,8,640]{2,1,0:T(8,128)(2,1)S(1)}, u32[]{:S(2)}, u32[]{:S(2)}) async-start(bf16[16,8,640]{2,1,0:T(8,128)(2,1)} %bitcast.3), calls=%async_computation.4 | async-start | bytes 327680 | tf_op jit(solution)/shard_map/all_to_all | solution.py:29
  77.5 0.6 copy-done.4
  78.1 1.3 %pair.1 = bf16[8,128,128]{2,1,0:T(8,128)(2,1)} custom-call(bf16[128,1024]{1,0:T(8,128)(2,1)S(1)} %get-tuple-element.46.d_zn_ref, bf16[8,128,128]{2,1,0:T(8,128)(2,1)S(1)} %get-tuple-element.47.d_logit_ref, bf16[8,128,128]{2,1,0:T(8,128)(2,1)S(1)} %copy-done.1, f32[1,128]{1,0:T(1,128)S(1)} %bitcast.7, bf16[128,128]{1,0:T(8,128)(2,1)S(1)} %copy-done.7), custom_call_target="tpu_custom_call" | custom-call | flops 2000000000 | bytes 1081856 | tf_op jit(solution)/shard_map/pair/pallas_call | solution.py:262
  79.4 6.5 %all-to-all-done.4.got_ref = bf16[16,8,640]{2,1,0:T(8,128)(2,1)S(1)} async-done(((bf16[16,8,640]{2,1,0:T(8,128)(2,1)}), bf16[16,8,640]{2,1,0:T(8,128)(2,1)S(1)}, u32[]{:S(2)}, u32[]{:S(2)}) %all-to-all-start.4) | async-done | bytes 163872 | tf_op jit(solution)/shard_map/all_to_all | solution.py:29
  86.0 11.1 %all_to_all.32.got_ref = bf16[16,8,640]{2,1,0:T(8,128)(2,1)S(1)} all-to-all(bf16[16,8,640]{2,1,0:T(8,128)(2,1)S(1)} %sum.1), channel_id=1, replica_groups=mesh['groups'=2,'wide'=16,'narrow'=1] {'wide','narrow'}, dimensions={0} | all-to-all | bytes 327680 | tf_op jit(solution)/shard_map/all_to_all | solution.py:29
  97.0 0.7 finish.1
  (23 shorter events, 0.2 us)
Async XLA Ops:
  3.2 8.4 %copy-start = (bf16[128,512]{1,0:T(8,128)(2,1)S(1)}, bf16[128,512]{1,0:T(8,128)(2,1)}, u32[]{:S(2)}) copy-start(bf16[128,512]{1,0:T(8,128)(2,1)} %w_ref.3) | copy-start | bytes 393220
  3.2 8.4 %copy-start.2 = (bf16[128,1024]{1,0:T(8,128)(2,1)S(1)}, bf16[128,1024]{1,0:T(8,128)(2,1)}, u32[]{:S(2)}) copy-start(bf16[128,1024]{1,0:T(8,128)(2,1)} %get-tuple-element.29.zn_ref) | copy-start | bytes 786436
  3.2 8.4 %copy-start.5 = (bf16[8,128,128]{2,1,0:T(8,128)(2,1)S(1)}, bf16[8,128,128]{2,1,0:T(8,128)(2,1)}, u32[]{:S(2)}) copy-start(bf16[8,128,128]{2,1,0:T(8,128)(2,1)} %adj_ref.3) | copy-start | bytes 786436
  3.2 8.4 %copy-start.6 = (bf16[128,128]{1,0:T(8,128)(2,1)S(1)}, bf16[128,128]{1,0:T(8,128)(2,1)}, u32[]{:S(2)}) copy-start(bf16[128,128]{1,0:T(8,128)(2,1)} %w_out_ref.3) | copy-start | bytes 98308
  3.2 8.4 %copy-start.7 = (bf16[128,128]{1,0:T(8,128)(2,1)S(1)}, bf16[128,128]{1,0:T(8,128)(2,1)}, u32[]{:S(2)}) copy-start(bf16[128,128]{1,0:T(8,128)(2,1)} %w_gate_ref.3) | copy-start | bytes 98308
  3.2 22.0 %all-to-all-start = ((bf16[16,128,128]{2,1,0:T(8,128)(2,1)}), bf16[16,128,128]{2,1,0:T(8,128)(2,1)S(1)}, u32[]{:S(2)}, u32[]{:S(2)}) async-start(bf16[16,128,128]{2,1,0:T(8,128)(2,1)} %get-tuple-element.28), calls=%async_computation | async-start | bytes 1048576 | tf_op jit(solution)/shard_map/all_to_all | solution.py:29
  10.7 0.7 copy-start.12
  11.6 0.7 copy-start.8
  11.6 0.7 copy-start.3
  11.6 0.7 copy-start.9
  13.8 0.8 copy-start.10
  40.7 13.5 %all-to-all-start.2 = ((bf16[16,64,128]{2,1,0:T(8,128)(2,1)}), bf16[16,64,128]{2,1,0:T(8,128)(2,1)S(1)}, u32[]{:S(2)}, u32[]{:S(2)}) async-start(bf16[16,64,128]{2,1,0:T(8,128)(2,1)} %get-tuple-element.38), calls=%async_computation.2 | async-start | bytes 524288 | tf_op jit(solution)/shard_map/all_to_all | solution.py:29
  44.2 1.0 %copy-start.11 = (f32[8,128,128]{2,1,0:T(8,128)S(1)}, f32[8,128,128]{2,1,0:T(8,128)}, u32[]{:S(2)}) copy-start(f32[8,128,128]{2,1,0:T(8,128)} %copy-done.10) | copy-start | bytes 1572868
  73.2 4.3 %copy-start.1 = (bf16[8,128,128]{2,1,0:T(8,128)(2,1)S(1)}, bf16[8,128,128]{2,1,0:T(8,128)(2,1)}, u32[]{:S(2)}) copy-start(bf16[8,128,128]{2,1,0:T(8,128)(2,1)} %pair_ref.1) | copy-start | bytes 786436
  73.2 12.7 %all-to-all-start.4 = ((bf16[16,8,640]{2,1,0:T(8,128)(2,1)}), bf16[16,8,640]{2,1,0:T(8,128)(2,1)S(1)}, u32[]{:S(2)}, u32[]{:S(2)}) async-start(bf16[16,8,640]{2,1,0:T(8,128)(2,1)} %bitcast.3), calls=%async_computation.4 | async-start | bytes 327680 | tf_op jit(solution)/shard_map/all_to_all | solution.py:29
  77.5 0.7 copy-start.4

commit v7 on v6

--- a/solution.py
+++ b/solution.py
@@ -145,7 +145,8 @@
         gate = jax.nn.sigmoid(dot(w_gate, zn) + bias).T
         gate_ref[row] = gate
         d_out = (adj_ref[row].astype(F32) * gate).astype(BF)
-        t_ref[:, lanes] = (dot(w_out_ref[...], d_out, ((1,), (1,))) * gain).astype(BF)
+        t = dot(w_out_ref[...], d_out, ((1,), (1,))) * gain
+        t_ref[:, lanes] = (t - jnp.mean(t, 0, keepdims=True)).astype(BF)
 
 
 def mix_kernel(got_ref, sent_ref, left_ref, right_ref, left_s, right_s, out_s):
@@ -210,7 +211,7 @@
 
 
 def cells_kernel(
-    got_ref, factor_ref, zn_ref, gate_part_ref, w_ref, d_zn_ref, part_ref, cells_ref
+    got_ref, factor_ref, zn_ref, gate_part_ref, w_ref, gain_ref, u_ref, part_ref, cells_ref
 ):
     devices, depth, cols = got_ref.shape
     half = depth // 2
@@ -227,18 +228,19 @@
     total = dot(zn_ref[...], cells_ref[...], ((1,), (1,)))
     part_ref[:, : 4 * hidden] = total.astype(BF)
     part_ref[:, 4 * hidden :] = gate_part_ref[...].astype(BF)
-    d_zn_ref[...] = dot(w_ref[...], cells_ref[...]).astype(BF)
-
-
-def pair_kernel(d_zn_ref, d_logit_ref, pair_ref, gain_ref, w_gate_ref, d_pair_ref):
+    u = dot(w_ref[...], cells_ref[...]) * column(gain_ref[...])[:, :1]
+    u_ref[...] = (u - jnp.mean(u, 0, keepdims=True)).astype(BF)
+
+
+def pair_kernel(u_ref, d_logit_ref, pair_ref, gain_ref, w_gate_ref, d_pair_ref):
     rows, cols, width = pair_ref.shape
     gain = column(gain_ref[...])
     for row in range(rows):
         lanes = slice(row * cols, (row + 1) * cols)
         hat, rstd = centred(pair_ref[row].astype(F32).T)
-        d_zn = d_zn_ref[:, lanes].astype(F32)
-        d_zn = d_zn + dot(w_gate_ref[...], d_logit_ref[row], ((1,), (1,)))
-        d_pair_ref[row] = back_t(d_zn * gain, hat, rstd).T.astype(BF)
+        u = dot(w_gate_ref[...], d_logit_ref[row], ((1,), (1,))) * gain
+        u = u + u_ref[:, lanes].astype(F32)
+        d_pair_ref[row] = back_t(u, hat, rstd).T.astype(BF)
 
 
 def sum_kernel(residues, got_ref, sent_ref):
@@ -328,15 +330,15 @@
         unmix_kernel, [shape((devices, 2 * half, cols), BF)], [field] * 3, name="unmix"
     )(got, left, right)[0]
     got = swap(sent)
-    d_zn, part = call(
+    u, part = call(
         cells_kernel,
         [shape((width, cells), BF), shape((width, 4 * hidden + width), BF)],
         [pltpu.VMEM((4 * hidden, cells), BF)],
         name="cells",
-    )(got, factor, zn, gate_part, w_proj)
+    )(got, factor, zn, gate_part, w_proj, gain_in)
     got = swap(part.reshape(devices, width // devices, -1))
     d_pair = call(pair_kernel, [shape(pair.shape, BF)], flops=2 * 10**9, name="pair")(
-        d_zn, d_logit, pair, gain_in, w_gate
+        u, d_logit, pair, gain_in, w_gate
     )[0]
     got, d_pair = lax.optimization_barrier((got, d_pair))
     sent = call(

time: 98.4 us -> 99.1 us (level)
  no operation moved by 1% of the time
where the time goes in v7:
time: 99.1 us; the launch traced here: 98.4 us
  blocking collectives  42.2 us (43%)
  waiting for transfers between devices  25.6 us (26%)
  starting transfers between devices  15.3 us (15%)
  Pallas kernels  10.5 us (11%)
  local copies, waits for them, and re-layouts  3.91 us (4%)
    all_to_all x3, blocking collectives, swap(): lax.all_to_all(blocks, ('wide', 'narrow'), split_axis=0, concat_axis=0, t...  42.2 us
    all_to_all x3, waiting for transfers between devices, swap(): lax.all_to_all(blocks, ('wide', 'narrow'), split_axis=0, concat_axis=0, t...  25.6 us
    all_to_all x3, starting transfers between devices, swap(): lax.all_to_all(blocks, ('wide', 'narrow'), split_axis=0, concat_axis=0, t...  15.3 us
    pallas_call x10, Pallas kernels, run(): pl.pallas_call(kernel, out_shape=list(outs), in_specs=[pl.BlockSpec(memor...  10.5 us
    unnamed x26, local copies, waits for them, and re-layouts  3.83 us
  transfers between devices with their start and end apart: 3, of which 3 were waited for; matrix products, arithmetic and copies ran while one was open for 0% of the time, Pallas kernels for 4%

profile of v7, /device:TPU:0, one launch (start us, length us, event | category | flops | bytes accessed | tf_op | source)
XLA Modules:
  0.0 98.4 jit_solution(10419011886516009646)
XLA Ops:
  0.6 2.5 %project.1 = (bf16[16,128,128]{2,1,0:T(8,128)(2,1)}, bf16[128,1024]{1,0:T(8,128)(2,1)}, f32[8,128]{1,0:T(8,128)}) custom-call(bf16[8,128,128]{2,1,0:T(8,128)(2,1)} %pair_ref.1, s32[1,128]{1,0:T(1,128)} %bitcast.9, f32[1,128]{1,0:T(1,128)} %bitcast.4, bf16[128,512]{1,0:T(8,128)(2,1)} %w_ref.3), custom_call_target="tpu_custom_call" | custom-call | bytes 1184768 | tf_op jit(solution)/shard_map/project/pallas_call | solution.py:264
  3.2 7.5 %all-to-all-start = ((bf16[16,128,128]{2,1,0:T(8,128)(2,1)}), bf16[16,128,128]{2,1,0:T(8,128)(2,1)S(1)}, u32[]{:S(2)}, u32[]{:S(2)}) async-start(bf16[16,128,128]{2,1,0:T(8,128)(2,1)} %get-tuple-element.28), calls=%async_computation | async-start | bytes 1048576 | tf_op jit(solution)/shard_map/all_to_all | solution.py:29
  10.8 0.6 copy-done.12
  11.5 0.1 compare_convert_fusion.same_ref
  11.6 0.6 copy-done.8
  12.3 1.6 %gate.1 = (bf16[512,1024]{1,0:T(8,128)(2,1)S(1)}, f32[8,128,128]{2,1,0:T(8,128)S(1)}, bf16[128,1024]{1,0:T(8,128)(2,1)S(1)}) custom-call(bf16[128,1024]{1,0:T(8,128)(2,1)S(1)} %copy-done.1, bf16[8,128,128]{2,1,0:T(8,128)(2,1)S(1)} %copy-done.5, f32[8,128]{1,0:T(8,128)S(1)} %copy-done.8, f32[8,128]{1,0:T(8,128)S(1)} %compare_convert_fusion.same_ref, ...), custom_call_target="tpu_custom_call" | custom-call | flops 2000000000 | bytes 2565632 | tf_op jit(solution)/shard_map/gate/pallas_call | solution.py:264
  13.8 0.8 copy-done.10
  14.6 10.6 %all-to-all-done.got_ref = bf16[16,128,128]{2,1,0:T(8,128)(2,1)S(1)} async-done(((bf16[16,128,128]{2,1,0:T(8,128)(2,1)}), bf16[16,128,128]{2,1,0:T(8,128)(2,1)S(1)}, u32[]{:S(2)}, u32[]{:S(2)}) %all-to-all-start) | async-done | bytes 524320 | tf_op jit(solution)/shard_map/all_to_all | solution.py:29
  25.2 0.4 mix.1
  25.6 13.9 %all_to_all.30.got_ref = bf16[16,64,128]{2,1,0:T(8,128)(2,1)S(1)} all-to-all(bf16[16,64,128]{2,1,0:T(8,128)(2,1)S(1)} %get-tuple-element.33), channel_id=1, replica_groups=mesh['groups'=2,'wide'=16,'narrow'=1] {'wide','narrow'}, dimensions={0} | all-to-all | bytes 524288 | tf_op jit(solution)/shard_map/all_to_all | solution.py:29
  39.5 1.1 %norm.1 = (bf16[16,64,128]{2,1,0:T(8,128)(2,1)}, bf16[128,1024]{1,0:T(8,128)(2,1)S(1)}) custom-call(bf16[16,64,128]{2,1,0:T(8,128)(2,1)S(1)} %all_to_all.30.got_ref, bf16[128,1024]{1,0:T(8,128)(2,1)S(1)} %get-tuple-element.34.t_ref, f32[1,128]{1,0:T(1,128)S(1)} %bitcast.8), custom_call_target="tpu_custom_call" | custom-call | bytes 1049088 | tf_op jit(solution)/shard_map/norm/pallas_call | solution.py:264
  40.7 3.5 %all-to-all-start.2 = ((bf16[16,64,128]{2,1,0:T(8,128)(2,1)}), bf16[16,64,128]{2,1,0:T(8,128)(2,1)S(1)}, u32[]{:S(2)}, u32[]{:S(2)}) async-start(bf16[16,64,128]{2,1,0:T(8,128)(2,1)} %get-tuple-element.38), calls=%async_computation.2 | async-start | bytes 524288 | tf_op jit(solution)/shard_map/all_to_all | solution.py:29
  44.2 1.0 %copy-done.11 = f32[8,128,128]{2,1,0:T(8,128)S(1)} copy-done((f32[8,128,128]{2,1,0:T(8,128)S(1)}, f32[8,128,128]{2,1,0:T(8,128)}, u32[]{:S(2)}) %copy-start.11) | copy-done | bytes 524312
  45.2 1.0 %output.1 = (bf16[8,128,128]{2,1,0:T(8,128)(2,1)}, bf16[8,128,128]{2,1,0:T(8,128)(2,1)S(1)}, f32[128,128]{1,0:T(8,128)S(1)}) custom-call(bf16[128,1024]{1,0:T(8,128)(2,1)S(1)} %get-tuple-element.35.xn_ref, f32[8,128,128]{2,1,0:T(8,128)S(1)} %copy-done.11, bf16[8,128,128]{2,1,0:T(8,128)(2,1)S(1)} %copy-done.5, bf16[128,1024]{1,0:T(8,128)(2,1)S(1)} %copy-done.1, ...), custom_call_target="tpu_custom_call" | custom-call | flops 2000000000 | bytes 1933312 | tf_op jit(solution)/shard_map/output/pallas_call | solution.py:264
  46.3 7.9 %all-to-all-done.2.got_ref = bf16[16,64,128]{2,1,0:T(8,128)(2,1)S(1)} async-done(((bf16[16,64,128]{2,1,0:T(8,128)(2,1)}), bf16[16,64,128]{2,1,0:T(8,128)(2,1)S(1)}, u32[]{:S(2)}, u32[]{:S(2)}) %all-to-all-start.2) | async-done | bytes 262176 | tf_op jit(solution)/shard_map/all_to_all | solution.py:29
  54.2 0.4 unmix.1
  54.6 17.2 %all_to_all.31.got_ref = bf16[16,128,128]{2,1,0:T(8,128)(2,1)S(1)} all-to-all(bf16[16,128,128]{2,1,0:T(8,128)(2,1)S(1)} %unmix.1), channel_id=1, replica_groups=mesh['groups'=2,'wide'=16,'narrow'=1] {'wide','narrow'}, dimensions={0} | all-to-all | bytes 1048576 | tf_op jit(solution)/shard_map/all_to_all | solution.py:29
  71.9 0.7 copy-done.3
  72.5 1.4 %cells.1 = (bf16[128,1024]{1,0:T(8,128)(2,1)S(1)}, bf16[128,640]{1,0:T(8,128)(2,1)}) custom-call(bf16[16,128,128]{2,1,0:T(8,128)(2,1)S(1)} %all_to_all.31.got_ref, bf16[512,1024]{1,0:T(8,128)(2,1)S(1)} %get-tuple-element.43.factor_ref, bf16[128,1024]{1,0:T(8,128)(2,1)S(1)} %copy-done.1, f32[128,128]{1,0:T(8,128)S(1)} %get-tuple-element.44.gate_part_ref, ...), custom_call_target="tpu_custom_call" | custom-call | bytes 2458112 | tf_op jit(solution)/shard_map/cells/pallas_call | solution.py:264
  73.9 4.2 %all-to-all-start.4 = ((bf16[16,8,640]{2,1,0:T(8,128)(2,1)}), bf16[16,8,640]{2,1,0:T(8,128)(2,1)S(1)}, u32[]{:S(2)}, u32[]{:S(2)}) async-start(bf16[16,8,640]{2,1,0:T(8,128)(2,1)} %bitcast.3), calls=%async_computation.4 | async-start | bytes 327680 | tf_op jit(solution)/shard_map/all_to_all | solution.py:29
  78.2 1.3 %pair.1 = bf16[8,128,128]{2,1,0:T(8,128)(2,1)} custom-call(bf16[128,1024]{1,0:T(8,128)(2,1)S(1)} %get-tuple-element.46.u_ref, bf16[8,128,128]{2,1,0:T(8,128)(2,1)S(1)} %get-tuple-element.47.d_logit_ref, bf16[8,128,128]{2,1,0:T(8,128)(2,1)S(1)} %copy-done.2, f32[1,128]{1,0:T(1,128)S(1)} %bitcast.6, bf16[128,128]{1,0:T(8,128)(2,1)S(1)} %copy-done.7), custom_call_target="tpu_custom_call" | custom-call | flops 2000000000 | bytes 1081856 | tf_op jit(solution)/shard_map/pair/pallas_call | solution.py:264
  79.5 7.1 %all-to-all-done.4.got_ref = bf16[16,8,640]{2,1,0:T(8,128)(2,1)S(1)} async-done(((bf16[16,8,640]{2,1,0:T(8,128)(2,1)}), bf16[16,8,640]{2,1,0:T(8,128)(2,1)S(1)}, u32[]{:S(2)}, u32[]{:S(2)}) %all-to-all-start.4) | async-done | bytes 163872 | tf_op jit(solution)/shard_map/all_to_all | solution.py:29
  86.7 11.1 %all_to_all.32.got_ref = bf16[16,8,640]{2,1,0:T(8,128)(2,1)S(1)} all-to-all(bf16[16,8,640]{2,1,0:T(8,128)(2,1)S(1)} %sum.1), channel_id=1, replica_groups=mesh['groups'=2,'wide'=16,'narrow'=1] {'wide','narrow'}, dimensions={0} | all-to-all | bytes 327680 | tf_op jit(solution)/shard_map/all_to_all | solution.py:29
  97.7 0.7 finish.1
  (23 shorter events, 0.2 us)
Async XLA Ops:
  3.2 8.4 %copy-start = (bf16[128,512]{1,0:T(8,128)(2,1)S(1)}, bf16[128,512]{1,0:T(8,128)(2,1)}, u32[]{:S(2)}) copy-start(bf16[128,512]{1,0:T(8,128)(2,1)} %w_ref.3) | copy-start | bytes 393220
  3.2 8.4 %copy-start.1 = (bf16[128,1024]{1,0:T(8,128)(2,1)S(1)}, bf16[128,1024]{1,0:T(8,128)(2,1)}, u32[]{:S(2)}) copy-start(bf16[128,1024]{1,0:T(8,128)(2,1)} %get-tuple-element.29.zn_ref) | copy-start | bytes 786436
  3.2 8.4 %copy-start.5 = (bf16[8,128,128]{2,1,0:T(8,128)(2,1)S(1)}, bf16[8,128,128]{2,1,0:T(8,128)(2,1)}, u32[]{:S(2)}) copy-start(bf16[8,128,128]{2,1,0:T(8,128)(2,1)} %adj_ref.3) | copy-start | bytes 786436
  3.2 8.4 %copy-start.6 = (bf16[128,128]{1,0:T(8,128)(2,1)S(1)}, bf16[128,128]{1,0:T(8,128)(2,1)}, u32[]{:S(2)}) copy-start(bf16[128,128]{1,0:T(8,128)(2,1)} %w_out_ref.3) | copy-start | bytes 98308
  3.2 8.4 %copy-start.7 = (bf16[128,128]{1,0:T(8,128)(2,1)S(1)}, bf16[128,128]{1,0:T(8,128)(2,1)}, u32[]{:S(2)}) copy-start(bf16[128,128]{1,0:T(8,128)(2,1)} %w_gate_ref.3) | copy-start | bytes 98308
  3.2 22.0 %all-to-all-start = ((bf16[16,128,128]{2,1,0:T(8,128)(2,1)}), bf16[16,128,128]{2,1,0:T(8,128)(2,1)S(1)}, u32[]{:S(2)}, u32[]{:S(2)}) async-start(bf16[16,128,128]{2,1,0:T(8,128)(2,1)} %get-tuple-element.28), calls=%async_computation | async-start | bytes 1048576 | tf_op jit(solution)/shard_map/all_to_all | solution.py:29
  10.7 0.7 copy-start.12
  11.6 0.7 copy-start.8
  11.6 0.7 copy-start.4
  11.6 0.7 copy-start.9
  13.8 0.8 copy-start.10
  40.7 13.5 %all-to-all-start.2 = ((bf16[16,64,128]{2,1,0:T(8,128)(2,1)}), bf16[16,64,128]{2,1,0:T(8,128)(2,1)S(1)}, u32[]{:S(2)}, u32[]{:S(2)}) async-start(bf16[16,64,128]{2,1,0:T(8,128)(2,1)} %get-tuple-element.38), calls=%async_computation.2 | async-start | bytes 524288 | tf_op jit(solution)/shard_map/all_to_all | solution.py:29
  44.2 1.0 %copy-start.11 = (f32[8,128,128]{2,1,0:T(8,128)S(1)}, f32[8,128,128]{2,1,0:T(8,128)}, u32[]{:S(2)}) copy-start(f32[8,128,128]{2,1,0:T(8,128)} %copy-done.10) | copy-start | bytes 1572868
  71.9 0.7 copy-start.3
  73.9 4.2 %copy-start.2 = (bf16[8,128,128]{2,1,0:T(8,128)(2,1)S(1)}, bf16[8,128,128]{2,1,0:T(8,128)(2,1)}, u32[]{:S(2)}) copy-start(bf16[8,128,128]{2,1,0:T(8,128)(2,1)} %pair_ref.1) | copy-start | bytes 786436
  73.9 12.7 %all-to-all-start.4 = ((bf16[16,8,640]{2,1,0:T(8,128)(2,1)}), bf16[16,8,640]{2,1,0:T(8,128)(2,1)S(1)}, u32[]{:S(2)}, u32[]{:S(2)}) async-start(bf16[16,8,640]{2,1,0:T(8,128)(2,1)} %bitcast.3), calls=%async_computation.4 | async-start | bytes 327680 | tf_op jit(solution)/shard_map/all_to_all | solution.py:29

commit v8 on v7

--- a/solution.py
+++ b/solution.py
@@ -121,7 +121,7 @@
 
 def gate_kernel(
     zn_ref, adj_ref, mask_ref, same_ref, w_ref, w_gate_ref, bias_ref, gain_ref, w_out_ref,
-    factor_ref, gate_ref, t_ref,
+    gain_in_ref, factor_ref, gate_ref, t_ref, columns_ref,
 ):
     rows, cols, width = adj_ref.shape
     weights = w_ref[...].astype(F32).T.astype(BF)
@@ -129,6 +129,7 @@
     w_gate = w_gate_ref[...].astype(F32).T.astype(BF)
     across, within = column(bias_ref[0:1, :]), column(bias_ref[1:2, :])
     gain = column(gain_ref[...])
+    columns_ref[...] = column(gain_in_ref[...])
     for row in range(rows):
         lanes = slice(row * cols, (row + 1) * cols)
         zn = zn_ref[:, lanes]
@@ -211,7 +212,7 @@
 
 
 def cells_kernel(
-    got_ref, factor_ref, zn_ref, gate_part_ref, w_ref, gain_ref, u_ref, part_ref, cells_ref
+    got_ref, factor_ref, zn_ref, gate_part_ref, w_ref, columns_ref, u_ref, part_ref, cells_ref
 ):
     devices, depth, cols = got_ref.shape
     half = depth // 2
@@ -228,7 +229,7 @@
     total = dot(zn_ref[...], cells_ref[...], ((1,), (1,)))
     part_ref[:, : 4 * hidden] = total.astype(BF)
     part_ref[:, 4 * hidden :] = gate_part_ref[...].astype(BF)
-    u = dot(w_ref[...], cells_ref[...]) * column(gain_ref[...])[:, :1]
+    u = dot(w_ref[...], cells_ref[...]) * columns_ref[:, :1]
     u_ref[...] = (u - jnp.mean(u, 0, keepdims=True)).astype(BF)
 
 
@@ -305,12 +306,12 @@
         mib=56,
     )(pair, mask[None], gain_in, w_proj)
     got = swap(sent)
-    factor, gate, t = call(
+    factor, gate, t, columns = call(
         gate_kernel,
-        [shape((4 * hidden, cells), BF), shape((rows, cols, width), F32), shape((hidden, cells), BF)],
+        [shape((4 * hidden, cells), BF), shape((rows, cols, width), F32), shape((hidden, cells), BF), shape((width, width), F32)],
         flops=2 * 10**9,
         name="gate",
-    )(zn, adjoint, cell_mask, same, w_proj, w_gate, chain_bias, gain_out, w_out)
+    )(zn, adjoint, cell_mask, same, w_proj, w_gate, chain_bias, gain_out, w_out, gain_in)
     field = pltpu.VMEM((devices * half, cols), F32)
     channels = shape((own, residues, cols), BF)
     block = shape((devices, half, cols), BF)
@@ -335,7 +336,7 @@
         [shape((width, cells), BF), shape((width, 4 * hidden + width), BF)],
         [pltpu.VMEM((4 * hidden, cells), BF)],
         name="cells",
-    )(got, factor, zn, gate_part, w_proj, gain_in)
+    )(got, factor, zn, gate_part, w_proj, columns)
     got = swap(part.reshape(devices, width // devices, -1))
     d_pair = call(pair_kernel, [shape(pair.shape, BF)], flops=2 * 10**9, name="pair")(
         u, d_logit, pair, gain_in, w_gate

time: 99.1 us -> 98.4 us (level)
  no operation moved by 1% of the time
where the time goes in v8:
time: 98.4 us; the launch traced here: 97.8 us
  blocking collectives  42.2 us (43%)
  waiting for transfers between devices  25.6 us (26%)
  starting transfers between devices  15.3 us (16%)
  Pallas kernels  10.6 us (11%)
  local copies, waits for them, and re-layouts  3.23 us (3%)
    all_to_all x3, blocking collectives, swap(): lax.all_to_all(blocks, ('wide', 'narrow'), split_axis=0, concat_axis=0, t...  42.2 us
    all_to_all x3, waiting for transfers between devices, swap(): lax.all_to_all(blocks, ('wide', 'narrow'), split_axis=0, concat_axis=0, t...  25.6 us
    all_to_all x3, starting transfers between devices, swap(): lax.all_to_all(blocks, ('wide', 'narrow'), split_axis=0, concat_axis=0, t...  15.3 us
    pallas_call x10, Pallas kernels, run(): pl.pallas_call(kernel, out_shape=list(outs), in_specs=[pl.BlockSpec(memor...  10.6 us
    unnamed x26, local copies, waits for them, and re-layouts  3.16 us
  transfers between devices with their start and end apart: 3, of which 3 were waited for; matrix products, arithmetic and copies ran while one was open for 0% of the time, Pallas kernels for 4%

profile of v8, /device:TPU:0, one launch (start us, length us, event | category | flops | bytes accessed | tf_op | source)
XLA Modules:
  0.0 97.8 jit_solution(7868583112347225384)
XLA Ops:
  0.6 2.5 %project.1 = (bf16[16,128,128]{2,1,0:T(8,128)(2,1)}, bf16[128,1024]{1,0:T(8,128)(2,1)}, f32[8,128]{1,0:T(8,128)}) custom-call(bf16[8,128,128]{2,1,0:T(8,128)(2,1)} %pair_ref.1, s32[1,128]{1,0:T(1,128)} %bitcast.9, f32[1,128]{1,0:T(1,128)} %bitcast.6, bf16[128,512]{1,0:T(8,128)(2,1)} %w_ref.3), custom_call_target="tpu_custom_call" | custom-call | bytes 1184768 | tf_op jit(solution)/shard_map/project/pallas_call | solution.py:265
  3.2 7.5 %all-to-all-start = ((bf16[16,128,128]{2,1,0:T(8,128)(2,1)}), bf16[16,128,128]{2,1,0:T(8,128)(2,1)S(1)}, u32[]{:S(2)}, u32[]{:S(2)}) async-start(bf16[16,128,128]{2,1,0:T(8,128)(2,1)} %get-tuple-element.29), calls=%async_computation | async-start | bytes 1048576 | tf_op jit(solution)/shard_map/all_to_all | solution.py:29
  10.8 0.7 copy-done.12
  11.4 0.1 dynamic_slice.3
  11.5 0.1 compare_convert_fusion.same_ref
  11.6 0.6 copy-done.8
  12.3 1.6 %gate.1 = (bf16[512,1024]{1,0:T(8,128)(2,1)S(1)}, f32[8,128,128]{2,1,0:T(8,128)S(1)}, bf16[128,1024]{1,0:T(8,128)(2,1)S(1)}, f32[128,128]{1,0:T(8,128)S(1)}) custom-call(bf16[128,1024]{1,0:T(8,128)(2,1)S(1)} %copy-done.2, bf16[8,128,128]{2,1,0:T(8,128)(2,1)S(1)} %copy-done.5, f32[8,128]{1,0:T(8,128)S(1)} %copy-done.8, ...), custom_call_target="tpu_custom_call" | custom-call | flops 2000000000 | bytes 2631680 | tf_op jit(solution)/shard_map/gate/pallas_call | solution.py:265
  13.9 0.8 copy-done.10
  14.6 10.6 %all-to-all-done.got_ref = bf16[16,128,128]{2,1,0:T(8,128)(2,1)S(1)} async-done(((bf16[16,128,128]{2,1,0:T(8,128)(2,1)}), bf16[16,128,128]{2,1,0:T(8,128)(2,1)S(1)}, u32[]{:S(2)}, u32[]{:S(2)}) %all-to-all-start) | async-done | bytes 524320 | tf_op jit(solution)/shard_map/all_to_all | solution.py:29
  25.2 0.4 mix.1
  25.6 13.9 %all_to_all.30.got_ref = bf16[16,64,128]{2,1,0:T(8,128)(2,1)S(1)} all-to-all(bf16[16,64,128]{2,1,0:T(8,128)(2,1)S(1)} %get-tuple-element.34), channel_id=1, replica_groups=mesh['groups'=2,'wide'=16,'narrow'=1] {'wide','narrow'}, dimensions={0} | all-to-all | bytes 524288 | tf_op jit(solution)/shard_map/all_to_all | solution.py:29
  39.5 1.1 %norm.1 = (bf16[16,64,128]{2,1,0:T(8,128)(2,1)}, bf16[128,1024]{1,0:T(8,128)(2,1)S(1)}) custom-call(bf16[16,64,128]{2,1,0:T(8,128)(2,1)S(1)} %all_to_all.30.got_ref, bf16[128,1024]{1,0:T(8,128)(2,1)S(1)} %get-tuple-element.35.t_ref, f32[1,128]{1,0:T(1,128)S(1)} %bitcast.5), custom_call_target="tpu_custom_call" | custom-call | bytes 1049088 | tf_op jit(solution)/shard_map/norm/pallas_call | solution.py:265
  40.7 3.5 %all-to-all-start.2 = ((bf16[16,64,128]{2,1,0:T(8,128)(2,1)}), bf16[16,64,128]{2,1,0:T(8,128)(2,1)S(1)}, u32[]{:S(2)}, u32[]{:S(2)}) async-start(bf16[16,64,128]{2,1,0:T(8,128)(2,1)} %get-tuple-element.39), calls=%async_computation.2 | async-start | bytes 524288 | tf_op jit(solution)/shard_map/all_to_all | solution.py:29
  44.2 1.0 %copy-done.11 = f32[8,128,128]{2,1,0:T(8,128)S(1)} copy-done((f32[8,128,128]{2,1,0:T(8,128)S(1)}, f32[8,128,128]{2,1,0:T(8,128)}, u32[]{:S(2)}) %copy-start.11) | copy-done | bytes 524312
  45.2 1.1 %output.1 = (bf16[8,128,128]{2,1,0:T(8,128)(2,1)}, bf16[8,128,128]{2,1,0:T(8,128)(2,1)S(1)}, f32[128,128]{1,0:T(8,128)S(1)}) custom-call(bf16[128,1024]{1,0:T(8,128)(2,1)S(1)} %get-tuple-element.36.xn_ref, f32[8,128,128]{2,1,0:T(8,128)S(1)} %copy-done.11, bf16[8,128,128]{2,1,0:T(8,128)(2,1)S(1)} %copy-done.5, bf16[128,1024]{1,0:T(8,128)(2,1)S(1)} %copy-done.2, ...), custom_call_target="tpu_custom_call" | custom-call | flops 2000000000 | bytes 1933312 | tf_op jit(solution)/shard_map/output/pallas_call | solution.py:265
  46.3 7.9 %all-to-all-done.2.got_ref = bf16[16,64,128]{2,1,0:T(8,128)(2,1)S(1)} async-done(((bf16[16,64,128]{2,1,0:T(8,128)(2,1)}), bf16[16,64,128]{2,1,0:T(8,128)(2,1)S(1)}, u32[]{:S(2)}, u32[]{:S(2)}) %all-to-all-start.2) | async-done | bytes 262176 | tf_op jit(solution)/shard_map/all_to_all | solution.py:29
  54.2 0.4 unmix.1
  54.6 17.2 %all_to_all.31.got_ref = bf16[16,128,128]{2,1,0:T(8,128)(2,1)S(1)} all-to-all(bf16[16,128,128]{2,1,0:T(8,128)(2,1)S(1)} %unmix.1), channel_id=1, replica_groups=mesh['groups'=2,'wide'=16,'narrow'=1] {'wide','narrow'}, dimensions={0} | all-to-all | bytes 1048576 | tf_op jit(solution)/shard_map/all_to_all | solution.py:29
  71.9 1.4 %cells.1 = (bf16[128,1024]{1,0:T(8,128)(2,1)S(1)}, bf16[128,640]{1,0:T(8,128)(2,1)}) custom-call(bf16[16,128,128]{2,1,0:T(8,128)(2,1)S(1)} %all_to_all.31.got_ref, bf16[512,1024]{1,0:T(8,128)(2,1)S(1)} %get-tuple-element.44.factor_ref, bf16[128,1024]{1,0:T(8,128)(2,1)S(1)} %copy-done.2, f32[128,128]{1,0:T(8,128)S(1)} %get-tuple-element.45.gate_part_ref, ...), custom_call_target="tpu_custom_call" | custom-call | bytes 2523136 | tf_op jit(solution)/shard_map/cells/pallas_call | solution.py:265
  73.3 4.2 %all-to-all-start.4 = ((bf16[16,8,640]{2,1,0:T(8,128)(2,1)}), bf16[16,8,640]{2,1,0:T(8,128)(2,1)S(1)}, u32[]{:S(2)}, u32[]{:S(2)}) async-start(bf16[16,8,640]{2,1,0:T(8,128)(2,1)} %bitcast.3), calls=%async_computation.4 | async-start | bytes 327680 | tf_op jit(solution)/shard_map/all_to_all | solution.py:29
  77.5 1.3 %pair.1 = bf16[8,128,128]{2,1,0:T(8,128)(2,1)} custom-call(bf16[128,1024]{1,0:T(8,128)(2,1)S(1)} %get-tuple-element.48.u_ref, bf16[8,128,128]{2,1,0:T(8,128)(2,1)S(1)} %get-tuple-element.49.d_logit_ref, bf16[8,128,128]{2,1,0:T(8,128)(2,1)S(1)} %copy-done.1, f32[1,128]{1,0:T(1,128)S(1)} %bitcast.8, bf16[128,128]{1,0:T(8,128)(2,1)S(1)} %copy-done.7), custom_call_target="tpu_custom_call" | custom-call | flops 2000000000 | bytes 1081856 | tf_op jit(solution)/shard_map/pair/pallas_call | solution.py:265
  78.8 7.1 %all-to-all-done.4.got_ref = bf16[16,8,640]{2,1,0:T(8,128)(2,1)S(1)} async-done(((bf16[16,8,640]{2,1,0:T(8,128)(2,1)}), bf16[16,8,640]{2,1,0:T(8,128)(2,1)S(1)}, u32[]{:S(2)}, u32[]{:S(2)}) %all-to-all-start.4) | async-done | bytes 163872 | tf_op jit(solution)/shard_map/all_to_all | solution.py:29
  86.0 11.1 %all_to_all.32.got_ref = bf16[16,8,640]{2,1,0:T(8,128)(2,1)S(1)} all-to-all(bf16[16,8,640]{2,1,0:T(8,128)(2,1)S(1)} %sum.1), channel_id=1, replica_groups=mesh['groups'=2,'wide'=16,'narrow'=1] {'wide','narrow'}, dimensions={0} | all-to-all | bytes 327680 | tf_op jit(solution)/shard_map/all_to_all | solution.py:29
  97.1 0.7 finish.1
  (23 shorter events, 0.1 us)
Async XLA Ops:
  3.2 8.4 %copy-start = (bf16[128,512]{1,0:T(8,128)(2,1)S(1)}, bf16[128,512]{1,0:T(8,128)(2,1)}, u32[]{:S(2)}) copy-start(bf16[128,512]{1,0:T(8,128)(2,1)} %w_ref.3) | copy-start | bytes 393220
  3.2 8.4 %copy-start.2 = (bf16[128,1024]{1,0:T(8,128)(2,1)S(1)}, bf16[128,1024]{1,0:T(8,128)(2,1)}, u32[]{:S(2)}) copy-start(bf16[128,1024]{1,0:T(8,128)(2,1)} %get-tuple-element.30.zn_ref) | copy-start | bytes 786436
  3.2 8.4 %copy-start.5 = (bf16[8,128,128]{2,1,0:T(8,128)(2,1)S(1)}, bf16[8,128,128]{2,1,0:T(8,128)(2,1)}, u32[]{:S(2)}) copy-start(bf16[8,128,128]{2,1,0:T(8,128)(2,1)} %adj_ref.3) | copy-start | bytes 786436
  3.2 8.4 %copy-start.6 = (bf16[128,128]{1,0:T(8,128)(2,1)S(1)}, bf16[128,128]{1,0:T(8,128)(2,1)}, u32[]{:S(2)}) copy-start(bf16[128,128]{1,0:T(8,128)(2,1)} %w_out_ref.3) | copy-start | bytes 98308
  3.2 8.4 %copy-start.7 = (bf16[128,128]{1,0:T(8,128)(2,1)S(1)}, bf16[128,128]{1,0:T(8,128)(2,1)}, u32[]{:S(2)}) copy-start(bf16[128,128]{1,0:T(8,128)(2,1)} %w_gate_ref.3) | copy-start | bytes 98308
  3.2 22.0 %all-to-all-start = ((bf16[16,128,128]{2,1,0:T(8,128)(2,1)}), bf16[16,128,128]{2,1,0:T(8,128)(2,1)S(1)}, u32[]{:S(2)}, u32[]{:S(2)}) async-start(bf16[16,128,128]{2,1,0:T(8,128)(2,1)} %get-tuple-element.29), calls=%async_computation | async-start | bytes 1048576 | tf_op jit(solution)/shard_map/all_to_all | solution.py:29
  10.7 0.9 copy-start.9
  10.8 0.7 copy-start.12
  11.6 0.7 copy-start.8
  11.6 0.7 copy-start.3
  11.6 0.7 copy-start.4
  13.8 0.8 copy-start.10
  40.7 13.5 %all-to-all-start.2 = ((bf16[16,64,128]{2,1,0:T(8,128)(2,1)}), bf16[16,64,128]{2,1,0:T(8,128)(2,1)S(1)}, u32[]{:S(2)}, u32[]{:S(2)}) async-start(bf16[16,64,128]{2,1,0:T(8,128)(2,1)} %get-tuple-element.39), calls=%async_computation.2 | async-start | bytes 524288 | tf_op jit(solution)/shard_map/all_to_all | solution.py:29
  44.2 1.0 %copy-start.11 = (f32[8,128,128]{2,1,0:T(8,128)S(1)}, f32[8,128,128]{2,1,0:T(8,128)}, u32[]{:S(2)}) copy-start(f32[8,128,128]{2,1,0:T(8,128)} %copy-done.10) | copy-start | bytes 1572868
  73.3 4.2 %copy-start.1 = (bf16[8,128,128]{2,1,0:T(8,128)(2,1)S(1)}, bf16[8,128,128]{2,1,0:T(8,128)(2,1)}, u32[]{:S(2)}) copy-start(bf16[8,128,128]{2,1,0:T(8,128)(2,1)} %pair_ref.1) | copy-start | bytes 786436
  73.3 12.7 %all-to-all-start.4 = ((bf16[16,8,640]{2,1,0:T(8,128)(2,1)}), bf16[16,8,640]{2,1,0:T(8,128)(2,1)S(1)}, u32[]{:S(2)}, u32[]{:S(2)}) async-start(bf16[16,8,640]{2,1,0:T(8,128)(2,1)} %bitcast.3), calls=%async_computation.4 | async-start | bytes 327680 | tf_op jit(solution)/shard_map/all_to_all | solution.py:29

commit v9 on v8

--- a/solution.py
+++ b/solution.py
@@ -166,9 +166,10 @@
     sent_ref[...] = out_s[...].reshape(devices, half, cols).astype(BF)
 
 
-def norm_kernel(got_ref, t_ref, gain_ref, sent_ref, xn_ref):
+def norm_kernel(got_ref, t_ref, gain_ref, sent_out, xn_ref, sent_ref, sems):
     devices, depth, cols = got_ref.shape
     gain = column(gain_ref[...])
+    copies = []
     for two in range(depth // 16):
         pieces = []
         for part, mixed in enumerate(apart(got_ref[:, two * 16 : two * 16 + 16, :], devices)):
@@ -178,6 +179,13 @@
             xn_ref[:, lanes] = (hat * gain).astype(BF)
             pieces.append(back_t(t_ref[:, lanes].astype(F32), hat, rstd))
         sent_ref[:, two * 16 : two * 16 + 16, :] = two_rows(*pieces, devices)
+        place = (slice(None), pl.ds(two * 16, 16))
+        copies.append(
+            pltpu.make_async_copy(sent_ref.at[place], sent_out.at[place], sems.at[two])
+        )
+        copies[-1].start()
+    for copy in copies:
+        copy.wait()
 
 
 def output_kernel(
@@ -212,7 +220,8 @@
 
 
 def cells_kernel(
-    got_ref, factor_ref, zn_ref, gate_part_ref, w_ref, columns_ref, u_ref, part_ref, cells_ref
+    got_ref, factor_ref, zn_ref, gate_part_ref, w_ref, columns_ref, u_ref, part_out,
+    cells_ref, part_ref, sem,
 ):
     devices, depth, cols = got_ref.shape
     half = depth // 2
@@ -229,8 +238,11 @@
     total = dot(zn_ref[...], cells_ref[...], ((1,), (1,)))
     part_ref[:, : 4 * hidden] = total.astype(BF)
     part_ref[:, 4 * hidden :] = gate_part_ref[...].astype(BF)
+    copy = pltpu.make_async_copy(part_ref, part_out, sem)
+    copy.start()
     u = dot(w_ref[...], cells_ref[...]) * columns_ref[:, :1]
     u_ref[...] = (u - jnp.mean(u, 0, keepdims=True)).astype(BF)
+    copy.wait()
 
 
 def pair_kernel(u_ref, d_logit_ref, pair_ref, gain_ref, w_gate_ref, d_pair_ref):
@@ -257,7 +269,7 @@
     gate_ref[...] = total[:, wide:]
 
 
-def call(kernel, outs, scratch=(), flops=0, name=None, space=pltpu.VMEM, mib=12):
+def call(kernel, outs, scratch=(), flops=0, name=None, space=pltpu.VMEM, mib=12, away=()):
     spec = pl.BlockSpec(memory_space=pltpu.VMEM)
 
     def run(*args):
@@ -266,7 +278,7 @@
             kernel,
             out_shape=list(outs),
             in_specs=[pl.BlockSpec(memory_space=space)] * len(args),
-            out_specs=[spec] * len(outs),
+            out_specs=[pl.BlockSpec(memory_space=pl.ANY) if i in away else spec for i in range(len(outs))],
             scratch_shapes=list(scratch),
             compiler_params=pltpu.CompilerParams(vmem_limit_bytes=mib * 1024 * 1024),
             cost_estimate=pl.CostEstimate(
@@ -318,7 +330,13 @@
     got, t = lax.optimization_barrier((got, t))
     sent, left, right = call(mix_kernel, [block, channels, channels], [field] * 3, name="mix")(got)
     got = swap(sent)
-    sent, xn = call(norm_kernel, [block, shape((hidden, cells), BF)], name="norm")(got, t, gain_out)
+    sent, xn = call(
+        norm_kernel,
+        [block, shape((hidden, cells), BF)],
+        [pltpu.VMEM(block.shape, BF), pltpu.SemaphoreType.DMA((half // 16,))],
+        name="norm",
+        away=(0,),
+    )(got, t, gain_out)
     got = swap(sent)
     output, d_logit, gate_part = call(
         output_kernel,
@@ -334,8 +352,13 @@
     u, part = call(
         cells_kernel,
         [shape((width, cells), BF), shape((width, 4 * hidden + width), BF)],
-        [pltpu.VMEM((4 * hidden, cells), BF)],
+        [
+            pltpu.VMEM((4 * hidden, cells), BF),
+            pltpu.VMEM((width, 4 * hidden + width), BF),
+            pltpu.SemaphoreType.DMA,
+        ],
         name="cells",
+        away=(1,),
     )(got, factor, zn, gate_part, w_proj, columns)
     got = swap(part.reshape(devices, width // devices, -1))
     d_pair = call(pair_kernel, [shape(pair.shape, BF)], flops=2 * 10**9, name="pair")(

time: 98.4 us -> 98.4 us (level)
  no operation moved by 1% of the time
where the time goes in v9:
time: 98.4 us; the launch traced here: 97.8 us
  blocking collectives  42.2 us (43%)
  waiting for transfers between devices  25.6 us (26%)
  starting transfers between devices  15.3 us (16%)
  Pallas kernels  10.5 us (11%)
  local copies, waits for them, and re-layouts  3.24 us (3%)
    all_to_all x3, blocking collectives, swap(): lax.all_to_all(blocks, ('wide', 'narrow'), split_axis=0, concat_axis=0, t...  42.2 us
    all_to_all x3, waiting for transfers between devices, swap(): lax.all_to_all(blocks, ('wide', 'narrow'), split_axis=0, concat_axis=0, t...  25.6 us
    all_to_all x3, starting transfers between devices, swap(): lax.all_to_all(blocks, ('wide', 'narrow'), split_axis=0, concat_axis=0, t...  15.3 us
    pallas_call x10, Pallas kernels, run(): pl.pallas_call(kernel, out_shape=list(outs), in_specs=[pl.BlockSpec(memor...  10.5 us
    unnamed x26, local copies, waits for them, and re-layouts  3.16 us
  transfers between devices with their start and end apart: 3, of which 3 were waited for; matrix products, arithmetic and copies ran while one was open for 0% of the time, Pallas kernels for 4%

profile of v9, /device:TPU:0, one launch (start us, length us, event | category | flops | bytes accessed | tf_op | source)
XLA Modules:
  0.0 97.8 jit_solution(4677577246873688540)
XLA Ops:
  0.6 2.5 %project.1 = (bf16[16,128,128]{2,1,0:T(8,128)(2,1)}, bf16[128,1024]{1,0:T(8,128)(2,1)}, f32[8,128]{1,0:T(8,128)}) custom-call(bf16[8,128,128]{2,1,0:T(8,128)(2,1)} %pair_ref.1, s32[1,128]{1,0:T(1,128)} %bitcast.9, f32[1,128]{1,0:T(1,128)} %bitcast.6, bf16[128,512]{1,0:T(8,128)(2,1)} %w_ref.3), custom_call_target="tpu_custom_call" | custom-call | bytes 1184768 | tf_op jit(solution)/shard_map/project/pallas_call | solution.py:277
  3.2 7.5 %all-to-all-start = ((bf16[16,128,128]{2,1,0:T(8,128)(2,1)}), bf16[16,128,128]{2,1,0:T(8,128)(2,1)S(1)}, u32[]{:S(2)}, u32[]{:S(2)}) async-start(bf16[16,128,128]{2,1,0:T(8,128)(2,1)} %get-tuple-element.29), calls=%async_computation | async-start | bytes 1048576 | tf_op jit(solution)/shard_map/all_to_all | solution.py:29
  10.8 0.7 copy-done.12
  11.4 0.1 dynamic_slice.3
  11.5 0.1 compare_convert_fusion.same_ref
  11.6 0.6 copy-done.8
  12.3 1.6 %gate.1 = (bf16[512,1024]{1,0:T(8,128)(2,1)S(1)}, f32[8,128,128]{2,1,0:T(8,128)S(1)}, bf16[128,1024]{1,0:T(8,128)(2,1)S(1)}, f32[128,128]{1,0:T(8,128)S(1)}) custom-call(bf16[128,1024]{1,0:T(8,128)(2,1)S(1)} %copy-done.2, bf16[8,128,128]{2,1,0:T(8,128)(2,1)S(1)} %copy-done.5, f32[8,128]{1,0:T(8,128)S(1)} %copy-done.8, ...), custom_call_target="tpu_custom_call" | custom-call | flops 2000000000 | bytes 2631680 | tf_op jit(solution)/shard_map/gate/pallas_call | solution.py:277
  13.9 0.8 copy-done.10
  14.6 10.6 %all-to-all-done.got_ref = bf16[16,128,128]{2,1,0:T(8,128)(2,1)S(1)} async-done(((bf16[16,128,128]{2,1,0:T(8,128)(2,1)}), bf16[16,128,128]{2,1,0:T(8,128)(2,1)S(1)}, u32[]{:S(2)}, u32[]{:S(2)}) %all-to-all-start) | async-done | bytes 524320 | tf_op jit(solution)/shard_map/all_to_all | solution.py:29
  25.2 0.4 mix.1
  25.6 13.9 %all_to_all.30.got_ref = bf16[16,64,128]{2,1,0:T(8,128)(2,1)S(1)} all-to-all(bf16[16,64,128]{2,1,0:T(8,128)(2,1)S(1)} %get-tuple-element.34), channel_id=1, replica_groups=mesh['groups'=2,'wide'=16,'narrow'=1] {'wide','narrow'}, dimensions={0} | all-to-all | bytes 524288 | tf_op jit(solution)/shard_map/all_to_all | solution.py:29
  39.5 1.1 %norm.1 = (bf16[16,64,128]{2,1,0:T(8,128)(2,1)}, bf16[128,1024]{1,0:T(8,128)(2,1)S(1)}) custom-call(bf16[16,64,128]{2,1,0:T(8,128)(2,1)S(1)} %all_to_all.30.got_ref, bf16[128,1024]{1,0:T(8,128)(2,1)S(1)} %get-tuple-element.35.t_ref, f32[1,128]{1,0:T(1,128)S(1)} %bitcast.5), custom_call_target="tpu_custom_call" | custom-call | bytes 1049088 | tf_op jit(solution)/shard_map/norm/pallas_call | solution.py:277
  40.6 3.5 %all-to-all-start.2 = ((bf16[16,64,128]{2,1,0:T(8,128)(2,1)}), bf16[16,64,128]{2,1,0:T(8,128)(2,1)S(1)}, u32[]{:S(2)}, u32[]{:S(2)}) async-start(bf16[16,64,128]{2,1,0:T(8,128)(2,1)} %get-tuple-element.39), calls=%async_computation.2 | async-start | bytes 524288 | tf_op jit(solution)/shard_map/all_to_all | solution.py:29
  44.2 1.0 %copy-done.11 = f32[8,128,128]{2,1,0:T(8,128)S(1)} copy-done((f32[8,128,128]{2,1,0:T(8,128)S(1)}, f32[8,128,128]{2,1,0:T(8,128)}, u32[]{:S(2)}) %copy-start.11) | copy-done | bytes 524312
  45.2 1.1 %output.1 = (bf16[8,128,128]{2,1,0:T(8,128)(2,1)}, bf16[8,128,128]{2,1,0:T(8,128)(2,1)S(1)}, f32[128,128]{1,0:T(8,128)S(1)}) custom-call(bf16[128,1024]{1,0:T(8,128)(2,1)S(1)} %get-tuple-element.36.xn_ref, f32[8,128,128]{2,1,0:T(8,128)S(1)} %copy-done.11, bf16[8,128,128]{2,1,0:T(8,128)(2,1)S(1)} %copy-done.5, bf16[128,1024]{1,0:T(8,128)(2,1)S(1)} %copy-done.2, ...), custom_call_target="tpu_custom_call" | custom-call | flops 2000000000 | bytes 1933312 | tf_op jit(solution)/shard_map/output/pallas_call | solution.py:277
  46.3 7.9 %all-to-all-done.2.got_ref = bf16[16,64,128]{2,1,0:T(8,128)(2,1)S(1)} async-done(((bf16[16,64,128]{2,1,0:T(8,128)(2,1)}), bf16[16,64,128]{2,1,0:T(8,128)(2,1)S(1)}, u32[]{:S(2)}, u32[]{:S(2)}) %all-to-all-start.2) | async-done | bytes 262176 | tf_op jit(solution)/shard_map/all_to_all | solution.py:29
  54.2 0.4 unmix.1
  54.6 17.2 %all_to_all.31.got_ref = bf16[16,128,128]{2,1,0:T(8,128)(2,1)S(1)} all-to-all(bf16[16,128,128]{2,1,0:T(8,128)(2,1)S(1)} %unmix.1), channel_id=1, replica_groups=mesh['groups'=2,'wide'=16,'narrow'=1] {'wide','narrow'}, dimensions={0} | all-to-all | bytes 1048576 | tf_op jit(solution)/shard_map/all_to_all | solution.py:29
  71.9 1.4 %cells.1 = (bf16[128,1024]{1,0:T(8,128)(2,1)S(1)}, bf16[128,640]{1,0:T(8,128)(2,1)}) custom-call(bf16[16,128,128]{2,1,0:T(8,128)(2,1)S(1)} %all_to_all.31.got_ref, bf16[512,1024]{1,0:T(8,128)(2,1)S(1)} %get-tuple-element.44.factor_ref, bf16[128,1024]{1,0:T(8,128)(2,1)S(1)} %copy-done.2, f32[128,128]{1,0:T(8,128)S(1)} %get-tuple-element.45.gate_part_ref, ...), custom_call_target="tpu_custom_call" | custom-call | bytes 2523136 | tf_op jit(solution)/shard_map/cells/pallas_call | solution.py:277
  73.3 4.2 %all-to-all-start.4 = ((bf16[16,8,640]{2,1,0:T(8,128)(2,1)}), bf16[16,8,640]{2,1,0:T(8,128)(2,1)S(1)}, u32[]{:S(2)}, u32[]{:S(2)}) async-start(bf16[16,8,640]{2,1,0:T(8,128)(2,1)} %bitcast.3), calls=%async_computation.4 | async-start | bytes 327680 | tf_op jit(solution)/shard_map/all_to_all | solution.py:29
  77.5 1.3 %pair.1 = bf16[8,128,128]{2,1,0:T(8,128)(2,1)} custom-call(bf16[128,1024]{1,0:T(8,128)(2,1)S(1)} %get-tuple-element.48.u_ref, bf16[8,128,128]{2,1,0:T(8,128)(2,1)S(1)} %get-tuple-element.49.d_logit_ref, bf16[8,128,128]{2,1,0:T(8,128)(2,1)S(1)} %copy-done.1, f32[1,128]{1,0:T(1,128)S(1)} %bitcast.8, bf16[128,128]{1,0:T(8,128)(2,1)S(1)} %copy-done.7), custom_call_target="tpu_custom_call" | custom-call | flops 2000000000 | bytes 1081856 | tf_op jit(solution)/shard_map/pair/pallas_call | solution.py:277
  78.9 7.1 %all-to-all-done.4.got_ref = bf16[16,8,640]{2,1,0:T(8,128)(2,1)S(1)} async-done(((bf16[16,8,640]{2,1,0:T(8,128)(2,1)}), bf16[16,8,640]{2,1,0:T(8,128)(2,1)S(1)}, u32[]{:S(2)}, u32[]{:S(2)}) %all-to-all-start.4) | async-done | bytes 163872 | tf_op jit(solution)/shard_map/all_to_all | solution.py:29
  86.0 11.1 %all_to_all.32.got_ref = bf16[16,8,640]{2,1,0:T(8,128)(2,1)S(1)} all-to-all(bf16[16,8,640]{2,1,0:T(8,128)(2,1)S(1)} %sum.1), channel_id=1, replica_groups=mesh['groups'=2,'wide'=16,'narrow'=1] {'wide','narrow'}, dimensions={0} | all-to-all | bytes 327680 | tf_op jit(solution)/shard_map/all_to_all | solution.py:29
  97.1 0.7 finish.1
  (23 shorter events, 0.1 us)
Async XLA Ops:
  3.2 8.4 %copy-start = (bf16[128,512]{1,0:T(8,128)(2,1)S(1)}, bf16[128,512]{1,0:T(8,128)(2,1)}, u32[]{:S(2)}) copy-start(bf16[128,512]{1,0:T(8,128)(2,1)} %w_ref.3) | copy-start | bytes 393220
  3.2 8.4 %copy-start.2 = (bf16[128,1024]{1,0:T(8,128)(2,1)S(1)}, bf16[128,1024]{1,0:T(8,128)(2,1)}, u32[]{:S(2)}) copy-start(bf16[128,1024]{1,0:T(8,128)(2,1)} %get-tuple-element.30.zn_ref) | copy-start | bytes 786436
  3.2 8.4 %copy-start.5 = (bf16[8,128,128]{2,1,0:T(8,128)(2,1)S(1)}, bf16[8,128,128]{2,1,0:T(8,128)(2,1)}, u32[]{:S(2)}) copy-start(bf16[8,128,128]{2,1,0:T(8,128)(2,1)} %adj_ref.3) | copy-start | bytes 786436
  3.2 8.4 %copy-start.6 = (bf16[128,128]{1,0:T(8,128)(2,1)S(1)}, bf16[128,128]{1,0:T(8,128)(2,1)}, u32[]{:S(2)}) copy-start(bf16[128,128]{1,0:T(8,128)(2,1)} %w_out_ref.3) | copy-start | bytes 98308
  3.2 8.4 %copy-start.7 = (bf16[128,128]{1,0:T(8,128)(2,1)S(1)}, bf16[128,128]{1,0:T(8,128)(2,1)}, u32[]{:S(2)}) copy-start(bf16[128,128]{1,0:T(8,128)(2,1)} %w_gate_ref.3) | copy-start | bytes 98308
  3.2 22.0 %all-to-all-start = ((bf16[16,128,128]{2,1,0:T(8,128)(2,1)}), bf16[16,128,128]{2,1,0:T(8,128)(2,1)S(1)}, u32[]{:S(2)}, u32[]{:S(2)}) async-start(bf16[16,128,128]{2,1,0:T(8,128)(2,1)} %get-tuple-element.29), calls=%async_computation | async-start | bytes 1048576 | tf_op jit(solution)/shard_map/all_to_all | solution.py:29
  10.7 0.9 copy-start.9
  10.8 0.7 copy-start.12
  11.6 0.7 copy-start.8
  11.6 0.7 copy-start.3
  11.6 0.7 copy-start.4
  13.8 0.8 copy-start.10
  40.6 13.6 %all-to-all-start.2 = ((bf16[16,64,128]{2,1,0:T(8,128)(2,1)}), bf16[16,64,128]{2,1,0:T(8,128)(2,1)S(1)}, u32[]{:S(2)}, u32[]{:S(2)}) async-start(bf16[16,64,128]{2,1,0:T(8,128)(2,1)} %get-tuple-element.39), calls=%async_computation.2 | async-start | bytes 524288 | tf_op jit(solution)/shard_map/all_to_all | solution.py:29
  44.2 1.0 %copy-start.11 = (f32[8,128,128]{2,1,0:T(8,128)S(1)}, f32[8,128,128]{2,1,0:T(8,128)}, u32[]{:S(2)}) copy-start(f32[8,128,128]{2,1,0:T(8,128)} %copy-done.10) | copy-start | bytes 1572868
  73.3 4.3 %copy-start.1 = (bf16[8,128,128]{2,1,0:T(8,128)(2,1)S(1)}, bf16[8,128,128]{2,1,0:T(8,128)(2,1)}, u32[]{:S(2)}) copy-start(bf16[8,128,128]{2,1,0:T(8,128)(2,1)} %pair_ref.1) | copy-start | bytes 786436
  73.3 12.7 %all-to-all-start.4 = ((bf16[16,8,640]{2,1,0:T(8,128)(2,1)}), bf16[16,8,640]{2,1,0:T(8,128)(2,1)S(1)}, u32[]{:S(2)}, u32[]{:S(2)}) async-start(bf16[16,8,640]{2,1,0:T(8,128)(2,1)} %bitcast.3), calls=%async_computation.4 | async-start | bytes 327680 | tf_op jit(solution)/shard_map/all_to_all | solution.py:29

commit v10 on v8

--- a/solution.py
+++ b/solution.py
@@ -166,36 +166,38 @@
     sent_ref[...] = out_s[...].reshape(devices, half, cols).astype(BF)
 
 
-def norm_kernel(got_ref, t_ref, gain_ref, sent_ref, xn_ref):
+def norm_kernel(
+    got_ref, t_ref, gain_ref, gate_ref, adj_ref, zn_ref, w_out_ref,
+    sent_ref, xn_ref, d_logit_ref, part_ref,
+):
     devices, depth, cols = got_ref.shape
     gain = column(gain_ref[...])
+    total = None
     for two in range(depth // 16):
         pieces = []
         for part, mixed in enumerate(apart(got_ref[:, two * 16 : two * 16 + 16, :], devices)):
             row = 2 * two + part
             lanes = slice(row * cols, (row + 1) * cols)
             hat, rstd = centred(mixed)
-            xn_ref[:, lanes] = (hat * gain).astype(BF)
             pieces.append(back_t(t_ref[:, lanes].astype(F32), hat, rstd))
+            scaled = hat * gain
+            xn_ref[:, lanes] = scaled.astype(BF)
+            proj_out = dot(scaled.T.astype(BF), w_out_ref[...])
+            gate = gate_ref[row]
+            d_logit = (adj_ref[row].astype(F32) * proj_out * gate * (1.0 - gate)).astype(BF)
+            d_logit_ref[row] = d_logit
+            term = dot(zn_ref[:, lanes], d_logit)
+            total = term if total is None else total + term
         sent_ref[:, two * 16 : two * 16 + 16, :] = two_rows(*pieces, devices)
-
-
-def output_kernel(
-    xn_ref, gate_ref, adj_ref, zn_ref, w_out_ref, output_ref, d_logit_ref, part_ref
-):
-    rows, cols, width = adj_ref.shape
-    total = None
+    part_ref[...] = total
+
+
+def output_kernel(xn_ref, gate_ref, w_out_ref, output_ref):
+    rows, cols, width = gate_ref.shape
     for row in range(rows):
         lanes = slice(row * cols, (row + 1) * cols)
         xn = xn_ref[:, lanes].astype(F32).T.astype(BF)
-        proj_out = dot(xn, w_out_ref[...])
-        gate = gate_ref[row]
-        output_ref[row] = (gate * proj_out).astype(BF)
-        d_logit = (adj_ref[row].astype(F32) * proj_out * gate * (1.0 - gate)).astype(BF)
-        d_logit_ref[row] = d_logit
-        term = dot(zn_ref[:, lanes], d_logit)
-        total = term if total is None else total + term
-    part_ref[...] = total
+        output_ref[row] = (gate_ref[row] * dot(xn, w_out_ref[...])).astype(BF)
 
 
 def unmix_kernel(got_ref, left_ref, right_ref, sent_ref, in_s, left_s, right_s):
@@ -318,15 +320,12 @@
     got, t = lax.optimization_barrier((got, t))
     sent, left, right = call(mix_kernel, [block, channels, channels], [field] * 3, name="mix")(got)
     got = swap(sent)
-    sent, xn = call(norm_kernel, [block, shape((hidden, cells), BF)], name="norm")(got, t, gain_out)
+    sent, xn, d_logit, gate_part = call(
+        norm_kernel,
+        [block, shape((hidden, cells), BF), shape(pair.shape, BF), shape((width, width), F32)],
+        name="norm",
+    )(got, t, gain_out, gate, adjoint, zn, w_out)
     got = swap(sent)
-    output, d_logit, gate_part = call(
-        output_kernel,
-        [shape(pair.shape, BF), shape(pair.shape, BF), shape((width, width), F32)],
-        flops=2 * 10**9,
-        name="output",
-    )(xn, gate, adjoint, zn, w_out)
-    got, gate_part = lax.optimization_barrier((got, gate_part))
     sent = call(
         unmix_kernel, [shape((devices, 2 * half, cols), BF)], [field] * 3, name="unmix"
     )(got, left, right)[0]
@@ -341,7 +340,10 @@
     d_pair = call(pair_kernel, [shape(pair.shape, BF)], flops=2 * 10**9, name="pair")(
         u, d_logit, pair, gain_in, w_gate
     )[0]
-    got, d_pair = lax.optimization_barrier((got, d_pair))
+    output = call(output_kernel, [shape(pair.shape, BF)], flops=2 * 10**9, name="output")(
+        xn, gate, w_out
+    )[0]
+    got, d_pair, output = lax.optimization_barrier((got, d_pair, output))
     sent = call(
         functools.partial(sum_kernel, residues), [shape(got.shape, BF)], name="sum"
     )(got)[0]

time: 98.4 us -> 97.3 us (0.989)
  blocking collectives: 42.2 us -> 55.1 us
  waiting for transfers between devices: 25.6 us -> 17.5 us
  starting transfers between devices: 15.3 us -> 11.7 us
  local copies, waits for them, and re-layouts: 3.23 us -> 1.42 us
    all_to_all x3 -> x4, blocking collectives: 42.2 us -> 55.1 us  [swap(): lax.all_to_all(blocks, ('wide', 'narrow'), split_axis=0, concat_axis=0, t...]
    all_to_all x3 -> x2, waiting for transfers between devices: 25.6 us -> 17.5 us  [swap(): lax.all_to_all(blocks, ('wide', 'narrow'), split_axis=0, concat_axis=0, t...]
    all_to_all x3 -> x2, starting transfers between devices: 15.3 us -> 11.7 us  [swap(): lax.all_to_all(blocks, ('wide', 'narrow'), split_axis=0, concat_axis=0, t...]
    unnamed x26, local copies, waits for them, and re-layouts: 3.16 us -> 1.34 us
  transfers between devices with their start and end apart: 3 -> 2, of which waited for: 3 -> 2; matrix products, arithmetic and copies ran while one was open for 0% -> 0% of each run, Pallas kernels for 4% -> 4%
where the time goes in v10:
time: 97.3 us; the launch traced here: 96.7 us
  blocking collectives  55.1 us (57%)
  waiting for transfers between devices  17.5 us (18%)
  starting transfers between devices  11.7 us (12%)
  Pallas kernels  10.1 us (10%)
  local copies, waits for them, and re-layouts  1.42 us (1%)
    all_to_all x4, blocking collectives, swap(): lax.all_to_all(blocks, ('wide', 'narrow'), split_axis=0, concat_axis=0, t...  55.1 us
    all_to_all x2, waiting for transfers between devices, swap(): lax.all_to_all(blocks, ('wide', 'narrow'), split_axis=0, concat_axis=0, t...  17.5 us
    all_to_all x2, starting transfers between devices, swap(): lax.all_to_all(blocks, ('wide', 'narrow'), split_axis=0, concat_axis=0, t...  11.7 us
    pallas_call x10, Pallas kernels, run(): pl.pallas_call(kernel, out_shape=list(outs), in_specs=[pl.BlockSpec(memor...  10.1 us
  transfers between devices with their start and end apart: 2, of which 2 were waited for; matrix products, arithmetic and copies ran while one was open for 0% of the time, Pallas kernels for 4%

profile of v10, /device:TPU:0, one launch (start us, length us, event | category | flops | bytes accessed | tf_op | source)
XLA Modules:
  0.0 96.7 jit_solution(541698863683012929)
XLA Ops:
  0.6 2.5 %project.1 = (bf16[16,128,128]{2,1,0:T(8,128)(2,1)}, bf16[128,1024]{1,0:T(8,128)(2,1)}, f32[8,128]{1,0:T(8,128)}) custom-call(bf16[8,128,128]{2,1,0:T(8,128)(2,1)} %pair_ref.1, s32[1,128]{1,0:T(1,128)} %bitcast.9, f32[1,128]{1,0:T(1,128)} %bitcast.6, bf16[128,512]{1,0:T(8,128)(2,1)} %w_ref.3), custom_call_target="tpu_custom_call" | custom-call | bytes 1184768 | tf_op jit(solution)/shard_map/project/pallas_call | solution.py:267
  3.2 0.0 copy-start.1
  3.2 0.0 copy-start.3
  3.2 7.5 %all-to-all-start = ((bf16[16,128,128]{2,1,0:T(8,128)(2,1)}), bf16[16,128,128]{2,1,0:T(8,128)(2,1)S(1)}, u32[]{:S(2)}, u32[]{:S(2)}) async-start(bf16[16,128,128]{2,1,0:T(8,128)(2,1)} %get-tuple-element.27), calls=%async_computation | async-start | bytes 1048576 | tf_op jit(solution)/shard_map/all_to_all | solution.py:29
  10.8 0.0 copy-start.12
  10.8 0.7 copy-done.12
  11.4 0.1 dynamic_slice.3
  11.5 0.1 compare_convert_fusion.same_ref
  11.6 0.6 copy-done.10
  12.3 1.6 %gate.1 = (bf16[512,1024]{1,0:T(8,128)(2,1)S(1)}, f32[8,128,128]{2,1,0:T(8,128)S(1)}, bf16[128,1024]{1,0:T(8,128)(2,1)S(1)}, f32[128,128]{1,0:T(8,128)S(1)}) custom-call(bf16[128,1024]{1,0:T(8,128)(2,1)S(1)} %copy-done, bf16[8,128,128]{2,1,0:T(8,128)(2,1)S(1)} %copy-done.3, f32[8,128]{1,0:T(8,128)S(1)} %copy-done.10, ...), custom_call_target="tpu_custom_call" | custom-call | flops 2000000000 | bytes 2631680 | tf_op jit(solution)/shard_map/gate/pallas_call | solution.py:267
  13.8 11.4 %all-to-all-done.got_ref = bf16[16,128,128]{2,1,0:T(8,128)(2,1)S(1)} async-done(((bf16[16,128,128]{2,1,0:T(8,128)(2,1)}), bf16[16,128,128]{2,1,0:T(8,128)(2,1)S(1)}, u32[]{:S(2)}, u32[]{:S(2)}) %all-to-all-start) | async-done | bytes 524320 | tf_op jit(solution)/shard_map/all_to_all | solution.py:29
  25.2 0.4 mix.1
  25.6 13.9 %all_to_all.30.got_ref = bf16[16,64,128]{2,1,0:T(8,128)(2,1)S(1)} all-to-all(bf16[16,64,128]{2,1,0:T(8,128)(2,1)S(1)} %get-tuple-element.32), channel_id=1, replica_groups=mesh['groups'=2,'wide'=16,'narrow'=1] {'wide','narrow'}, dimensions={0} | all-to-all | bytes 524288 | tf_op jit(solution)/shard_map/all_to_all | solution.py:29
  39.5 0.8 norm.1
  40.3 12.8 %all_to_all.31.got_ref = bf16[16,64,128]{2,1,0:T(8,128)(2,1)S(1)} all-to-all(bf16[16,64,128]{2,1,0:T(8,128)(2,1)S(1)} %get-tuple-element.35), channel_id=1, replica_groups=mesh['groups'=2,'wide'=16,'narrow'=1] {'wide','narrow'}, dimensions={0} | all-to-all | bytes 524288 | tf_op jit(solution)/shard_map/all_to_all | solution.py:29
  53.1 0.4 unmix.1
  53.6 17.2 %all_to_all.32.got_ref = bf16[16,128,128]{2,1,0:T(8,128)(2,1)S(1)} all-to-all(bf16[16,128,128]{2,1,0:T(8,128)(2,1)S(1)} %unmix.1), channel_id=1, replica_groups=mesh['groups'=2,'wide'=16,'narrow'=1] {'wide','narrow'}, dimensions={0} | all-to-all | bytes 1048576 | tf_op jit(solution)/shard_map/all_to_all | solution.py:29
  70.8 1.4 %cells.1 = (bf16[128,1024]{1,0:T(8,128)(2,1)S(1)}, bf16[128,640]{1,0:T(8,128)(2,1)}) custom-call(bf16[16,128,128]{2,1,0:T(8,128)(2,1)S(1)} %all_to_all.32.got_ref, bf16[512,1024]{1,0:T(8,128)(2,1)S(1)} %get-tuple-element.38.factor_ref, bf16[128,1024]{1,0:T(8,128)(2,1)S(1)} %copy-done, f32[128,128]{1,0:T(8,128)S(1)} %get-tuple-element.39.gate_part_ref, ...), custom_call_target="tpu_custom_call" | custom-call | bytes 2523136 | tf_op jit(solution)/shard_map/cells/pallas_call | solution.py:267
  72.2 4.2 %all-to-all-start.4 = ((bf16[16,8,640]{2,1,0:T(8,128)(2,1)}), bf16[16,8,640]{2,1,0:T(8,128)(2,1)S(1)}, u32[]{:S(2)}, u32[]{:S(2)}) async-start(bf16[16,8,640]{2,1,0:T(8,128)(2,1)} %bitcast.3), calls=%async_computation.4 | async-start | bytes 327680 | tf_op jit(solution)/shard_map/all_to_all | solution.py:29
  76.5 1.0 %output.1 = bf16[8,128,128]{2,1,0:T(8,128)(2,1)} custom-call(bf16[128,1024]{1,0:T(8,128)(2,1)S(1)} %copy-done.8, f32[8,128,128]{2,1,0:T(8,128)S(1)} %get-tuple-element.34.gate_ref, bf16[128,128]{1,0:T(8,128)(2,1)S(1)} %copy-done.4), custom_call_target="tpu_custom_call" | custom-call | flops 2000000000 | bytes 1081344 | tf_op jit(solution)/shard_map/output/pallas_call | solution.py:267
  77.5 1.3 %pair.1 = bf16[8,128,128]{2,1,0:T(8,128)(2,1)} custom-call(bf16[128,1024]{1,0:T(8,128)(2,1)S(1)} %get-tuple-element.42.u_ref, bf16[8,128,128]{2,1,0:T(8,128)(2,1)S(1)} %get-tuple-element.43.d_logit_ref, bf16[8,128,128]{2,1,0:T(8,128)(2,1)S(1)} %copy-done.2, f32[1,128]{1,0:T(1,128)S(1)} %bitcast.8, bf16[128,128]{1,0:T(8,128)(2,1)S(1)} %copy-done.9), custom_call_target="tpu_custom_call" | custom-call | flops 2000000000 | bytes 1081856 | tf_op jit(solution)/shard_map/pair/pallas_call | solution.py:267
  78.8 6.1 %all-to-all-done.4.got_ref = bf16[16,8,640]{2,1,0:T(8,128)(2,1)S(1)} async-done(((bf16[16,8,640]{2,1,0:T(8,128)(2,1)}), bf16[16,8,640]{2,1,0:T(8,128)(2,1)S(1)}, u32[]{:S(2)}, u32[]{:S(2)}) %all-to-all-start.4) | async-done | bytes 163872 | tf_op jit(solution)/shard_map/all_to_all | solution.py:29
  84.9 11.1 %all_to_all.33.got_ref = bf16[16,8,640]{2,1,0:T(8,128)(2,1)S(1)} all-to-all(bf16[16,8,640]{2,1,0:T(8,128)(2,1)S(1)} %sum.1), channel_id=1, replica_groups=mesh['groups'=2,'wide'=16,'narrow'=1] {'wide','narrow'}, dimensions={0} | all-to-all | bytes 327680 | tf_op jit(solution)/shard_map/all_to_all | solution.py:29
  96.0 0.7 finish.1
  (22 shorter events, 0.1 us)
Async XLA Ops:
  3.2 8.4 %copy-start = (bf16[128,1024]{1,0:T(8,128)(2,1)S(1)}, bf16[128,1024]{1,0:T(8,128)(2,1)}, u32[]{:S(2)}) copy-start(bf16[128,1024]{1,0:T(8,128)(2,1)} %get-tuple-element.28.zn_ref) | copy-start | bytes 786436
  3.2 8.4 %copy-start.1 = (bf16[128,512]{1,0:T(8,128)(2,1)S(1)}, bf16[128,512]{1,0:T(8,128)(2,1)}, u32[]{:S(2)}) copy-start(bf16[128,512]{1,0:T(8,128)(2,1)} %w_ref.3) | copy-start | bytes 393220
  3.2 8.4 %copy-start.3 = (bf16[8,128,128]{2,1,0:T(8,128)(2,1)S(1)}, bf16[8,128,128]{2,1,0:T(8,128)(2,1)}, u32[]{:S(2)}) copy-start(bf16[8,128,128]{2,1,0:T(8,128)(2,1)} %adj_ref.3) | copy-start | bytes 786436
  3.2 8.4 %copy-start.4 = (bf16[128,128]{1,0:T(8,128)(2,1)S(1)}, bf16[128,128]{1,0:T(8,128)(2,1)}, u32[]{:S(2)}) copy-start(bf16[128,128]{1,0:T(8,128)(2,1)} %w_out_ref.5) | copy-start | bytes 98308
  3.2 8.4 %copy-start.9 = (bf16[128,128]{1,0:T(8,128)(2,1)S(1)}, bf16[128,128]{1,0:T(8,128)(2,1)}, u32[]{:S(2)}) copy-start(bf16[128,128]{1,0:T(8,128)(2,1)} %w_gate_ref.3) | copy-start | bytes 98308
  3.2 22.0 %all-to-all-start = ((bf16[16,128,128]{2,1,0:T(8,128)(2,1)}), bf16[16,128,128]{2,1,0:T(8,128)(2,1)S(1)}, u32[]{:S(2)}, u32[]{:S(2)}) async-start(bf16[16,128,128]{2,1,0:T(8,128)(2,1)} %get-tuple-element.27), calls=%async_computation | async-start | bytes 1048576 | tf_op jit(solution)/shard_map/all_to_all | solution.py:29
  10.7 0.9 copy-start.11
  10.8 0.7 copy-start.12
  11.6 0.7 copy-start.10
  11.6 0.7 copy-start.5
  11.6 0.7 copy-start.6
  40.3 12.8 %copy-start.7 = (bf16[128,1024]{1,0:T(8,128)(2,1)}, bf16[128,1024]{1,0:T(8,128)(2,1)S(1)}, u32[]{:S(2)}) copy-start(bf16[128,1024]{1,0:T(8,128)(2,1)S(1)} %get-tuple-element.44.xn_ref) | copy-start | bytes 786436
  72.2 4.2 %copy-start.8 = (bf16[128,1024]{1,0:T(8,128)(2,1)S(1)}, bf16[128,1024]{1,0:T(8,128)(2,1)}, u32[]{:S(2)}) copy-start(bf16[128,1024]{1,0:T(8,128)(2,1)} %copy-done.7) | copy-start | bytes 786436
  72.2 12.7 %all-to-all-start.4 = ((bf16[16,8,640]{2,1,0:T(8,128)(2,1)}), bf16[16,8,640]{2,1,0:T(8,128)(2,1)S(1)}, u32[]{:S(2)}, u32[]{:S(2)}) async-start(bf16[16,8,640]{2,1,0:T(8,128)(2,1)} %bitcast.3), calls=%async_computation.4 | async-start | bytes 327680 | tf_op jit(solution)/shard_map/all_to_all | solution.py:29
  76.4 1.0 %copy-start.2 = (bf16[8,128,128]{2,1,0:T(8,128)(2,1)S(1)}, bf16[8,128,128]{2,1,0:T(8,128)(2,1)}, u32[]{:S(2)}) copy-start(bf16[8,128,128]{2,1,0:T(8,128)(2,1)} %pair_ref.1) | copy-start | bytes 786436

commit v11 on v10

--- a/solution.py
+++ b/solution.py
@@ -168,7 +168,7 @@
 
 def norm_kernel(
     got_ref, t_ref, gain_ref, gate_ref, adj_ref, zn_ref, w_out_ref,
-    sent_ref, xn_ref, d_logit_ref, part_ref,
+    sent_ref, output_ref, d_logit_ref, part_ref,
 ):
     devices, depth, cols = got_ref.shape
     gain = column(gain_ref[...])
@@ -180,24 +180,15 @@
             lanes = slice(row * cols, (row + 1) * cols)
             hat, rstd = centred(mixed)
             pieces.append(back_t(t_ref[:, lanes].astype(F32), hat, rstd))
-            scaled = hat * gain
-            xn_ref[:, lanes] = scaled.astype(BF)
-            proj_out = dot(scaled.T.astype(BF), w_out_ref[...])
+            proj_out = dot((hat * gain).T.astype(BF), w_out_ref[...])
             gate = gate_ref[row]
+            output_ref[row] = (gate * proj_out).astype(BF)
             d_logit = (adj_ref[row].astype(F32) * proj_out * gate * (1.0 - gate)).astype(BF)
             d_logit_ref[row] = d_logit
             term = dot(zn_ref[:, lanes], d_logit)
             total = term if total is None else total + term
         sent_ref[:, two * 16 : two * 16 + 16, :] = two_rows(*pieces, devices)
     part_ref[...] = total
-
-
-def output_kernel(xn_ref, gate_ref, w_out_ref, output_ref):
-    rows, cols, width = gate_ref.shape
-    for row in range(rows):
-        lanes = slice(row * cols, (row + 1) * cols)
-        xn = xn_ref[:, lanes].astype(F32).T.astype(BF)
-        output_ref[row] = (gate_ref[row] * dot(xn, w_out_ref[...])).astype(BF)
 
 
 def unmix_kernel(got_ref, left_ref, right_ref, sent_ref, in_s, left_s, right_s):
@@ -235,31 +226,48 @@
     u_ref[...] = (u - jnp.mean(u, 0, keepdims=True)).astype(BF)
 
 
-def pair_kernel(u_ref, d_logit_ref, pair_ref, gain_ref, w_gate_ref, d_pair_ref):
+def sum_kernel(residues, got_ref, sent_ref):
+    total = jnp.sum(got_ref[...].astype(F32), 0) / residues
+    sent_ref[...] = jnp.broadcast_to(total.astype(BF)[None], sent_ref.shape)
+
+
+def finish_kernel(
+    got_ref, output_ref, u_ref, d_logit_ref, pair_ref, gain_ref, w_gate_ref,
+    output_out, d_pair_out, proj_out, gate_out,
+    d_pair_ref, proj_ref, gate_ref, sems, row_sems,
+):
+    devices, chunk, depth = got_ref.shape
     rows, cols, width = pair_ref.shape
+    wide = proj_ref.shape[1]
+    copies = [pltpu.make_async_copy(output_ref, output_out, sems.at[0])]
+    copies[0].start()
+    total = got_ref[...].astype(F32).reshape(devices * chunk, depth)
+    proj_ref[...] = total[:, :wide]
+    gate_ref[...] = total[:, wide:]
+    copies.append(pltpu.make_async_copy(proj_ref, proj_out, sems.at[1]))
+    copies.append(pltpu.make_async_copy(gate_ref, gate_out, sems.at[2]))
+    copies[1].start()
+    copies[2].start()
     gain = column(gain_ref[...])
+    half = rows // 2
     for row in range(rows):
         lanes = slice(row * cols, (row + 1) * cols)
         hat, rstd = centred(pair_ref[row].astype(F32).T)
         u = dot(w_gate_ref[...], d_logit_ref[row], ((1,), (1,))) * gain
         u = u + u_ref[:, lanes].astype(F32)
         d_pair_ref[row] = back_t(u, hat, rstd).T.astype(BF)
-
-
-def sum_kernel(residues, got_ref, sent_ref):
-    total = jnp.sum(got_ref[...].astype(F32), 0) / residues
-    sent_ref[...] = jnp.broadcast_to(total.astype(BF)[None], sent_ref.shape)
-
-
-def finish_kernel(got_ref, proj_ref, gate_ref):
-    devices, chunk, depth = got_ref.shape
-    wide = proj_ref.shape[1]
-    total = got_ref[...].astype(F32).reshape(devices * chunk, depth)
-    proj_ref[...] = total[:, :wide]
-    gate_ref[...] = total[:, wide:]
-
-
-def call(kernel, outs, scratch=(), flops=0, name=None, space=pltpu.VMEM, mib=12):
+        if row + 1 in (half, rows):
+            place = pl.ds(row + 1 - half, half)
+            at = row // half
+            copies.append(
+                pltpu.make_async_copy(d_pair_ref.at[place], d_pair_out.at[place], row_sems.at[at])
+            )
+            copies[-1].start()
+    for copy in copies:
+        copy.wait()
+
+
+def call(kernel, outs, scratch=(), flops=0, name=None, space=pltpu.VMEM, mib=12, away=()):
     spec = pl.BlockSpec(memory_space=pltpu.VMEM)
 
     def run(*args):
@@ -268,7 +276,7 @@
             kernel,
             out_shape=list(outs),
             in_specs=[pl.BlockSpec(memory_space=space)] * len(args),
-            out_specs=[spec] * len(outs),
+            out_specs=[pl.BlockSpec(memory_space=pl.ANY) if i in away else spec for i in range(len(outs))],
             scratch_shapes=list(scratch),
             compiler_params=pltpu.CompilerParams(vmem_limit_bytes=mib * 1024 * 1024),
             cost_estimate=pl.CostEstimate(
@@ -320,9 +328,9 @@
     got, t = lax.optimization_barrier((got, t))
     sent, left, right = call(mix_kernel, [block, channels, channels], [field] * 3, name="mix")(got)
     got = swap(sent)
-    sent, xn, d_logit, gate_part = call(
+    sent, output, d_logit, gate_part = call(
         norm_kernel,
-        [block, shape((hidden, cells), BF), shape(pair.shape, BF), shape((width, width), F32)],
+        [block, shape(pair.shape, BF), shape(pair.shape, BF), shape((width, width), F32)],
         name="norm",
     )(got, t, gain_out, gate, adjoint, zn, w_out)
     got = swap(sent)
@@ -337,20 +345,29 @@
         name="cells",
     )(got, factor, zn, gate_part, w_proj, columns)
     got = swap(part.reshape(devices, width // devices, -1))
-    d_pair = call(pair_kernel, [shape(pair.shape, BF)], flops=2 * 10**9, name="pair")(
-        u, d_logit, pair, gain_in, w_gate
-    )[0]
-    output = call(output_kernel, [shape(pair.shape, BF)], flops=2 * 10**9, name="output")(
-        xn, gate, w_out
-    )[0]
-    got, d_pair, output = lax.optimization_barrier((got, d_pair, output))
     sent = call(
         functools.partial(sum_kernel, residues), [shape(got.shape, BF)], name="sum"
     )(got)[0]
-    d_proj, d_gate = call(
-        finish_kernel, [shape((width, 4 * hidden), F32), shape((width, width), F32)], name="finish"
-    )(swap(sent))
-    return (output, d_pair, d_proj, d_gate)
+    return tuple(
+        call(
+            finish_kernel,
+            [
+                shape(pair.shape, BF),
+                shape(pair.shape, BF),
+                shape((width, 4 * hidden), F32),
+                shape((width, width), F32),
+            ],
+            [
+                pltpu.VMEM(pair.shape, BF),
+                pltpu.VMEM((width, 4 * hidden), F32),
+                pltpu.VMEM((width, width), F32),
+                pltpu.SemaphoreType.DMA((3,)),
+                pltpu.SemaphoreType.DMA((2,)),
+            ],
+            name="finish",
+            away=(0, 1, 2, 3),
+        )(swap(sent), output, u, d_logit, pair, gain_in, w_gate)
+    )
 
 
 def per_device(pair, adjoint, mask, chain, gain_in, w_proj, w_gate, chain_bias, gain_out, w_out):

time: 97.3 us -> 97.1 us (level)
  blocking collectives: 55.1 us -> 67.6 us
  waiting for transfers between devices: 17.5 us -> 11.4 us
  starting transfers between devices: 11.7 us -> 7.5 us
  Pallas kernels: 10.1 us -> 7.88 us
    all_to_all x4 -> x5, blocking collectives: 55.1 us -> 67.6 us  [swap(): lax.all_to_all(blocks, ('wide', 'narrow'), split_axis=0, concat_axis=0, t...]
    all_to_all x2 -> x1, waiting for transfers between devices: 17.5 us -> 11.4 us  [swap(): lax.all_to_all(blocks, ('wide', 'narrow'), split_axis=0, concat_axis=0, t...]
    all_to_all x2 -> x1, starting transfers between devices: 11.7 us -> 7.5 us  [swap(): lax.all_to_all(blocks, ('wide', 'narrow'), split_axis=0, concat_axis=0, t...]
    pallas_call x10 -> x8, Pallas kernels: 10.1 us -> 7.88 us  [run(): pl.pallas_call(kernel, out_shape=list(outs), in_specs=[pl.BlockSpec(memor...]
  transfers between devices with their start and end apart: 2 -> 1, of which waited for: 2 -> 1; matrix products, arithmetic and copies ran while one was open for 0% -> 0% of each run, Pallas kernels for 4% -> 2%
where the time goes in v11:
time: 97.1 us; the launch traced here: 96.6 us
  blocking collectives  67.6 us (70%)
  waiting for transfers between devices  11.4 us (12%)
  Pallas kernels  7.88 us (8%)
  starting transfers between devices  7.5 us (8%)
  local copies, waits for them, and re-layouts  1.4 us (1%)
    all_to_all x5, blocking collectives, swap(): lax.all_to_all(blocks, ('wide', 'narrow'), split_axis=0, concat_axis=0, t...  67.6 us
    all_to_all x1, waiting for transfers between devices, swap(): lax.all_to_all(blocks, ('wide', 'narrow'), split_axis=0, concat_axis=0, t...  11.4 us
    pallas_call x8, Pallas kernels, run(): pl.pallas_call(kernel, out_shape=list(outs), in_specs=[pl.BlockSpec(memor...  7.88 us
    all_to_all x1, starting transfers between devices, swap(): lax.all_to_all(blocks, ('wide', 'narrow'), split_axis=0, concat_axis=0, t...  7.5 us
  transfers between devices with their start and end apart: 1, of which 1 were waited for; matrix products, arithmetic and copies ran while one was open for 0% of the time, Pallas kernels for 2%

profile of v11, /device:TPU:0, one launch (start us, length us, event | category | flops | bytes accessed | tf_op | source)
XLA Modules:
  0.0 96.6 jit_solution(10831912459849448473)
XLA Ops:
  0.6 2.5 %project.1 = (bf16[16,128,128]{2,1,0:T(8,128)(2,1)}, bf16[128,1024]{1,0:T(8,128)(2,1)}, f32[8,128]{1,0:T(8,128)}) custom-call(bf16[8,128,128]{2,1,0:T(8,128)(2,1)} %pair_ref.1, s32[1,128]{1,0:T(1,128)} %bitcast.10, f32[1,128]{1,0:T(1,128)} %bitcast.5, bf16[128,512]{1,0:T(8,128)(2,1)} %w_ref.3), custom_call_target="tpu_custom_call" | custom-call | bytes 1184768 | tf_op jit(solution)/shard_map/project/pallas_call | solution.py:275
  3.2 0.0 copy-start.1
  3.2 0.0 copy-start.2
  3.2 0.0 copy-start.3
  3.2 0.0 copy-start.4
  3.2 0.0 copy-start.5
  3.2 7.5 %all-to-all-start = ((bf16[16,128,128]{2,1,0:T(8,128)(2,1)}), bf16[16,128,128]{2,1,0:T(8,128)(2,1)S(1)}, u32[]{:S(2)}, u32[]{:S(2)}) async-start(bf16[16,128,128]{2,1,0:T(8,128)(2,1)} %get-tuple-element.22), calls=%async_computation | async-start | bytes 1048576 | tf_op jit(solution)/shard_map/all_to_all | solution.py:29
  10.7 0.0 copy-start.10
  10.8 0.7 copy-done.10
  11.4 0.1 dynamic_slice.3
  11.5 0.1 compare_convert_fusion.same_ref
  11.6 0.6 copy-done.8
  12.2 1.6 %gate.1 = (bf16[512,1024]{1,0:T(8,128)(2,1)S(1)}, f32[8,128,128]{2,1,0:T(8,128)S(1)}, bf16[128,1024]{1,0:T(8,128)(2,1)S(1)}, f32[128,128]{1,0:T(8,128)S(1)}) custom-call(bf16[128,1024]{1,0:T(8,128)(2,1)S(1)} %copy-done.1, bf16[8,128,128]{2,1,0:T(8,128)(2,1)S(1)} %copy-done.3, f32[8,128]{1,0:T(8,128)S(1)} %copy-done.8, ...), custom_call_target="tpu_custom_call" | custom-call | flops 2000000000 | bytes 2631680 | tf_op jit(solution)/shard_map/gate/pallas_call | solution.py:275
  13.8 11.4 %all-to-all-done.got_ref = bf16[16,128,128]{2,1,0:T(8,128)(2,1)S(1)} async-done(((bf16[16,128,128]{2,1,0:T(8,128)(2,1)}), bf16[16,128,128]{2,1,0:T(8,128)(2,1)S(1)}, u32[]{:S(2)}, u32[]{:S(2)}) %all-to-all-start) | async-done | bytes 524320 | tf_op jit(solution)/shard_map/all_to_all | solution.py:29
  25.2 0.4 mix.1
  25.6 13.9 %all_to_all.30.got_ref = bf16[16,64,128]{2,1,0:T(8,128)(2,1)S(1)} all-to-all(bf16[16,64,128]{2,1,0:T(8,128)(2,1)S(1)} %get-tuple-element.27), channel_id=1, replica_groups=mesh['groups'=2,'wide'=16,'narrow'=1] {'wide','narrow'}, dimensions={0} | all-to-all | bytes 524288 | tf_op jit(solution)/shard_map/all_to_all | solution.py:29
  39.5 0.7 norm.1
  40.3 12.8 %all_to_all.31.got_ref = bf16[16,64,128]{2,1,0:T(8,128)(2,1)S(1)} all-to-all(bf16[16,64,128]{2,1,0:T(8,128)(2,1)S(1)} %get-tuple-element.30), channel_id=1, replica_groups=mesh['groups'=2,'wide'=16,'narrow'=1] {'wide','narrow'}, dimensions={0} | all-to-all | bytes 524288 | tf_op jit(solution)/shard_map/all_to_all | solution.py:29
  53.1 0.4 unmix.1
  53.5 17.2 %all_to_all.32.got_ref = bf16[16,128,128]{2,1,0:T(8,128)(2,1)S(1)} all-to-all(bf16[16,128,128]{2,1,0:T(8,128)(2,1)S(1)} %unmix.1), channel_id=1, replica_groups=mesh['groups'=2,'wide'=16,'narrow'=1] {'wide','narrow'}, dimensions={0} | all-to-all | bytes 1048576 | tf_op jit(solution)/shard_map/all_to_all | solution.py:29
  70.8 0.8 cells.1
  71.6 12.4 %all_to_all.33.got_ref = bf16[16,8,640]{2,1,0:T(8,128)(2,1)S(1)} all-to-all(bf16[16,8,640]{2,1,0:T(8,128)(2,1)S(1)} %bitcast.4), channel_id=1, replica_groups=mesh['groups'=2,'wide'=16,'narrow'=1] {'wide','narrow'}, dimensions={0} | all-to-all | bytes 327680 | tf_op jit(solution)/shard_map/all_to_all | solution.py:29
  84.0 11.2 %all_to_all.34.got_ref = bf16[16,8,640]{2,1,0:T(8,128)(2,1)S(1)} all-to-all(bf16[16,8,640]{2,1,0:T(8,128)(2,1)S(1)} %sum.1), channel_id=1, replica_groups=mesh['groups'=2,'wide'=16,'narrow'=1] {'wide','narrow'}, dimensions={0} | all-to-all | bytes 327680 | tf_op jit(solution)/shard_map/all_to_all | solution.py:29
  95.2 1.4 %finish.1 = (bf16[8,128,128]{2,1,0:T(8,128)(2,1)}, bf16[8,128,128]{2,1,0:T(8,128)(2,1)}, f32[128,512]{1,0:T(8,128)}, f32[128,128]{1,0:T(8,128)}) custom-call(bf16[16,8,640]{2,1,0:T(8,128)(2,1)S(1)} %all_to_all.34.got_ref, bf16[8,128,128]{2,1,0:T(8,128)(2,1)S(1)} %get-tuple-element.37.output_ref, bf16[128,1024]{1,0:T(8,128)(2,1)S(1)} %get-tuple-element.38.u_ref, ...), custom_call_target="tpu_custom_call" | custom-call | bytes 2097664 | tf_op jit(solution)/shard_map/finish/pallas_call | solution.py:275
  (15 shorter events, 0.1 us)
Async XLA Ops:
  3.2 8.4 %copy-start.1 = (bf16[128,1024]{1,0:T(8,128)(2,1)S(1)}, bf16[128,1024]{1,0:T(8,128)(2,1)}, u32[]{:S(2)}) copy-start(bf16[128,1024]{1,0:T(8,128)(2,1)} %get-tuple-element.23.zn_ref) | copy-start | bytes 786436
  3.2 8.4 %copy-start.2 = (bf16[128,512]{1,0:T(8,128)(2,1)S(1)}, bf16[128,512]{1,0:T(8,128)(2,1)}, u32[]{:S(2)}) copy-start(bf16[128,512]{1,0:T(8,128)(2,1)} %w_ref.3) | copy-start | bytes 393220
  3.2 8.4 %copy-start.3 = (bf16[8,128,128]{2,1,0:T(8,128)(2,1)S(1)}, bf16[8,128,128]{2,1,0:T(8,128)(2,1)}, u32[]{:S(2)}) copy-start(bf16[8,128,128]{2,1,0:T(8,128)(2,1)} %adj_ref.3) | copy-start | bytes 786436
  3.2 8.4 %copy-start.4 = (bf16[128,128]{1,0:T(8,128)(2,1)S(1)}, bf16[128,128]{1,0:T(8,128)(2,1)}, u32[]{:S(2)}) copy-start(bf16[128,128]{1,0:T(8,128)(2,1)} %w_out_ref.3) | copy-start | bytes 98308
  3.2 8.4 %copy-start.5 = (bf16[128,128]{1,0:T(8,128)(2,1)S(1)}, bf16[128,128]{1,0:T(8,128)(2,1)}, u32[]{:S(2)}) copy-start(bf16[128,128]{1,0:T(8,128)(2,1)} %w_gate_ref.3) | copy-start | bytes 98308
  3.2 22.0 %all-to-all-start = ((bf16[16,128,128]{2,1,0:T(8,128)(2,1)}), bf16[16,128,128]{2,1,0:T(8,128)(2,1)S(1)}, u32[]{:S(2)}, u32[]{:S(2)}) async-start(bf16[16,128,128]{2,1,0:T(8,128)(2,1)} %get-tuple-element.22), calls=%async_computation | async-start | bytes 1048576 | tf_op jit(solution)/shard_map/all_to_all | solution.py:29
  10.7 0.9 copy-start.9
  10.7 0.7 copy-start.10
  11.6 0.7 copy-start.8
  11.6 0.7 copy-start.6
  11.6 0.7 copy-start.7
  83.9 11.2 %copy-start = (bf16[8,128,128]{2,1,0:T(8,128)(2,1)S(1)}, bf16[8,128,128]{2,1,0:T(8,128)(2,1)}, u32[]{:S(2)}) copy-start(bf16[8,128,128]{2,1,0:T(8,128)(2,1)} %pair_ref.1) | copy-start | bytes 786436

commit v12 on v11

--- a/solution.py
+++ b/solution.py
@@ -121,7 +121,7 @@
 
 def gate_kernel(
     zn_ref, adj_ref, mask_ref, same_ref, w_ref, w_gate_ref, bias_ref, gain_ref, w_out_ref,
-    gain_in_ref, factor_ref, gate_ref, t_ref, columns_ref,
+    gain_in_ref, pair_ref, factor_ref, gate_ref, t_ref, columns_ref, hat_ref, rstd_ref,
 ):
     rows, cols, width = adj_ref.shape
     weights = w_ref[...].astype(F32).T.astype(BF)
@@ -148,6 +148,9 @@
         d_out = (adj_ref[row].astype(F32) * gate).astype(BF)
         t = dot(w_out_ref[...], d_out, ((1,), (1,))) * gain
         t_ref[:, lanes] = (t - jnp.mean(t, 0, keepdims=True)).astype(BF)
+        hat, rstd = centred(pair_ref[row].astype(F32).T)
+        hat_ref[:, lanes] = hat
+        rstd_ref[row : row + 1, :] = rstd
 
 
 def mix_kernel(got_ref, sent_ref, left_ref, right_ref, left_s, right_s, out_s):
@@ -232,12 +235,12 @@
 
 
 def finish_kernel(
-    got_ref, output_ref, u_ref, d_logit_ref, pair_ref, gain_ref, w_gate_ref,
+    got_ref, output_ref, u_ref, d_logit_ref, hat_ref, rstd_ref, columns_ref, w_gate_ref,
     output_out, d_pair_out, proj_out, gate_out,
     d_pair_ref, proj_ref, gate_ref, sems, row_sems,
 ):
     devices, chunk, depth = got_ref.shape
-    rows, cols, width = pair_ref.shape
+    rows, cols, width = d_logit_ref.shape
     wide = proj_ref.shape[1]
     copies = [pltpu.make_async_copy(output_ref, output_out, sems.at[0])]
     copies[0].start()
@@ -248,14 +251,15 @@
     copies.append(pltpu.make_async_copy(gate_ref, gate_out, sems.at[2]))
     copies[1].start()
     copies[2].start()
-    gain = column(gain_ref[...])
+    gain = columns_ref[...]
     half = rows // 2
     for row in range(rows):
         lanes = slice(row * cols, (row + 1) * cols)
-        hat, rstd = centred(pair_ref[row].astype(F32).T)
         u = dot(w_gate_ref[...], d_logit_ref[row], ((1,), (1,))) * gain
         u = u + u_ref[:, lanes].astype(F32)
-        d_pair_ref[row] = back_t(u, hat, rstd).T.astype(BF)
+        d_pair_ref[row] = back_t(
+            u, hat_ref[:, lanes], rstd_ref[row : row + 1, :]
+        ).T.astype(BF)
         if row + 1 in (half, rows):
             place = pl.ds(row + 1 - half, half)
             at = row // half
@@ -316,12 +320,12 @@
         mib=56,
     )(pair, mask[None], gain_in, w_proj)
     got = swap(sent)
-    factor, gate, t, columns = call(
+    factor, gate, t, columns, hat, rstd = call(
         gate_kernel,
-        [shape((4 * hidden, cells), BF), shape((rows, cols, width), F32), shape((hidden, cells), BF), shape((width, width), F32)],
+        [shape((4 * hidden, cells), BF), shape((rows, cols, width), F32), shape((hidden, cells), BF), shape((width, width), F32), shape((width, cells), F32), shape((rows, cols), F32)],
         flops=2 * 10**9,
         name="gate",
-    )(zn, adjoint, cell_mask, same, w_proj, w_gate, chain_bias, gain_out, w_out, gain_in)
+    )(zn, adjoint, cell_mask, same, w_proj, w_gate, chain_bias, gain_out, w_out, gain_in, pair)
     field = pltpu.VMEM((devices * half, cols), F32)
     channels = shape((own, residues, cols), BF)
     block = shape((devices, half, cols), BF)
@@ -366,7 +370,7 @@
             ],
             name="finish",
             away=(0, 1, 2, 3),
-        )(swap(sent), output, u, d_logit, pair, gain_in, w_gate)
+        )(swap(sent), output, u, d_logit, hat, rstd, columns, w_gate)
     )
 
 

time: 97.1 us -> 96.9 us (level)
  waiting for transfers between devices: 11.4 us -> 9.61 us
  local copies, waits for them, and re-layouts: 1.4 us -> 3.06 us
    all_to_all x1, waiting for transfers between devices: 11.4 us -> 9.61 us  [swap(): lax.all_to_all(blocks, ('wide', 'narrow'), split_axis=0, concat_axis=0, t...]
    unnamed x22 -> x28, local copies, waits for them, and re-layouts: 1.33 us -> 2.99 us
where the time goes in v12:
time: 96.9 us; the launch traced here: 96.4 us
  blocking collectives  67.5 us (70%)
  waiting for transfers between devices  9.61 us (10%)
  Pallas kernels  7.8 us (8%)
  starting transfers between devices  7.5 us (8%)
  local copies, waits for them, and re-layouts  3.06 us (3%)
    all_to_all x5, blocking collectives, swap(): lax.all_to_all(blocks, ('wide', 'narrow'), split_axis=0, concat_axis=0, t...  67.5 us
    all_to_all x1, waiting for transfers between devices, swap(): lax.all_to_all(blocks, ('wide', 'narrow'), split_axis=0, concat_axis=0, t...  9.61 us
    pallas_call x8, Pallas kernels, run(): pl.pallas_call(kernel, out_shape=list(outs), in_specs=[pl.BlockSpec(memor...  7.8 us
    all_to_all x1, starting transfers between devices, swap(): lax.all_to_all(blocks, ('wide', 'narrow'), split_axis=0, concat_axis=0, t...  7.5 us
    unnamed x28, local copies, waits for them, and re-layouts  2.99 us
  transfers between devices with their start and end apart: 1, of which 1 were waited for; matrix products, arithmetic and copies ran while one was open for 0% of the time, Pallas kernels for 2%

profile of v12, /device:TPU:0, one launch (start us, length us, event | category | flops | bytes accessed | tf_op | source)
XLA Modules:
  0.0 96.4 jit_solution(11400141047512293679)
XLA Ops:
  0.6 2.5 %project.1 = (bf16[16,128,128]{2,1,0:T(8,128)(2,1)}, bf16[128,1024]{1,0:T(8,128)(2,1)}, f32[8,128]{1,0:T(8,128)}) custom-call(bf16[8,128,128]{2,1,0:T(8,128)(2,1)} %pair_ref.1, s32[1,128]{1,0:T(1,128)} %bitcast.9, f32[1,128]{1,0:T(1,128)} %bitcast.5, bf16[128,512]{1,0:T(8,128)(2,1)} %w_ref.3), custom_call_target="tpu_custom_call" | custom-call | bytes 1184768 | tf_op jit(solution)/shard_map/project/pallas_call | solution.py:279
  3.2 0.0 copy-start
  3.2 0.0 copy-start.1
  3.2 0.0 copy-start.2
  3.2 7.5 %all-to-all-start = ((bf16[16,128,128]{2,1,0:T(8,128)(2,1)}), bf16[16,128,128]{2,1,0:T(8,128)(2,1)S(1)}, u32[]{:S(2)}, u32[]{:S(2)}) async-start(bf16[16,128,128]{2,1,0:T(8,128)(2,1)} %get-tuple-element.24), calls=%async_computation | async-start | bytes 1048576 | tf_op jit(solution)/shard_map/all_to_all | solution.py:29
  10.7 0.0 copy-start.13
  10.8 0.7 copy-done.13
  11.4 0.1 dynamic_slice.3
  11.5 0.1 compare_convert_fusion.same_ref
  11.6 0.6 copy-done.11
  12.2 0.9 copy-done.3
  13.2 1.7 %gate.1 = (bf16[512,1024]{1,0:T(8,128)(2,1)S(1)}, f32[8,128,128]{2,1,0:T(8,128)S(1)}, bf16[128,1024]{1,0:T(8,128)(2,1)S(1)}, f32[128,128]{1,0:T(8,128)S(1)}, f32...) custom-call(bf16[128,1024]{1,0:T(8,128)(2,1)S(1)} %copy-done, bf16[8,128,128]{2,1,0:T(8,128)(2,1)S(1)} %copy-done.3, ...), custom_call_target="tpu_custom_call" | custom-call | flops 2000000000 | bytes 3422208 | tf_op jit(solution)/shard_map/gate/pallas_call | solution.py:279
  14.9 0.7 copy-done.5
  15.6 9.6 %all-to-all-done.got_ref = bf16[16,128,128]{2,1,0:T(8,128)(2,1)S(1)} async-done(((bf16[16,128,128]{2,1,0:T(8,128)(2,1)}), bf16[16,128,128]{2,1,0:T(8,128)(2,1)S(1)}, u32[]{:S(2)}, u32[]{:S(2)}) %all-to-all-start) | async-done | bytes 524320 | tf_op jit(solution)/shard_map/all_to_all | solution.py:29
  25.2 0.4 mix.1
  25.6 14.1 %all_to_all.30.got_ref = bf16[16,64,128]{2,1,0:T(8,128)(2,1)S(1)} all-to-all(bf16[16,64,128]{2,1,0:T(8,128)(2,1)S(1)} %get-tuple-element.29), channel_id=1, replica_groups=mesh['groups'=2,'wide'=16,'narrow'=1] {'wide','narrow'}, dimensions={0} | all-to-all | bytes 524288 | tf_op jit(solution)/shard_map/all_to_all | solution.py:29
  39.7 0.7 norm.1
  40.4 12.8 %all_to_all.31.got_ref = bf16[16,64,128]{2,1,0:T(8,128)(2,1)S(1)} all-to-all(bf16[16,64,128]{2,1,0:T(8,128)(2,1)S(1)} %get-tuple-element.32), channel_id=1, replica_groups=mesh['groups'=2,'wide'=16,'narrow'=1] {'wide','narrow'}, dimensions={0} | all-to-all | bytes 524288 | tf_op jit(solution)/shard_map/all_to_all | solution.py:29
  53.2 0.4 unmix.1
  53.7 17.2 %all_to_all.32.got_ref = bf16[16,128,128]{2,1,0:T(8,128)(2,1)S(1)} all-to-all(bf16[16,128,128]{2,1,0:T(8,128)(2,1)S(1)} %unmix.1), channel_id=1, replica_groups=mesh['groups'=2,'wide'=16,'narrow'=1] {'wide','narrow'}, dimensions={0} | all-to-all | bytes 1048576 | tf_op jit(solution)/shard_map/all_to_all | solution.py:29
  70.9 0.8 cells.1
  71.7 12.4 %all_to_all.33.got_ref = bf16[16,8,640]{2,1,0:T(8,128)(2,1)S(1)} all-to-all(bf16[16,8,640]{2,1,0:T(8,128)(2,1)S(1)} %bitcast.4), channel_id=1, replica_groups=mesh['groups'=2,'wide'=16,'narrow'=1] {'wide','narrow'}, dimensions={0} | all-to-all | bytes 327680 | tf_op jit(solution)/shard_map/all_to_all | solution.py:29
  84.1 11.1 %all_to_all.34.got_ref = bf16[16,8,640]{2,1,0:T(8,128)(2,1)S(1)} all-to-all(bf16[16,8,640]{2,1,0:T(8,128)(2,1)S(1)} %sum.1), channel_id=1, replica_groups=mesh['groups'=2,'wide'=16,'narrow'=1] {'wide','narrow'}, dimensions={0} | all-to-all | bytes 327680 | tf_op jit(solution)/shard_map/all_to_all | solution.py:29
  95.1 1.3 %finish.1 = (bf16[8,128,128]{2,1,0:T(8,128)(2,1)}, bf16[8,128,128]{2,1,0:T(8,128)(2,1)}, f32[128,512]{1,0:T(8,128)}, f32[128,128]{1,0:T(8,128)}) custom-call(bf16[16,8,640]{2,1,0:T(8,128)(2,1)S(1)} %all_to_all.34.got_ref, bf16[8,128,128]{2,1,0:T(8,128)(2,1)S(1)} %get-tuple-element.39.output_ref, bf16[128,1024]{1,0:T(8,128)(2,1)S(1)} %get-tuple-element.40.u_ref, ...), custom_call_target="tpu_custom_call" | custom-call | bytes 2428928 | tf_op jit(solution)/shard_map/finish/pallas_call | solution.py:279
  (21 shorter events, 0.1 us)
Async XLA Ops:
  3.2 8.4 %copy-start = (bf16[128,1024]{1,0:T(8,128)(2,1)S(1)}, bf16[128,1024]{1,0:T(8,128)(2,1)}, u32[]{:S(2)}) copy-start(bf16[128,1024]{1,0:T(8,128)(2,1)} %get-tuple-element.25.zn_ref) | copy-start | bytes 786436
  3.2 8.4 %copy-start.1 = (bf16[128,512]{1,0:T(8,128)(2,1)S(1)}, bf16[128,512]{1,0:T(8,128)(2,1)}, u32[]{:S(2)}) copy-start(bf16[128,512]{1,0:T(8,128)(2,1)} %w_ref.3) | copy-start | bytes 393220
  3.2 8.4 %copy-start.2 = (bf16[8,128,128]{2,1,0:T(8,128)(2,1)S(1)}, bf16[8,128,128]{2,1,0:T(8,128)(2,1)}, u32[]{:S(2)}) copy-start(bf16[8,128,128]{2,1,0:T(8,128)(2,1)} %pair_ref.1) | copy-start | bytes 786436
  3.2 8.4 %copy-start.7 = (bf16[128,128]{1,0:T(8,128)(2,1)S(1)}, bf16[128,128]{1,0:T(8,128)(2,1)}, u32[]{:S(2)}) copy-start(bf16[128,128]{1,0:T(8,128)(2,1)} %w_out_ref.3) | copy-start | bytes 98308
  3.2 8.4 %copy-start.8 = (bf16[128,128]{1,0:T(8,128)(2,1)S(1)}, bf16[128,128]{1,0:T(8,128)(2,1)}, u32[]{:S(2)}) copy-start(bf16[128,128]{1,0:T(8,128)(2,1)} %w_gate_ref.3) | copy-start | bytes 98308
  3.2 22.0 %all-to-all-start = ((bf16[16,128,128]{2,1,0:T(8,128)(2,1)}), bf16[16,128,128]{2,1,0:T(8,128)(2,1)S(1)}, u32[]{:S(2)}, u32[]{:S(2)}) async-start(bf16[16,128,128]{2,1,0:T(8,128)(2,1)} %get-tuple-element.24), calls=%async_computation | async-start | bytes 1048576 | tf_op jit(solution)/shard_map/all_to_all | solution.py:29
  10.7 0.9 copy-start.12
  10.7 0.7 copy-start.13
  11.6 0.7 copy-start.11
  11.6 0.7 copy-start.9
  11.6 0.7 copy-start.10
  12.2 1.0 copy-start.3
  14.9 0.7 copy-start.5
  25.6 14.1 %copy-start.4 = (bf16[8,128,128]{2,1,0:T(8,128)(2,1)S(1)}, bf16[8,128,128]{2,1,0:T(8,128)(2,1)}, u32[]{:S(2)}) copy-start(bf16[8,128,128]{2,1,0:T(8,128)(2,1)} %adj_ref.3) | copy-start | bytes 786436
  25.6 14.1 %copy-start.6 = (bf16[128,1024]{1,0:T(8,128)(2,1)S(1)}, bf16[128,1024]{1,0:T(8,128)(2,1)}, u32[]{:S(2)}) copy-start(bf16[128,1024]{1,0:T(8,128)(2,1)} %copy-done.5) | copy-start | bytes 786436

commit v13 on v12

--- a/solution.py
+++ b/solution.py
@@ -86,10 +86,16 @@
     start = lax.axis_index("wide") * rows
     copies = [
         pltpu.make_async_copy(gain_hbm, gain_ref, sems.at[0]),
-        pltpu.make_async_copy(w_hbm, w_ref, sems.at[1]),
-        pltpu.make_async_copy(mask_hbm, mask_v, sems.at[2]),
-        pltpu.make_async_copy(pair_hbm, pair_ref, sems.at[3]),
+        pltpu.make_async_copy(mask_hbm, mask_v, sems.at[1]),
     ]
+    for at in range(4):
+        place = pl.ds(at * (rows // 4), rows // 4)
+        copies.append(
+            pltpu.make_async_copy(pair_hbm.at[place], pair_ref.at[place], sems.at[2 + at])
+        )
+    for at in range(2):
+        place = pl.ds(at * (width // 2), width // 2)
+        copies.append(pltpu.make_async_copy(w_hbm.at[place], w_ref.at[place], sems.at[6 + at]))
     for copy in copies:
         copy.start()
     for copy in copies:
@@ -313,7 +319,7 @@
             pltpu.VMEM((1, residues), jnp.int32),
             pltpu.VMEM(gain_in.shape, F32),
             pltpu.VMEM(w_proj.shape, BF),
-            pltpu.SemaphoreType.DMA((4,)),
+            pltpu.SemaphoreType.DMA((8,)),
         ],
         name="project",
         space=pltpu.HBM,

time: 96.9 us -> 97 us (level)
  no operation moved by 1% of the time
where the time goes in v13:
time: 97 us; the launch traced here: 96.4 us
  blocking collectives  67.6 us (70%)
  waiting for transfers between devices  9.61 us (10%)
  Pallas kernels  7.81 us (8%)
  starting transfers between devices  7.5 us (8%)
  local copies, waits for them, and re-layouts  3.06 us (3%)
    all_to_all x5, blocking collectives, swap(): lax.all_to_all(blocks, ('wide', 'narrow'), split_axis=0, concat_axis=0, t...  67.6 us
    all_to_all x1, waiting for transfers between devices, swap(): lax.all_to_all(blocks, ('wide', 'narrow'), split_axis=0, concat_axis=0, t...  9.61 us
    pallas_call x8, Pallas kernels, run(): pl.pallas_call(kernel, out_shape=list(outs), in_specs=[pl.BlockSpec(memor...  7.81 us
    all_to_all x1, starting transfers between devices, swap(): lax.all_to_all(blocks, ('wide', 'narrow'), split_axis=0, concat_axis=0, t...  7.5 us
    unnamed x28, local copies, waits for them, and re-layouts  2.99 us
  transfers between devices with their start and end apart: 1, of which 1 were waited for; matrix products, arithmetic and copies ran while one was open for 0% of the time, Pallas kernels for 2%

profile of v13, /device:TPU:0, one launch (start us, length us, event | category | flops | bytes accessed | tf_op | source)
XLA Modules:
  0.0 96.4 jit_solution(11520954265384019802)
XLA Ops:
  0.6 2.5 %project.1 = (bf16[16,128,128]{2,1,0:T(8,128)(2,1)}, bf16[128,1024]{1,0:T(8,128)(2,1)}, f32[8,128]{1,0:T(8,128)}) custom-call(bf16[8,128,128]{2,1,0:T(8,128)(2,1)} %pair_ref.1, s32[1,128]{1,0:T(1,128)} %bitcast.9, f32[1,128]{1,0:T(1,128)} %bitcast.5, bf16[128,512]{1,0:T(8,128)(2,1)} %w_ref.3), custom_call_target="tpu_custom_call" | custom-call | bytes 1184768 | tf_op jit(solution)/shard_map/project/pallas_call | solution.py:285
  3.2 0.0 copy-start
  3.2 0.0 copy-start.7
  3.2 0.0 copy-start.8
  3.2 7.5 %all-to-all-start = ((bf16[16,128,128]{2,1,0:T(8,128)(2,1)}), bf16[16,128,128]{2,1,0:T(8,128)(2,1)S(1)}, u32[]{:S(2)}, u32[]{:S(2)}) async-start(bf16[16,128,128]{2,1,0:T(8,128)(2,1)} %get-tuple-element.24), calls=%async_computation | async-start | bytes 1048576 | tf_op jit(solution)/shard_map/all_to_all | solution.py:29
  10.8 0.0 copy-start.13
  10.8 0.7 copy-done.13
  11.4 0.1 dynamic_slice.3
  11.5 0.1 compare_convert_fusion.same_ref
  11.6 0.6 copy-done.11
  12.3 0.9 copy-done.3
  13.2 1.7 %gate.1 = (bf16[512,1024]{1,0:T(8,128)(2,1)S(1)}, f32[8,128,128]{2,1,0:T(8,128)S(1)}, bf16[128,1024]{1,0:T(8,128)(2,1)S(1)}, f32[128,128]{1,0:T(8,128)S(1)}, f32...) custom-call(bf16[128,1024]{1,0:T(8,128)(2,1)S(1)} %copy-done, bf16[8,128,128]{2,1,0:T(8,128)(2,1)S(1)} %copy-done.3, ...), custom_call_target="tpu_custom_call" | custom-call | flops 2000000000 | bytes 3422208 | tf_op jit(solution)/shard_map/gate/pallas_call | solution.py:285
  14.9 0.7 copy-done.5
  15.6 9.6 %all-to-all-done.got_ref = bf16[16,128,128]{2,1,0:T(8,128)(2,1)S(1)} async-done(((bf16[16,128,128]{2,1,0:T(8,128)(2,1)}), bf16[16,128,128]{2,1,0:T(8,128)(2,1)S(1)}, u32[]{:S(2)}, u32[]{:S(2)}) %all-to-all-start) | async-done | bytes 524320 | tf_op jit(solution)/shard_map/all_to_all | solution.py:29
  25.2 0.4 mix.1
  25.6 14.1 %all_to_all.30.got_ref = bf16[16,64,128]{2,1,0:T(8,128)(2,1)S(1)} all-to-all(bf16[16,64,128]{2,1,0:T(8,128)(2,1)S(1)} %get-tuple-element.29), channel_id=1, replica_groups=mesh['groups'=2,'wide'=16,'narrow'=1] {'wide','narrow'}, dimensions={0} | all-to-all | bytes 524288 | tf_op jit(solution)/shard_map/all_to_all | solution.py:29
  39.7 0.7 norm.1
  40.4 12.8 %all_to_all.31.got_ref = bf16[16,64,128]{2,1,0:T(8,128)(2,1)S(1)} all-to-all(bf16[16,64,128]{2,1,0:T(8,128)(2,1)S(1)} %get-tuple-element.32), channel_id=1, replica_groups=mesh['groups'=2,'wide'=16,'narrow'=1] {'wide','narrow'}, dimensions={0} | all-to-all | bytes 524288 | tf_op jit(solution)/shard_map/all_to_all | solution.py:29
  53.3 0.4 unmix.1
  53.7 17.2 %all_to_all.32.got_ref = bf16[16,128,128]{2,1,0:T(8,128)(2,1)S(1)} all-to-all(bf16[16,128,128]{2,1,0:T(8,128)(2,1)S(1)} %unmix.1), channel_id=1, replica_groups=mesh['groups'=2,'wide'=16,'narrow'=1] {'wide','narrow'}, dimensions={0} | all-to-all | bytes 1048576 | tf_op jit(solution)/shard_map/all_to_all | solution.py:29
  70.9 0.8 cells.1
  71.7 12.4 %all_to_all.33.got_ref = bf16[16,8,640]{2,1,0:T(8,128)(2,1)S(1)} all-to-all(bf16[16,8,640]{2,1,0:T(8,128)(2,1)S(1)} %bitcast.4), channel_id=1, replica_groups=mesh['groups'=2,'wide'=16,'narrow'=1] {'wide','narrow'}, dimensions={0} | all-to-all | bytes 327680 | tf_op jit(solution)/shard_map/all_to_all | solution.py:29
  84.1 11.1 %all_to_all.34.got_ref = bf16[16,8,640]{2,1,0:T(8,128)(2,1)S(1)} all-to-all(bf16[16,8,640]{2,1,0:T(8,128)(2,1)S(1)} %sum.1), channel_id=1, replica_groups=mesh['groups'=2,'wide'=16,'narrow'=1] {'wide','narrow'}, dimensions={0} | all-to-all | bytes 327680 | tf_op jit(solution)/shard_map/all_to_all | solution.py:29
  95.2 1.3 %finish.1 = (bf16[8,128,128]{2,1,0:T(8,128)(2,1)}, bf16[8,128,128]{2,1,0:T(8,128)(2,1)}, f32[128,512]{1,0:T(8,128)}, f32[128,128]{1,0:T(8,128)}) custom-call(bf16[16,8,640]{2,1,0:T(8,128)(2,1)S(1)} %all_to_all.34.got_ref, bf16[8,128,128]{2,1,0:T(8,128)(2,1)S(1)} %get-tuple-element.39.output_ref, bf16[128,1024]{1,0:T(8,128)(2,1)S(1)} %get-tuple-element.40.u_ref, ...), custom_call_target="tpu_custom_call" | custom-call | bytes 2428928 | tf_op jit(solution)/shard_map/finish/pallas_call | solution.py:285
  (21 shorter events, 0.1 us)
Async XLA Ops:
  3.2 8.4 %copy-start = (bf16[128,1024]{1,0:T(8,128)(2,1)S(1)}, bf16[128,1024]{1,0:T(8,128)(2,1)}, u32[]{:S(2)}) copy-start(bf16[128,1024]{1,0:T(8,128)(2,1)} %get-tuple-element.25.zn_ref) | copy-start | bytes 786436
  3.2 8.4 %copy-start.1 = (bf16[128,512]{1,0:T(8,128)(2,1)S(1)}, bf16[128,512]{1,0:T(8,128)(2,1)}, u32[]{:S(2)}) copy-start(bf16[128,512]{1,0:T(8,128)(2,1)} %w_ref.3) | copy-start | bytes 393220
  3.2 8.4 %copy-start.2 = (bf16[8,128,128]{2,1,0:T(8,128)(2,1)S(1)}, bf16[8,128,128]{2,1,0:T(8,128)(2,1)}, u32[]{:S(2)}) copy-start(bf16[8,128,128]{2,1,0:T(8,128)(2,1)} %pair_ref.1) | copy-start | bytes 786436
  3.2 8.4 %copy-start.7 = (bf16[128,128]{1,0:T(8,128)(2,1)S(1)}, bf16[128,128]{1,0:T(8,128)(2,1)}, u32[]{:S(2)}) copy-start(bf16[128,128]{1,0:T(8,128)(2,1)} %w_out_ref.3) | copy-start | bytes 98308
  3.2 8.4 %copy-start.8 = (bf16[128,128]{1,0:T(8,128)(2,1)S(1)}, bf16[128,128]{1,0:T(8,128)(2,1)}, u32[]{:S(2)}) copy-start(bf16[128,128]{1,0:T(8,128)(2,1)} %w_gate_ref.3) | copy-start | bytes 98308
  3.2 22.0 %all-to-all-start = ((bf16[16,128,128]{2,1,0:T(8,128)(2,1)}), bf16[16,128,128]{2,1,0:T(8,128)(2,1)S(1)}, u32[]{:S(2)}, u32[]{:S(2)}) async-start(bf16[16,128,128]{2,1,0:T(8,128)(2,1)} %get-tuple-element.24), calls=%async_computation | async-start | bytes 1048576 | tf_op jit(solution)/shard_map/all_to_all | solution.py:29
  10.7 0.9 copy-start.12
  10.8 0.7 copy-start.13
  11.6 0.7 copy-start.11
  11.6 0.7 copy-start.9
  11.6 0.7 copy-start.10
  12.3 1.0 copy-start.3
  14.9 0.7 copy-start.5
  25.6 14.1 %copy-start.4 = (bf16[8,128,128]{2,1,0:T(8,128)(2,1)S(1)}, bf16[8,128,128]{2,1,0:T(8,128)(2,1)}, u32[]{:S(2)}) copy-start(bf16[8,128,128]{2,1,0:T(8,128)(2,1)} %adj_ref.3) | copy-start | bytes 786436
  25.6 14.1 %copy-start.6 = (bf16[128,1024]{1,0:T(8,128)(2,1)S(1)}, bf16[128,1024]{1,0:T(8,128)(2,1)}, u32[]{:S(2)}) copy-start(bf16[128,1024]{1,0:T(8,128)(2,1)} %copy-done.5) | copy-start | bytes 786436

commit v14 on v13

--- a/solution.py
+++ b/solution.py
@@ -78,7 +78,7 @@
 
 
 def project_kernel(
-    pair_hbm, mask_hbm, gain_hbm, w_hbm, sent_ref, zn_ref, mask_ref,
+    pair_hbm, mask_hbm, gain_hbm, w_hbm, sent_ref, mask_ref,
     pair_ref, mask_v, gain_ref, w_ref, sems,
 ):
     devices, depth, _ = sent_ref.shape
@@ -114,7 +114,6 @@
         for row in (2 * two, 2 * two + 1):
             hat, _ = centred(pair_ref[row].astype(F32).T)
             zn = (hat * gain).astype(BF)
-            zn_ref[:, row * cols : (row + 1) * cols] = zn
             proj = dot(weights, zn)
             mask = mask_ref[row : row + 1, :]
             left = mask * jax.nn.sigmoid(proj[hidden : 2 * hidden]) * proj[:hidden]
@@ -126,8 +125,8 @@
 
 
 def gate_kernel(
-    zn_ref, adj_ref, mask_ref, same_ref, w_ref, w_gate_ref, bias_ref, gain_ref, w_out_ref,
-    gain_in_ref, pair_ref, factor_ref, gate_ref, t_ref, columns_ref, hat_ref, rstd_ref,
+    adj_ref, mask_ref, same_ref, w_ref, w_gate_ref, bias_ref, gain_ref, w_out_ref,
+    gain_in_ref, pair_ref, factor_ref, gate_ref, t_ref, columns_ref, hat_ref, rstd_ref, zn_ref,
 ):
     rows, cols, width = adj_ref.shape
     weights = w_ref[...].astype(F32).T.astype(BF)
@@ -135,10 +134,15 @@
     w_gate = w_gate_ref[...].astype(F32).T.astype(BF)
     across, within = column(bias_ref[0:1, :]), column(bias_ref[1:2, :])
     gain = column(gain_ref[...])
-    columns_ref[...] = column(gain_in_ref[...])
+    gain_in = column(gain_in_ref[...])
+    columns_ref[...] = gain_in
     for row in range(rows):
         lanes = slice(row * cols, (row + 1) * cols)
-        zn = zn_ref[:, lanes]
+        hat, rstd = centred(pair_ref[row].astype(F32).T)
+        hat_ref[:, lanes] = hat
+        rstd_ref[row : row + 1, :] = rstd
+        zn = (hat * gain_in).astype(BF)
+        zn_ref[:, lanes] = zn
         proj = dot(weights, zn)
         mask = mask_ref[row : row + 1, :]
         for side in range(2):
@@ -154,9 +158,6 @@
         d_out = (adj_ref[row].astype(F32) * gate).astype(BF)
         t = dot(w_out_ref[...], d_out, ((1,), (1,))) * gain
         t_ref[:, lanes] = (t - jnp.mean(t, 0, keepdims=True)).astype(BF)
-        hat, rstd = centred(pair_ref[row].astype(F32).T)
-        hat_ref[:, lanes] = hat
-        rstd_ref[row : row + 1, :] = rstd
 
 
 def mix_kernel(got_ref, sent_ref, left_ref, right_ref, left_s, right_s, out_s):
@@ -311,9 +312,9 @@
     row_chain = lax.dynamic_slice_in_dim(chain, start, rows, 0)
     same = (row_chain[:, None] == chain[None, :]).astype(F32)
     gain_in, gain_out = gain_in[None], gain_out[None]
-    sent, zn, cell_mask = call(
+    sent, cell_mask = call(
         project_kernel,
-        [shape((devices, 2 * half, cols), BF), shape((width, cells), BF), shape((rows, cols), F32)],
+        [shape((devices, 2 * half, cols), BF), shape((rows, cols), F32)],
         [
             pltpu.VMEM(pair.shape, BF),
             pltpu.VMEM((1, residues), jnp.int32),
@@ -326,12 +327,12 @@
         mib=56,
     )(pair, mask[None], gain_in, w_proj)
     got = swap(sent)
-    factor, gate, t, columns, hat, rstd = call(
+    factor, gate, t, columns, hat, rstd, zn = call(
         gate_kernel,
-        [shape((4 * hidden, cells), BF), shape((rows, cols, width), F32), shape((hidden, cells), BF), shape((width, width), F32), shape((width, cells), F32), shape((rows, cols), F32)],
+        [shape((4 * hidden, cells), BF), shape((rows, cols, width), F32), shape((hidden, cells), BF), shape((width, width), F32), shape((width, cells), F32), shape((rows, cols), F32), shape((width, cells), BF)],
         flops=2 * 10**9,
         name="gate",
-    )(zn, adjoint, cell_mask, same, w_proj, w_gate, chain_bias, gain_out, w_out, gain_in, pair)
+    )(adjoint, cell_mask, same, w_proj, w_gate, chain_bias, gain_out, w_out, gain_in, pair)
     field = pltpu.VMEM((devices * half, cols), F32)
     channels = shape((own, residues, cols), BF)
     block = shape((devices, half, cols), BF)

time: 97 us -> 97 us (level)
    unnamed x28 -> x26, local copies, waits for them, and re-layouts: 2.99 us -> 2.98 us
where the time goes in v14:
time: 97 us; the launch traced here: 96.4 us
  blocking collectives  67.6 us (70%)
  waiting for transfers between devices  9.61 us (10%)
  Pallas kernels  7.83 us (8%)
  starting transfers between devices  7.5 us (8%)
  local copies, waits for them, and re-layouts  3.05 us (3%)
    all_to_all x5, blocking collectives, swap(): lax.all_to_all(blocks, ('wide', 'narrow'), split_axis=0, concat_axis=0, t...  67.6 us
    all_to_all x1, waiting for transfers between devices, swap(): lax.all_to_all(blocks, ('wide', 'narrow'), split_axis=0, concat_axis=0, t...  9.61 us
    pallas_call x8, Pallas kernels, run(): pl.pallas_call(kernel, out_shape=list(outs), in_specs=[pl.BlockSpec(memor...  7.83 us
    all_to_all x1, starting transfers between devices, swap(): lax.all_to_all(blocks, ('wide', 'narrow'), split_axis=0, concat_axis=0, t...  7.5 us
    unnamed x26, local copies, waits for them, and re-layouts  2.98 us
  transfers between devices with their start and end apart: 1, of which 1 were waited for; matrix products, arithmetic and copies ran while one was open for 0% of the time, Pallas kernels for 2%

profile of v14, /device:TPU:0, one launch (start us, length us, event | category | flops | bytes accessed | tf_op | source)
XLA Modules:
  0.0 96.4 jit_solution(15933245246575654057)
XLA Ops:
  0.6 2.5 %project.1 = (bf16[16,128,128]{2,1,0:T(8,128)(2,1)}, f32[8,128]{1,0:T(8,128)}) custom-call(bf16[8,128,128]{2,1,0:T(8,128)(2,1)} %pair_ref.1, s32[1,128]{1,0:T(1,128)} %bitcast.9, f32[1,128]{1,0:T(1,128)} %bitcast.5, bf16[128,512]{1,0:T(8,128)(2,1)} %w_ref.3), custom_call_target="tpu_custom_call" | custom-call | bytes 922624 | tf_op jit(solution)/shard_map/project/pallas_call | solution.py:286
  3.2 0.0 copy-start
  3.2 0.0 copy-start.6
  3.2 7.5 %all-to-all-start = ((bf16[16,128,128]{2,1,0:T(8,128)(2,1)}), bf16[16,128,128]{2,1,0:T(8,128)(2,1)S(1)}, u32[]{:S(2)}, u32[]{:S(2)}) async-start(bf16[16,128,128]{2,1,0:T(8,128)(2,1)} %get-tuple-element.24), calls=%async_computation | async-start | bytes 1048576 | tf_op jit(solution)/shard_map/all_to_all | solution.py:29
  10.8 0.7 copy-done.12
  11.4 0.1 dynamic_slice.3
  11.5 0.1 compare_convert_fusion.same_ref
  11.6 0.6 copy-done.10
  12.2 0.0 copy-done.8
  12.2 0.0 copy-done.9
  12.2 0.9 copy-done.2
  13.2 1.7 %gate.1 = (bf16[512,1024]{1,0:T(8,128)(2,1)S(1)}, f32[8,128,128]{2,1,0:T(8,128)S(1)}, bf16[128,1024]{1,0:T(8,128)(2,1)S(1)}, f32[128,128]{1,0:T(8,128)S(1)}, f32...) custom-call(bf16[8,128,128]{2,1,0:T(8,128)(2,1)S(1)} %copy-done.2, ...), custom_call_target="tpu_custom_call" | custom-call | flops 2000000000 | bytes 3422208 | tf_op jit(solution)/shard_map/gate/pallas_call | solution.py:286
  14.9 0.7 copy-done.4
  15.6 9.6 %all-to-all-done.got_ref = bf16[16,128,128]{2,1,0:T(8,128)(2,1)S(1)} async-done(((bf16[16,128,128]{2,1,0:T(8,128)(2,1)}), bf16[16,128,128]{2,1,0:T(8,128)(2,1)S(1)}, u32[]{:S(2)}, u32[]{:S(2)}) %all-to-all-start) | async-done | bytes 524320 | tf_op jit(solution)/shard_map/all_to_all | solution.py:29
  25.2 0.4 mix.1
  25.6 14.1 %all_to_all.30.got_ref = bf16[16,64,128]{2,1,0:T(8,128)(2,1)S(1)} all-to-all(bf16[16,64,128]{2,1,0:T(8,128)(2,1)S(1)} %get-tuple-element.28), channel_id=1, replica_groups=mesh['groups'=2,'wide'=16,'narrow'=1] {'wide','narrow'}, dimensions={0} | all-to-all | bytes 524288 | tf_op jit(solution)/shard_map/all_to_all | solution.py:29
  39.7 0.7 norm.1
  40.4 12.8 %all_to_all.31.got_ref = bf16[16,64,128]{2,1,0:T(8,128)(2,1)S(1)} all-to-all(bf16[16,64,128]{2,1,0:T(8,128)(2,1)S(1)} %get-tuple-element.32), channel_id=1, replica_groups=mesh['groups'=2,'wide'=16,'narrow'=1] {'wide','narrow'}, dimensions={0} | all-to-all | bytes 524288 | tf_op jit(solution)/shard_map/all_to_all | solution.py:29
  53.2 0.4 unmix.1
  53.7 17.2 %all_to_all.32.got_ref = bf16[16,128,128]{2,1,0:T(8,128)(2,1)S(1)} all-to-all(bf16[16,128,128]{2,1,0:T(8,128)(2,1)S(1)} %unmix.1), channel_id=1, replica_groups=mesh['groups'=2,'wide'=16,'narrow'=1] {'wide','narrow'}, dimensions={0} | all-to-all | bytes 1048576 | tf_op jit(solution)/shard_map/all_to_all | solution.py:29
  70.9 0.8 cells.1
  71.7 12.4 %all_to_all.33.got_ref = bf16[16,8,640]{2,1,0:T(8,128)(2,1)S(1)} all-to-all(bf16[16,8,640]{2,1,0:T(8,128)(2,1)S(1)} %bitcast.4), channel_id=1, replica_groups=mesh['groups'=2,'wide'=16,'narrow'=1] {'wide','narrow'}, dimensions={0} | all-to-all | bytes 327680 | tf_op jit(solution)/shard_map/all_to_all | solution.py:29
  84.1 11.1 %all_to_all.34.got_ref = bf16[16,8,640]{2,1,0:T(8,128)(2,1)S(1)} all-to-all(bf16[16,8,640]{2,1,0:T(8,128)(2,1)S(1)} %sum.1), channel_id=1, replica_groups=mesh['groups'=2,'wide'=16,'narrow'=1] {'wide','narrow'}, dimensions={0} | all-to-all | bytes 327680 | tf_op jit(solution)/shard_map/all_to_all | solution.py:29
  95.2 1.3 %finish.1 = (bf16[8,128,128]{2,1,0:T(8,128)(2,1)}, bf16[8,128,128]{2,1,0:T(8,128)(2,1)}, f32[128,512]{1,0:T(8,128)}, f32[128,128]{1,0:T(8,128)}) custom-call(bf16[16,8,640]{2,1,0:T(8,128)(2,1)S(1)} %all_to_all.34.got_ref, bf16[8,128,128]{2,1,0:T(8,128)(2,1)S(1)} %get-tuple-element.39.output_ref, bf16[128,1024]{1,0:T(8,128)(2,1)S(1)} %get-tuple-element.40.u_ref, ...), custom_call_target="tpu_custom_call" | custom-call | bytes 2428928 | tf_op jit(solution)/shard_map/finish/pallas_call | solution.py:286
  (19 shorter events, 0.1 us)
Async XLA Ops:
  3.2 8.4 %copy-start = (bf16[128,512]{1,0:T(8,128)(2,1)S(1)}, bf16[128,512]{1,0:T(8,128)(2,1)}, u32[]{:S(2)}) copy-start(bf16[128,512]{1,0:T(8,128)(2,1)} %w_ref.3) | copy-start | bytes 393220
  3.2 8.4 %copy-start.1 = (bf16[8,128,128]{2,1,0:T(8,128)(2,1)S(1)}, bf16[8,128,128]{2,1,0:T(8,128)(2,1)}, u32[]{:S(2)}) copy-start(bf16[8,128,128]{2,1,0:T(8,128)(2,1)} %pair_ref.1) | copy-start | bytes 786436
  3.2 8.4 %copy-start.6 = (bf16[128,128]{1,0:T(8,128)(2,1)S(1)}, bf16[128,128]{1,0:T(8,128)(2,1)}, u32[]{:S(2)}) copy-start(bf16[128,128]{1,0:T(8,128)(2,1)} %w_out_ref.3) | copy-start | bytes 98308
  3.2 8.4 %copy-start.7 = (bf16[128,128]{1,0:T(8,128)(2,1)S(1)}, bf16[128,128]{1,0:T(8,128)(2,1)}, u32[]{:S(2)}) copy-start(bf16[128,128]{1,0:T(8,128)(2,1)} %w_gate_ref.3) | copy-start | bytes 98308
  3.2 22.0 %all-to-all-start = ((bf16[16,128,128]{2,1,0:T(8,128)(2,1)}), bf16[16,128,128]{2,1,0:T(8,128)(2,1)S(1)}, u32[]{:S(2)}, u32[]{:S(2)}) async-start(bf16[16,128,128]{2,1,0:T(8,128)(2,1)} %get-tuple-element.24), calls=%async_computation | async-start | bytes 1048576 | tf_op jit(solution)/shard_map/all_to_all | solution.py:29
  10.7 0.9 copy-start.11
  10.7 0.7 copy-start.12
  11.5 0.7 copy-start.10
  11.6 0.7 copy-start.8
  11.6 0.7 copy-start.9
  12.2 0.9 copy-start.2
  14.9 0.7 copy-start.4
  25.6 14.1 %copy-start.3 = (bf16[8,128,128]{2,1,0:T(8,128)(2,1)S(1)}, bf16[8,128,128]{2,1,0:T(8,128)(2,1)}, u32[]{:S(2)}) copy-start(bf16[8,128,128]{2,1,0:T(8,128)(2,1)} %adj_ref.3) | copy-start | bytes 786436
  25.6 14.1 %copy-start.5 = (bf16[128,1024]{1,0:T(8,128)(2,1)S(1)}, bf16[128,1024]{1,0:T(8,128)(2,1)}, u32[]{:S(2)}) copy-start(bf16[128,1024]{1,0:T(8,128)(2,1)} %copy-done.4) | copy-start | bytes 786436

commit v15 on v13

--- a/solution.py
+++ b/solution.py
@@ -127,7 +127,7 @@
 
 def gate_kernel(
     zn_ref, adj_ref, mask_ref, same_ref, w_ref, w_gate_ref, bias_ref, gain_ref, w_out_ref,
-    gain_in_ref, pair_ref, factor_ref, gate_ref, t_ref, columns_ref, hat_ref, rstd_ref,
+    gain_in_ref, pair_ref, factor_ref, gate_ref, t_ref, columns_ref, hat_ref, rstd_ref, slope_ref,
 ):
     rows, cols, width = adj_ref.shape
     weights = w_ref[...].astype(F32).T.astype(BF)
@@ -151,7 +151,9 @@
         bias = jnp.where(same_ref[row : row + 1, :] > 0.5, within, across)
         gate = jax.nn.sigmoid(dot(w_gate, zn) + bias).T
         gate_ref[row] = gate
-        d_out = (adj_ref[row].astype(F32) * gate).astype(BF)
+        scaled = adj_ref[row].astype(F32) * gate
+        slope_ref[row] = scaled * (1.0 - gate)
+        d_out = scaled.astype(BF)
         t = dot(w_out_ref[...], d_out, ((1,), (1,))) * gain
         t_ref[:, lanes] = (t - jnp.mean(t, 0, keepdims=True)).astype(BF)
         hat, rstd = centred(pair_ref[row].astype(F32).T)
@@ -176,7 +178,7 @@
 
 
 def norm_kernel(
-    got_ref, t_ref, gain_ref, gate_ref, adj_ref, zn_ref, w_out_ref,
+    got_ref, t_ref, gain_ref, gate_ref, slope_ref, zn_ref, w_out_ref,
     sent_ref, output_ref, d_logit_ref, part_ref,
 ):
     devices, depth, cols = got_ref.shape
@@ -190,9 +192,8 @@
             hat, rstd = centred(mixed)
             pieces.append(back_t(t_ref[:, lanes].astype(F32), hat, rstd))
             proj_out = dot((hat * gain).T.astype(BF), w_out_ref[...])
-            gate = gate_ref[row]
-            output_ref[row] = (gate * proj_out).astype(BF)
-            d_logit = (adj_ref[row].astype(F32) * proj_out * gate * (1.0 - gate)).astype(BF)
+            output_ref[row] = (gate_ref[row] * proj_out).astype(BF)
+            d_logit = (slope_ref[row] * proj_out).astype(BF)
             d_logit_ref[row] = d_logit
             term = dot(zn_ref[:, lanes], d_logit)
             total = term if total is None else total + term
@@ -326,9 +327,9 @@
         mib=56,
     )(pair, mask[None], gain_in, w_proj)
     got = swap(sent)
-    factor, gate, t, columns, hat, rstd = call(
+    factor, gate, t, columns, hat, rstd, slope = call(
         gate_kernel,
-        [shape((4 * hidden, cells), BF), shape((rows, cols, width), F32), shape((hidden, cells), BF), shape((width, width), F32), shape((width, cells), F32), shape((rows, cols), F32)],
+        [shape((4 * hidden, cells), BF), shape((rows, cols, width), F32), shape((hidden, cells), BF), shape((width, width), F32), shape((width, cells), F32), shape((rows, cols), F32), shape((rows, cols, width), F32)],
         flops=2 * 10**9,
         name="gate",
     )(zn, adjoint, cell_mask, same, w_proj, w_gate, chain_bias, gain_out, w_out, gain_in, pair)
@@ -342,7 +343,7 @@
         norm_kernel,
         [block, shape(pair.shape, BF), shape(pair.shape, BF), shape((width, width), F32)],
         name="norm",
-    )(got, t, gain_out, gate, adjoint, zn, w_out)
+    )(got, t, gain_out, gate, slope, zn, w_out)
     got = swap(sent)
     sent = call(
         unmix_kernel, [shape((devices, 2 * half, cols), BF)], [field] * 3, name="unmix"

time: 97 us -> 97.4 us (level)
  local copies, waits for them, and re-layouts: 3.06 us -> 6.18 us
  waiting for transfers between devices: 9.61 us -> 6.51 us
    unnamed x28 -> x34, local copies, waits for them, and re-layouts: 2.99 us -> 6.1 us
    all_to_all x1, waiting for transfers between devices: 9.61 us -> 6.51 us  [swap(): lax.all_to_all(blocks, ('wide', 'narrow'), split_axis=0, concat_axis=0, t...]
where the time goes in v15:
time: 97.4 us; the launch traced here: 96.6 us
  blocking collectives  67.7 us (70%)
  Pallas kernels  7.88 us (8%)
  starting transfers between devices  7.5 us (8%)
  waiting for transfers between devices  6.51 us (7%)
  local copies, waits for them, and re-layouts  6.18 us (6%)
    all_to_all x5, blocking collectives, swap(): lax.all_to_all(blocks, ('wide', 'narrow'), split_axis=0, concat_axis=0, t...  67.7 us
    pallas_call x8, Pallas kernels, run(): pl.pallas_call(kernel, out_shape=list(outs), in_specs=[pl.BlockSpec(memor...  7.88 us
    all_to_all x1, starting transfers between devices, swap(): lax.all_to_all(blocks, ('wide', 'narrow'), split_axis=0, concat_axis=0, t...  7.5 us
    all_to_all x1, waiting for transfers between devices, swap(): lax.all_to_all(blocks, ('wide', 'narrow'), split_axis=0, concat_axis=0, t...  6.51 us
    unnamed x34, local copies, waits for them, and re-layouts  6.1 us
  transfers between devices with their start and end apart: 1, of which 1 were waited for; matrix products, arithmetic and copies ran while one was open for 0% of the time, Pallas kernels for 2%

profile of v15, /device:TPU:0, one launch (start us, length us, event | category | flops | bytes accessed | tf_op | source)
XLA Modules:
  0.0 96.6 jit_solution(15734940807807777938)
XLA Ops:
  0.6 2.5 %project.1 = (bf16[16,128,128]{2,1,0:T(8,128)(2,1)}, bf16[128,1024]{1,0:T(8,128)(2,1)}, f32[8,128]{1,0:T(8,128)}) custom-call(bf16[8,128,128]{2,1,0:T(8,128)(2,1)} %pair_ref.1, s32[1,128]{1,0:T(1,128)} %bitcast.9, f32[1,128]{1,0:T(1,128)} %bitcast.5, bf16[128,512]{1,0:T(8,128)(2,1)} %w_ref.3), custom_call_target="tpu_custom_call" | custom-call | bytes 1184768 | tf_op jit(solution)/shard_map/project/pallas_call | solution.py:286
  3.2 7.5 %all-to-all-start = ((bf16[16,128,128]{2,1,0:T(8,128)(2,1)}), bf16[16,128,128]{2,1,0:T(8,128)(2,1)S(1)}, u32[]{:S(2)}, u32[]{:S(2)}) async-start(bf16[16,128,128]{2,1,0:T(8,128)(2,1)} %get-tuple-element.25), calls=%async_computation | async-start | bytes 1048576 | tf_op jit(solution)/shard_map/all_to_all | solution.py:29
  10.7 0.7 copy-done.16
  11.4 0.1 dynamic_slice.3
  11.5 0.1 compare_convert_fusion.same_ref
  11.6 0.7 copy-done.14
  12.2 0.9 copy-done.4
  13.2 0.8 copy-done.7
  13.9 0.8 copy-done.9
  14.7 0.9 copy-done.13
  15.7 1.7 %gate.1 = (bf16[512,1024]{1,0:T(8,128)(2,1)S(1)}, f32[8,128,128]{2,1,0:T(8,128)S(1)}, bf16[128,1024]{1,0:T(8,128)(2,1)S(1)}, f32[128,128]{1,0:T(8,128)S(1)}, f32...) custom-call(bf16[128,1024]{1,0:T(8,128)(2,1)S(1)} %copy-done, ...), custom_call_target="tpu_custom_call" | custom-call | flops 2000000000 | bytes 3946496 | tf_op jit(solution)/shard_map/gate/pallas_call | solution.py:286
  17.4 0.6 copy-done.2
  18.0 0.7 copy-done.5
  18.7 6.5 %all-to-all-done.got_ref = bf16[16,128,128]{2,1,0:T(8,128)(2,1)S(1)} async-done(((bf16[16,128,128]{2,1,0:T(8,128)(2,1)}), bf16[16,128,128]{2,1,0:T(8,128)(2,1)S(1)}, u32[]{:S(2)}, u32[]{:S(2)}) %all-to-all-start) | async-done | bytes 524320 | tf_op jit(solution)/shard_map/all_to_all | solution.py:29
  25.2 0.4 mix.1
  25.6 14.1 %all_to_all.30.got_ref = bf16[16,64,128]{2,1,0:T(8,128)(2,1)S(1)} all-to-all(bf16[16,64,128]{2,1,0:T(8,128)(2,1)S(1)} %get-tuple-element.30), channel_id=1, replica_groups=mesh['groups'=2,'wide'=16,'narrow'=1] {'wide','narrow'}, dimensions={0} | all-to-all | bytes 524288 | tf_op jit(solution)/shard_map/all_to_all | solution.py:29
  39.7 0.7 norm.1
  40.4 12.8 %all_to_all.31.got_ref = bf16[16,64,128]{2,1,0:T(8,128)(2,1)S(1)} all-to-all(bf16[16,64,128]{2,1,0:T(8,128)(2,1)S(1)} %get-tuple-element.34), channel_id=1, replica_groups=mesh['groups'=2,'wide'=16,'narrow'=1] {'wide','narrow'}, dimensions={0} | all-to-all | bytes 524288 | tf_op jit(solution)/shard_map/all_to_all | solution.py:29
  53.2 0.4 unmix.1
  53.7 17.4 %all_to_all.32.got_ref = bf16[16,128,128]{2,1,0:T(8,128)(2,1)S(1)} all-to-all(bf16[16,128,128]{2,1,0:T(8,128)(2,1)S(1)} %unmix.1), channel_id=1, replica_groups=mesh['groups'=2,'wide'=16,'narrow'=1] {'wide','narrow'}, dimensions={0} | all-to-all | bytes 1048576 | tf_op jit(solution)/shard_map/all_to_all | solution.py:29
  71.0 0.8 cells.1
  71.9 12.4 %all_to_all.33.got_ref = bf16[16,8,640]{2,1,0:T(8,128)(2,1)S(1)} all-to-all(bf16[16,8,640]{2,1,0:T(8,128)(2,1)S(1)} %bitcast.4), channel_id=1, replica_groups=mesh['groups'=2,'wide'=16,'narrow'=1] {'wide','narrow'}, dimensions={0} | all-to-all | bytes 327680 | tf_op jit(solution)/shard_map/all_to_all | solution.py:29
  84.3 11.1 %all_to_all.34.got_ref = bf16[16,8,640]{2,1,0:T(8,128)(2,1)S(1)} all-to-all(bf16[16,8,640]{2,1,0:T(8,128)(2,1)S(1)} %sum.1), channel_id=1, replica_groups=mesh['groups'=2,'wide'=16,'narrow'=1] {'wide','narrow'}, dimensions={0} | all-to-all | bytes 327680 | tf_op jit(solution)/shard_map/all_to_all | solution.py:29
  95.3 1.3 %finish.1 = (bf16[8,128,128]{2,1,0:T(8,128)(2,1)}, bf16[8,128,128]{2,1,0:T(8,128)(2,1)}, f32[128,512]{1,0:T(8,128)}, f32[128,128]{1,0:T(8,128)}) custom-call(bf16[16,8,640]{2,1,0:T(8,128)(2,1)S(1)} %all_to_all.34.got_ref, bf16[8,128,128]{2,1,0:T(8,128)(2,1)S(1)} %get-tuple-element.41.output_ref, bf16[128,1024]{1,0:T(8,128)(2,1)S(1)} %get-tuple-element.42.u_ref, ...), custom_call_target="tpu_custom_call" | custom-call | bytes 2428928 | tf_op jit(solution)/shard_map/finish/pallas_call | solution.py:286
  (27 shorter events, 0.1 us)
Async XLA Ops:
  3.2 8.4 %copy-start = (bf16[128,1024]{1,0:T(8,128)(2,1)S(1)}, bf16[128,1024]{1,0:T(8,128)(2,1)}, u32[]{:S(2)}) copy-start(bf16[128,1024]{1,0:T(8,128)(2,1)} %get-tuple-element.26.zn_ref) | copy-start | bytes 786436
  3.2 8.4 %copy-start.1 = (bf16[128,512]{1,0:T(8,128)(2,1)S(1)}, bf16[128,512]{1,0:T(8,128)(2,1)}, u32[]{:S(2)}) copy-start(bf16[128,512]{1,0:T(8,128)(2,1)} %w_ref.3) | copy-start | bytes 393220
  3.2 22.0 %all-to-all-start = ((bf16[16,128,128]{2,1,0:T(8,128)(2,1)}), bf16[16,128,128]{2,1,0:T(8,128)(2,1)S(1)}, u32[]{:S(2)}, u32[]{:S(2)}) async-start(bf16[16,128,128]{2,1,0:T(8,128)(2,1)} %get-tuple-element.25), calls=%async_computation | async-start | bytes 1048576 | tf_op jit(solution)/shard_map/all_to_all | solution.py:29
  10.7 0.8 copy-start.15
  10.7 0.7 copy-start.16
  11.5 0.7 copy-start.14
  11.5 0.7 copy-start.11
  11.5 0.7 copy-start.12
  12.2 1.0 copy-start.4
  13.2 0.8 copy-start.7
  13.9 0.8 copy-start.9
  14.7 0.9 copy-start.13
  17.3 0.6 copy-start.2
  18.0 0.7 copy-start.5
  25.6 14.1 %copy-start.6 = (bf16[128,1024]{1,0:T(8,128)(2,1)S(1)}, bf16[128,1024]{1,0:T(8,128)(2,1)}, u32[]{:S(2)}) copy-start(bf16[128,1024]{1,0:T(8,128)(2,1)} %copy-done.5) | copy-start | bytes 786436
  25.6 14.1 %copy-start.8 = (bf16[128,128]{1,0:T(8,128)(2,1)S(1)}, bf16[128,128]{1,0:T(8,128)(2,1)}, u32[]{:S(2)}) copy-start(bf16[128,128]{1,0:T(8,128)(2,1)} %w_out_ref.3) | copy-start | bytes 98308
  53.6 17.4 %copy-start.3 = (f32[128,128]{1,0:T(8,128)S(1)}, f32[128,128]{1,0:T(8,128)}, u32[]{:S(2)}) copy-start(f32[128,128]{1,0:T(8,128)} %copy-done.2) | copy-start | bytes 196612
  84.3 11.1 %copy-start.10 = (bf16[128,128]{1,0:T(8,128)(2,1)S(1)}, bf16[128,128]{1,0:T(8,128)(2,1)}, u32[]{:S(2)}) copy-start(bf16[128,128]{1,0:T(8,128)(2,1)} %w_gate_ref.3) | copy-start | bytes 98308

commit v16 on v13

--- a/solution.py
+++ b/solution.py
@@ -127,7 +127,7 @@
 
 def gate_kernel(
     zn_ref, adj_ref, mask_ref, same_ref, w_ref, w_gate_ref, bias_ref, gain_ref, w_out_ref,
-    gain_in_ref, pair_ref, factor_ref, gate_ref, t_ref, columns_ref, hat_ref, rstd_ref,
+    gain_in_ref, pair_ref, factor_ref, gate_ref, t_ref, columns_ref, hat_ref, rstd_ref, scale_ref,
 ):
     rows, cols, width = adj_ref.shape
     weights = w_ref[...].astype(F32).T.astype(BF)
@@ -136,6 +136,7 @@
     across, within = column(bias_ref[0:1, :]), column(bias_ref[1:2, :])
     gain = column(gain_ref[...])
     columns_ref[...] = column(gain_in_ref[...])
+    scale_ref[...] = gain
     for row in range(rows):
         lanes = slice(row * cols, (row + 1) * cols)
         zn = zn_ref[:, lanes]
@@ -180,7 +181,7 @@
     sent_ref, output_ref, d_logit_ref, part_ref,
 ):
     devices, depth, cols = got_ref.shape
-    gain = column(gain_ref[...])
+    gain = gain_ref[...]
     total = None
     for two in range(depth // 16):
         pieces = []
@@ -326,9 +327,9 @@
         mib=56,
     )(pair, mask[None], gain_in, w_proj)
     got = swap(sent)
-    factor, gate, t, columns, hat, rstd = call(
+    factor, gate, t, columns, hat, rstd, scale = call(
         gate_kernel,
-        [shape((4 * hidden, cells), BF), shape((rows, cols, width), F32), shape((hidden, cells), BF), shape((width, width), F32), shape((width, cells), F32), shape((rows, cols), F32)],
+        [shape((4 * hidden, cells), BF), shape((rows, cols, width), F32), shape((hidden, cells), BF), shape((width, width), F32), shape((width, cells), F32), shape((rows, cols), F32), shape((width, width), F32)],
         flops=2 * 10**9,
         name="gate",
     )(zn, adjoint, cell_mask, same, w_proj, w_gate, chain_bias, gain_out, w_out, gain_in, pair)
@@ -342,7 +343,7 @@
         norm_kernel,
         [block, shape(pair.shape, BF), shape(pair.shape, BF), shape((width, width), F32)],
         name="norm",
-    )(got, t, gain_out, gate, adjoint, zn, w_out)
+    )(got, t, scale, gate, adjoint, zn, w_out)
     got = swap(sent)
     sent = call(
         unmix_kernel, [shape((devices, 2 * half, cols), BF)], [field] * 3, name="unmix"

time: 97 us -> 97.4 us (level)
  local copies, waits for them, and re-layouts: 3.06 us -> 5.17 us
  waiting for transfers between devices: 9.61 us -> 7.51 us
    unnamed x28 -> x34, local copies, waits for them, and re-layouts: 2.99 us -> 5.09 us
    all_to_all x1, waiting for transfers between devices: 9.61 us -> 7.51 us  [swap(): lax.all_to_all(blocks, ('wide', 'narrow'), split_axis=0, concat_axis=0, t...]
where the time goes in v16:
time: 97.4 us; the launch traced here: 96.6 us
  blocking collectives  67.7 us (70%)
  Pallas kernels  7.89 us (8%)
  waiting for transfers between devices  7.51 us (8%)
  starting transfers between devices  7.5 us (8%)
  local copies, waits for them, and re-layouts  5.17 us (5%)
    all_to_all x5, blocking collectives, swap(): lax.all_to_all(blocks, ('wide', 'narrow'), split_axis=0, concat_axis=0, t...  67.7 us
    pallas_call x8, Pallas kernels, run(): pl.pallas_call(kernel, out_shape=list(outs), in_specs=[pl.BlockSpec(memor...  7.89 us
    all_to_all x1, waiting for transfers between devices, swap(): lax.all_to_all(blocks, ('wide', 'narrow'), split_axis=0, concat_axis=0, t...  7.51 us
    all_to_all x1, starting transfers between devices, swap(): lax.all_to_all(blocks, ('wide', 'narrow'), split_axis=0, concat_axis=0, t...  7.5 us
    unnamed x34, local copies, waits for them, and re-layouts  5.09 us
  transfers between devices with their start and end apart: 1, of which 1 were waited for; matrix products, arithmetic and copies ran while one was open for 0% of the time, Pallas kernels for 2%

profile of v16, /device:TPU:0, one launch (start us, length us, event | category | flops | bytes accessed | tf_op | source)
XLA Modules:
  0.0 96.6 jit_solution(11447873802104077764)
XLA Ops:
  0.6 2.5 %project.1 = (bf16[16,128,128]{2,1,0:T(8,128)(2,1)}, bf16[128,1024]{1,0:T(8,128)(2,1)}, f32[8,128]{1,0:T(8,128)}) custom-call(bf16[8,128,128]{2,1,0:T(8,128)(2,1)} %pair_ref.1, s32[1,128]{1,0:T(1,128)} %bitcast.8, f32[1,128]{1,0:T(1,128)} %bitcast.5, bf16[128,512]{1,0:T(8,128)(2,1)} %w_ref.3), custom_call_target="tpu_custom_call" | custom-call | bytes 1184768 | tf_op jit(solution)/shard_map/project/pallas_call | solution.py:286
  3.2 7.5 %all-to-all-start = ((bf16[16,128,128]{2,1,0:T(8,128)(2,1)}), bf16[16,128,128]{2,1,0:T(8,128)(2,1)S(1)}, u32[]{:S(2)}, u32[]{:S(2)}) async-start(bf16[16,128,128]{2,1,0:T(8,128)(2,1)} %get-tuple-element.25), calls=%async_computation | async-start | bytes 1048576 | tf_op jit(solution)/shard_map/all_to_all | solution.py:29
  10.8 0.7 copy-done.16
  11.4 0.1 dynamic_slice.3
  11.5 0.1 compare_convert_fusion.same_ref
  11.6 0.6 copy-done.13
  12.2 0.0 copy-done.14
  12.3 0.9 copy-done.5
  13.2 0.8 copy-done.8
  14.0 0.8 copy-done.10
  14.7 1.7 %gate.1 = (bf16[512,1024]{1,0:T(8,128)(2,1)S(1)}, f32[8,128,128]{2,1,0:T(8,128)S(1)}, bf16[128,1024]{1,0:T(8,128)(2,1)S(1)}, f32[128,128]{1,0:T(8,128)S(1)}, f32...) custom-call(bf16[128,1024]{1,0:T(8,128)(2,1)S(1)} %copy-done, ...), custom_call_target="tpu_custom_call" | custom-call | flops 2000000000 | bytes 3487744 | tf_op jit(solution)/shard_map/gate/pallas_call | solution.py:286
  16.4 0.6 copy-done.3
  17.1 0.6 copy-done.6
  17.7 7.5 %all-to-all-done.got_ref = bf16[16,128,128]{2,1,0:T(8,128)(2,1)S(1)} async-done(((bf16[16,128,128]{2,1,0:T(8,128)(2,1)}), bf16[16,128,128]{2,1,0:T(8,128)(2,1)S(1)}, u32[]{:S(2)}, u32[]{:S(2)}) %all-to-all-start) | async-done | bytes 524320 | tf_op jit(solution)/shard_map/all_to_all | solution.py:29
  25.2 0.4 mix.1
  25.6 14.1 %all_to_all.30.got_ref = bf16[16,64,128]{2,1,0:T(8,128)(2,1)S(1)} all-to-all(bf16[16,64,128]{2,1,0:T(8,128)(2,1)S(1)} %get-tuple-element.30), channel_id=1, replica_groups=mesh['groups'=2,'wide'=16,'narrow'=1] {'wide','narrow'}, dimensions={0} | all-to-all | bytes 524288 | tf_op jit(solution)/shard_map/all_to_all | solution.py:29
  39.7 0.7 norm.1
  40.4 12.8 %all_to_all.31.got_ref = bf16[16,64,128]{2,1,0:T(8,128)(2,1)S(1)} all-to-all(bf16[16,64,128]{2,1,0:T(8,128)(2,1)S(1)} %get-tuple-element.34), channel_id=1, replica_groups=mesh['groups'=2,'wide'=16,'narrow'=1] {'wide','narrow'}, dimensions={0} | all-to-all | bytes 524288 | tf_op jit(solution)/shard_map/all_to_all | solution.py:29
  53.2 0.4 unmix.1
  53.7 17.4 %all_to_all.32.got_ref = bf16[16,128,128]{2,1,0:T(8,128)(2,1)S(1)} all-to-all(bf16[16,128,128]{2,1,0:T(8,128)(2,1)S(1)} %unmix.1), channel_id=1, replica_groups=mesh['groups'=2,'wide'=16,'narrow'=1] {'wide','narrow'}, dimensions={0} | all-to-all | bytes 1048576 | tf_op jit(solution)/shard_map/all_to_all | solution.py:29
  71.1 0.8 cells.1
  71.9 12.4 %all_to_all.33.got_ref = bf16[16,8,640]{2,1,0:T(8,128)(2,1)S(1)} all-to-all(bf16[16,8,640]{2,1,0:T(8,128)(2,1)S(1)} %bitcast.4), channel_id=1, replica_groups=mesh['groups'=2,'wide'=16,'narrow'=1] {'wide','narrow'}, dimensions={0} | all-to-all | bytes 327680 | tf_op jit(solution)/shard_map/all_to_all | solution.py:29
  84.3 11.1 %all_to_all.34.got_ref = bf16[16,8,640]{2,1,0:T(8,128)(2,1)S(1)} all-to-all(bf16[16,8,640]{2,1,0:T(8,128)(2,1)S(1)} %sum.1), channel_id=1, replica_groups=mesh['groups'=2,'wide'=16,'narrow'=1] {'wide','narrow'}, dimensions={0} | all-to-all | bytes 327680 | tf_op jit(solution)/shard_map/all_to_all | solution.py:29
  95.4 1.3 %finish.1 = (bf16[8,128,128]{2,1,0:T(8,128)(2,1)}, bf16[8,128,128]{2,1,0:T(8,128)(2,1)}, f32[128,512]{1,0:T(8,128)}, f32[128,128]{1,0:T(8,128)}) custom-call(bf16[16,8,640]{2,1,0:T(8,128)(2,1)S(1)} %all_to_all.34.got_ref, bf16[8,128,128]{2,1,0:T(8,128)(2,1)S(1)} %get-tuple-element.41.output_ref, bf16[128,1024]{1,0:T(8,128)(2,1)S(1)} %get-tuple-element.42.u_ref, ...), custom_call_target="tpu_custom_call" | custom-call | bytes 2428928 | tf_op jit(solution)/shard_map/finish/pallas_call | solution.py:286
  (27 shorter events, 0.1 us)
Async XLA Ops:
  3.2 8.4 %copy-start = (bf16[128,1024]{1,0:T(8,128)(2,1)S(1)}, bf16[128,1024]{1,0:T(8,128)(2,1)}, u32[]{:S(2)}) copy-start(bf16[128,1024]{1,0:T(8,128)(2,1)} %get-tuple-element.26.zn_ref) | copy-start | bytes 786436
  3.2 8.4 %copy-start.1 = (bf16[128,512]{1,0:T(8,128)(2,1)S(1)}, bf16[128,512]{1,0:T(8,128)(2,1)}, u32[]{:S(2)}) copy-start(bf16[128,512]{1,0:T(8,128)(2,1)} %w_ref.3) | copy-start | bytes 393220
  3.2 8.4 %copy-start.2 = (bf16[8,128,128]{2,1,0:T(8,128)(2,1)S(1)}, bf16[8,128,128]{2,1,0:T(8,128)(2,1)}, u32[]{:S(2)}) copy-start(bf16[8,128,128]{2,1,0:T(8,128)(2,1)} %adj_ref.3) | copy-start | bytes 786436
  3.2 22.0 %all-to-all-start = ((bf16[16,128,128]{2,1,0:T(8,128)(2,1)}), bf16[16,128,128]{2,1,0:T(8,128)(2,1)S(1)}, u32[]{:S(2)}, u32[]{:S(2)}) async-start(bf16[16,128,128]{2,1,0:T(8,128)(2,1)} %get-tuple-element.25), calls=%async_computation | async-start | bytes 1048576 | tf_op jit(solution)/shard_map/all_to_all | solution.py:29
  10.7 0.9 copy-start.15
  10.7 0.7 copy-start.16
  11.6 0.7 copy-start.13
  11.6 0.7 copy-start.12
  11.6 0.7 copy-start.14
  12.3 0.9 copy-start.5
  13.2 0.8 copy-start.8
  14.0 0.8 copy-start.10
  16.4 0.6 copy-start.3
  17.1 0.6 copy-start.6
  25.6 14.1 %copy-start.7 = (f32[128,128]{1,0:T(8,128)S(1)}, f32[128,128]{1,0:T(8,128)}, u32[]{:S(2)}) copy-start(f32[128,128]{1,0:T(8,128)} %copy-done.6) | copy-start | bytes 196612
  25.6 14.1 %copy-start.9 = (bf16[128,128]{1,0:T(8,128)(2,1)S(1)}, bf16[128,128]{1,0:T(8,128)(2,1)}, u32[]{:S(2)}) copy-start(bf16[128,128]{1,0:T(8,128)(2,1)} %w_out_ref.3) | copy-start | bytes 98308
  53.7 17.4 %copy-start.4 = (f32[128,128]{1,0:T(8,128)S(1)}, f32[128,128]{1,0:T(8,128)}, u32[]{:S(2)}) copy-start(f32[128,128]{1,0:T(8,128)} %copy-done.3) | copy-start | bytes 196612
  84.3 11.1 %copy-start.11 = (bf16[128,128]{1,0:T(8,128)(2,1)S(1)}, bf16[128,128]{1,0:T(8,128)(2,1)}, u32[]{:S(2)}) copy-start(bf16[128,128]{1,0:T(8,128)(2,1)} %w_gate_ref.3) | copy-start | bytes 98308
